TPU v7x, 128 devices: a whole 4x4x4 slice. The times are simulated.
128 devices in a mesh: seq: 8 (over z, core), exp: 16 (over x, y).
Axes of the slice: x: 4, y: 4, z: 4, core: 2. Of those that a mesh axis runs over, the one named last changes fastest.
Arguments:
- queries: bfloat16 [8192, 4096], P('seq', 'exp'), may hold values from -6 to 6
- keys: bfloat16 [8192, 4096], P('seq', 'exp'), may hold values from -6 to 6
- values: bfloat16 [8192, 4096], P('seq', 'exp'), may hold values from -6 to 6
- gates: int32 [8, 3], replicated, may hold values from 0 to 7, as said below
- o_proj: bfloat16 [4096, 3584], P('exp'), may hold values from -0.5 to 0.5
- residual: bfloat16 [8192, 3584], P(('seq', 'exp')), may hold values from -40 to 40
- norm_gain: float32 [3584], replicated, may hold values from 0.25 to 1.75
- routes: int32 [8192, 8], P(('seq', 'exp')), may hold values from 0 to 127, all different within a row; in each aligned block of 64 rows (0 to 63, 64 to 127, ...) at most 8 rows name the same one
- route_weights: float32 [8192, 8], P(('seq', 'exp')), may hold values from 0.05 to 0.5
- w_gate: bfloat16 [128, 3584, 1024], P(('seq', 'exp')), may hold values from -0.09375 to 0.09375
- w_up: bfloat16 [128, 3584, 1024], P(('seq', 'exp')), may hold values from -0.09375 to 0.09375
- w_down: bfloat16 [128, 1024, 3584], P(('seq', 'exp')), may hold values from -0.1875 to 0.1875
Outputs:
- attn_proj: bfloat16 [8192, 3584], P(('seq', 'exp'))
- moe_out: bfloat16 [8192, 3584], P(('seq', 'exp'))
Inputs may be any that keep to these rules, and one draw needn't show every extreme that they name: `gates`: entry 0 of row b is b; every other entry is either a block below b, distinct within the row, or b itself marking an unused entry; row b names min(b, 2) blocks below b. `routes`: the 8 experts of a token are distinct; the rows of one device name each expert at most 8 times, a bound that some block reaches.
All inputs are finite; a program needn't handle non-finite values.
Results may differ from a plain program's by a relative error of at most 0.035.
Values may be sent and summed in bfloat16 or wider, within the bound.
No kernel may reach another device: no remote copies, remote signals or barrier semaphores. Data moves between devices by JAX's collectives and lax.ppermute only.
A program may use at most 128 MiB of HBM per device.

v0:
```python
import math

import jax
import jax.numpy as jnp
from jax import lax
from jax.sharding import PartitionSpec as P

HD = 128
BLOCK = 1024
ROUTE_K = 8


NEG_FILL = -1e30


def pair_partial(query_blk, key_blk, value_blk, own_block):
    inv_root = 1.0 / math.sqrt(query_blk.shape[-1])
    scores = (
        jnp.einsum("qhd,khd->hqk", query_blk, key_blk, preferred_element_type=jnp.float32)
        * inv_root
    )
    length = query_blk.shape[0]
    query_pos = lax.broadcasted_iota(jnp.int32, (length, length), 0)
    key_pos = lax.broadcasted_iota(jnp.int32, (length, length), 1)
    allowed = jnp.logical_or(jnp.logical_not(own_block), key_pos <= query_pos)[None]
    masked = jnp.where(allowed, scores, NEG_FILL)
    row_max = jnp.max(masked, axis=-1)
    weights = jnp.where(allowed, jnp.exp(masked - row_max[..., None]), 0.0)
    amount = jnp.sum(weights, axis=-1)
    mixed_rows = jnp.einsum(
        "hqk,khd->qhd", weights.astype(jnp.bfloat16), value_blk, preferred_element_type=jnp.float32
    )
    block_part = (mixed_rows / jnp.transpose(amount)[..., None]).astype(jnp.bfloat16)
    return (block_part, row_max, amount)


def merge_partial(carried, incoming):
    running_max, running_sum, running_out = carried
    block_part, row_max, amount = incoming
    new_max = jnp.maximum(running_max, row_max)
    old_factor = jnp.exp(running_max - new_max)
    new_factor = jnp.exp(row_max - new_max) * amount
    running_sum = running_sum * old_factor + new_factor
    running_out = (
        running_out * jnp.swapaxes(old_factor, -1, -2)[..., None]
        + block_part.astype(jnp.float32) * jnp.swapaxes(new_factor, -1, -2)[..., None]
    )
    return (new_max, running_sum, running_out)


def finish_attention(carried):
    running_max, running_sum, running_out = carried
    result = running_out / jnp.swapaxes(running_sum, -1, -2)[..., None]
    return result.astype(jnp.bfloat16)


def expert_rows(received, w_gate, w_up, w_down):
    n_here = w_gate.shape[0]
    slot_shape = received.shape
    grouped = received.reshape(slot_shape[0] // n_here, n_here, slot_shape[1], slot_shape[2])
    gate_proj = jnp.einsum("sxcd,xdf->sxcf", grouped, w_gate, preferred_element_type=jnp.float32)
    up_proj = jnp.einsum("sxcd,xdf->sxcf", grouped, w_up, preferred_element_type=jnp.float32)
    hidden = (jax.nn.silu(gate_proj) * up_proj).astype(jnp.bfloat16)
    result = jnp.einsum(
        "sxcf,xfd->sxcd", hidden, w_down, preferred_element_type=jnp.float32
    ).astype(jnp.bfloat16)
    return result.reshape(slot_shape)


def per_device(
    queries,
    keys,
    values,
    gates,
    o_proj,
    residual,
    norm_gain,
    routes,
    route_weights,
    w_gate,
    w_up,
    w_down,
):
    n_blocks = gates.shape[0]
    n_local = queries.shape[0] // BLOCK
    heads_here = queries.shape[1] // HD
    first_block = lax.axis_index("seq") * n_local
    block_ids = jnp.arange(n_blocks, dtype=jnp.int32)
    picked = jnp.any(gates[:, :, None] == block_ids[None, None, :], axis=1)
    query_loc = queries.reshape(n_local, BLOCK, heads_here, HD)
    start_state = (
        jnp.full((n_local, heads_here, BLOCK), NEG_FILL, jnp.float32),
        jnp.zeros((n_local, heads_here, BLOCK), jnp.float32),
        jnp.zeros((n_local, BLOCK, heads_here, HD), jnp.float32),
    )
    key_piece = lax.all_gather(keys, "seq", axis=0, tiled=True)
    value_piece = lax.all_gather(values, "seq", axis=0, tiled=True)
    block_count = key_piece.shape[0] // BLOCK
    key_blocks = key_piece.reshape(block_count, BLOCK, heads_here, HD)
    value_blocks = value_piece.reshape(block_count, BLOCK, heads_here, HD)

    def visit(inner_state, scanned):
        key_blk, value_blk, offset = scanned
        key_block_id = offset
        local_id = 0
        query_block_id = first_block + local_id
        current = tuple((member[local_id] for member in inner_state))

        def attend(
            held_state,
            local_id=local_id,
            key_blk=key_blk,
            value_blk=value_blk,
            key_block_id=key_block_id,
            query_block_id=query_block_id,
        ):
            return merge_partial(
                held_state,
                pair_partial(
                    query_loc[local_id], key_blk, value_blk, key_block_id == query_block_id
                ),
            )

        updated = [
            lax.cond(
                picked[query_block_id, key_block_id], attend, lambda held_state: held_state, current
            )
        ]
        stacked = tuple(
            (jnp.stack([entry[member_id] for entry in updated]) for member_id in range(3))
        )
        return (stacked, None)

    folded, unused_out = lax.scan(
        visit, start_state, (key_blocks, value_blocks, jnp.arange(block_count, dtype=jnp.int32))
    )
    attn = finish_attention(folded).reshape(n_local * BLOCK, heads_here * HD)
    tok_moe = residual.shape[0]
    summed = lax.psum_scatter(
        jnp.dot(attn, o_proj, preferred_element_type=jnp.float32).astype(jnp.bfloat16),
        "exp",
        scatter_dimension=0,
        tiled=True,
    )
    residual_sum = residual.astype(jnp.float32) + summed.astype(jnp.float32)
    norm_scale = lax.rsqrt(jnp.mean(residual_sum * residual_sum, axis=-1, keepdims=True) + 1e-06)
    moe_in = (residual_sum * norm_scale * norm_gain).astype(jnp.bfloat16)
    width = moe_in.shape[1]
    n_experts = w_gate.shape[0] * lax.axis_size("seq") * lax.axis_size("exp")
    cap = 2 * tok_moe * ROUTE_K // n_experts
    flat_routes = routes.reshape(-1)
    expert_ids = jnp.arange(n_experts, dtype=jnp.int32)
    onehot = (flat_routes[:, None] == expert_ids[None, :]).astype(jnp.int32)
    ranks = jnp.sum((jnp.cumsum(onehot, axis=0) - 1) * onehot, axis=1)
    slots = flat_routes * cap + ranks
    token_of = jnp.arange(flat_routes.shape[0], dtype=jnp.int32) // ROUTE_K
    senders = (
        jnp.zeros((n_experts * cap, width), jnp.bfloat16)
        .at[slots]
        .set(moe_in[token_of])
        .reshape(n_experts, cap, width)
    )
    produced = expert_rows(
        lax.all_to_all(senders, ("seq", "exp"), split_axis=0, concat_axis=0, tiled=True),
        w_gate,
        w_up,
        w_down,
    )
    returned = lax.all_to_all(produced, ("seq", "exp"), split_axis=0, concat_axis=0, tiled=True)
    picked_rows = returned.reshape(n_experts * cap, width)[slots]
    weighted = picked_rows.astype(jnp.float32) * route_weights.reshape(-1)[:, None]
    moe_out = jnp.sum(weighted.reshape(tok_moe, ROUTE_K, width), axis=1).astype(jnp.bfloat16)
    return (summed, moe_out)


def solution(mesh):
    in_specs = (
        P("seq", "exp"),
        P("seq", "exp"),
        P("seq", "exp"),
        P(),
        P("exp", None),
        P(("seq", "exp"), None),
        P(),
        P(("seq", "exp"), None),
        P(("seq", "exp"), None),
        P(("seq", "exp"), None, None),
        P(("seq", "exp"), None, None),
        P(("seq", "exp"), None, None),
    )
    out_specs = (P(("seq", "exp"), None), P(("seq", "exp"), None))
    return jax.shard_map(
        per_device, mesh=mesh, in_specs=in_specs, out_specs=out_specs, check_vma=False
    )
```

profile of v0, /device:TPU:5, one launch (start us, length us, event | category | flops | bytes accessed | tf_op | source)
XLA Modules:
  0.0 516.2 jit_solution(2745115614452372158)
XLA Ops:
  8.7 0.8 fusion.52
  9.5 35.4 %all-gather.3.cloned.1.call-done = bf16[8192,256]{1,0:T(8,128)(2,1)} async-done(((bf16[1024,256]{1,0:T(8,128)(2,1)}), bf16[8192,256]{1,0:T(8,128)(2,1)}) %all-gather.3.cloned.1.call-update) | async-done | bytes 4194320 | tf_op jit(solution)/shard_map/all_gather | solution.py:96
  44.9 6.9 %reshape.208 = bf16[8,1024,2,128]{3,2,1,0:T(2,128)(2,1)} reshape(bf16[8192,256]{1,0:T(8,128)(2,1)} %all-gather.3.cloned.1.call-done) | data formatting | bytes 8388608 | tf_op jit(solution)/shard_map/reshape | solution.py:99
  51.8 5.0 copy.55
  56.7 22.0 %all-gather.5.cloned.1.call-done = bf16[8192,256]{1,0:T(8,128)(2,1)} async-done(((bf16[1024,256]{1,0:T(8,128)(2,1)}), bf16[8192,256]{1,0:T(8,128)(2,1)}) %all-gather.5.cloned.1.call-update) | async-done | bytes 4194320 | tf_op jit(solution)/shard_map/all_gather | solution.py:97
  78.7 6.9 %reshape.209 = bf16[8,1024,2,128]{3,2,1,0:T(2,128)(2,1)} reshape(bf16[8192,256]{1,0:T(8,128)(2,1)} %all-gather.5.cloned.1.call-done) | data formatting | bytes 8388608 | tf_op jit(solution)/shard_map/reshape | solution.py:100
  85.7 5.0 copy.56
  90.8 50.3 %while.16 = (s32[]{:T(128)}, f32[1,2,1024]{2,1,0:T(2,128)S(1)}, f32[1,2,1024]{2,1,0:T(2,128)S(1)}, f32[1,1024,2,128]{3,1,2,0:T(8,128)S(1)}, s32[8]{0:T(128)S(1)}...) while((s32[]{:T(128)}, f32[1,2,1024]{2,1,0:T(2,128)S(1)}, ...), condition=%wide.region_6.7_spmd, body=%wide.region_1.6_spmd.sunk | while | flops 1104683008 | bytes 33154368 | solution.py:134
  94.2 11.0 %conditional.2 = (f32[1,2,1024]{2,1,0:T(2,128)S(1)}, f32[1,2,1024]{2,1,0:T(2,128)S(1)}, f32[1,1024,2,128]{3,1,2,0:T(8,128)S(1)}) conditional(s32[]{:T(128)} %bitcast.129, (f32[2,1024]{1,0:T(2,128)S(1)}, f32[2,1024]{1,0:T(2,128)S(1)}, f32[1024,2,128]{2,0,1:T(8,128)S(1)}) %tuple.76, (s32[]{:T(128)}, s32[]{:T(128)}, bf16[8,1024,2,128]{3,1,2,0:T(8,128)(2,1)}, ...), branch_computations={%region_2.2_spmd, %region_3.5_spmd} | conditional | flops 1104683008 | bytes 33154084 | solution.py:125
  95.2 2.9 fusion
  98.0 2.3 fusion.2
  100.3 4.9 add_bitcast_fusion
  108.7 11.0 %conditional.2 = (f32[1,2,1024]{2,1,0:T(2,128)S(1)}, f32[1,2,1024]{2,1,0:T(2,128)S(1)}, f32[1,1024,2,128]{3,1,2,0:T(8,128)S(1)}) conditional(s32[]{:T(128)} %bitcast.129, (f32[2,1024]{1,0:T(2,128)S(1)}, f32[2,1024]{1,0:T(2,128)S(1)}, f32[1024,2,128]{2,0,1:T(8,128)S(1)}) %tuple.76, (s32[]{:T(128)}, s32[]{:T(128)}, bf16[8,1024,2,128]{3,1,2,0:T(8,128)(2,1)}, ...), branch_computations={%region_2.2_spmd, %region_3.5_spmd} | conditional | flops 1104683008 | bytes 33154084 | solution.py:125
  109.6 2.9 fusion
  112.5 2.3 fusion.2
  114.8 4.9 add_bitcast_fusion
  141.1 1.3 copy.57
  142.4 1.3 divide_convert_fusion.1
  143.8 5.1 convolution_convert_fusion.1
  150.1 90.5 %reduce-scatter.2.cloned.1.call-done = bf16[64,3584]{1,0:T(8,128)(2,1)} async-done(((bf16[1024,3584]{1,0:T(8,128)(2,1)}), bf16[64,3584]{1,0:T(8,128)(2,1)}) %reduce-scatter.2.cloned.1.call-update) | async-done | bytes 458768 | tf_op jit(solution)/shard_map/reduce_scatter | solution.py:139
  240.6 1.3 multiply_reduce_fusion
  241.9 1.2 multiply_convert_fusion
  243.1 20.7 %scatter_custom_fusion = bf16[1024,3584]{1,0:T(8,128)(2,1)} fusion(s32[512]{0:T(512)S(1)} %bitcast.147, bf16[64,3584]{1,0:T(8,128)(2,1)S(1)} %multiply_convert_fusion, s32[1024]{0:T(1024)S(1)} %pad_clamp_fusion.1, bf16[]{:T(256)} %constant.91.clone.1), kind=kCustom, calls=%fused_computation.51 | custom fusion | bytes 7340034 | tf_op jit(solution)/shard_map/scatter | solution.py:160
  263.8 94.9 %all_to_all.10 = bf16[128,8,3584]{2,1,0:T(8,128)(2,1)S(1)} all-to-all(bf16[128,8,3584]{2,1,0:T(8,128)(2,1)} %bitcast.133), channel_id=1, replica_groups=mesh['seq'=8,'exp'=16] {'seq','exp'}, dimensions={0} | all-to-all | bytes 14680064 | tf_op jit(solution)/shard_map/all_to_all | solution.py:164
  358.7 10.1 %fusion.30 = f32[128,8,1024]{2,0,1:T(8,128)S(1)} fusion(bf16[1,3584,1024]{2,1,0:T(8,128)(2,1)} %param.26, bf16[128,8,3584]{2,1,0:T(8,128)(2,1)S(1)} %all_to_all.10), kind=kOutput, calls=%fused_computation.38 | convolution fusion | flops 7516192768 | bytes 18874368 | tf_op jit(solution)/shard_map/sxcd,xdf->sxcf/dot_general | solution.py:62
  368.9 8.5 %fusion.36 = bf16[128,1,8,1024]{3,0,2,1:T(8,128)(2,1)S(1)} fusion(f32[128,8,1024]{2,0,1:T(8,128)S(1)} %fusion.30, bf16[1,3584,1024]{2,1,0:T(8,128)(2,1)S(1)} %bitcast.151, bf16[128,8,3584]{2,1,0:T(8,128)(2,1)S(1)} %all_to_all.10), kind=kOutput, calls=%fused_computation.45 | convolution fusion | flops 7522484224 | bytes 20971520 | tf_op jit(solution)/shard_map/sxcd,xdf->sxcf/dot_general | solution.py:61
  377.4 11.3 %convolution_convert_fusion = bf16[128,8,3584]{2,0,1:T(8,128)(2,1)S(1)} fusion(bf16[1,1024,3584]{2,1,0:T(8,128)(2,1)} %param.27, bf16[128,1,8,1024]{3,0,2,1:T(8,128)(2,1)S(1)} %fusion.36), kind=kOutput, calls=%fused_computation.33 | convolution fusion | flops 7519862784 | bytes 16777216 | tf_op jit(solution)/shard_map/sxcf,xfd->sxcd/dot_general | solution.py:64
  388.7 7.0 %copy.65 = bf16[128,8,3584]{2,1,0:T(8,128)(2,1)} copy(bf16[128,8,3584]{2,0,1:T(8,128)(2,1)S(1)} %convolution_convert_fusion) | data formatting | bytes 14680064 | tf_op jit(solution)/shard_map/convert_element_type | solution.py:66
  395.8 6.1 %all-to-all-start.1 = ((bf16[128,8,3584]{2,1,0:T(8,128)(2,1)}), bf16[128,8,3584]{2,1,0:T(8,128)(2,1)}, u32[]{:S(2)}, u32[]{:S(2)}) async-start(bf16[128,8,3584]{2,1,0:T(8,128)(2,1)} %copy.65), calls=%async_computation.2 | async-start | bytes 14680064 | tf_op jit(solution)/shard_map/all_to_all | solution.py:169
  401.9 89.4 %all-to-all-done.1 = bf16[128,8,3584]{2,1,0:T(8,128)(2,1)} async-done(((bf16[128,8,3584]{2,1,0:T(8,128)(2,1)}), bf16[128,8,3584]{2,1,0:T(8,128)(2,1)}, u32[]{:S(2)}, u32[]{:S(2)}) %all-to-all-start.1) | async-done | bytes 7340064 | tf_op jit(solution)/shard_map/all_to_all | solution.py:169
  491.3 12.1 %gather_fusion = bf16[512,3584]{1,0:T(8,128)(2,1)} fusion(bf16[1024,3584]{1,0:T(8,128)(2,1)} %bitcast.43, s32[1024]{0:T(1024)S(1)} %pad_clamp_fusion), kind=kCustom, calls=%fused_computation.1 | custom fusion | bytes 7342080 | tf_op jit(solution)/shard_map/gather | solution.py:170
  503.4 5.8 %fusion.28 = bf16[64,3584]{1,0:T(8,128)(2,1)} fusion(bf16[512,3584]{1,0:T(8,128)(2,1)} %gather_fusion, f32[64,8]{1,0:T(8,128)S(1)} %copy.66), kind=kLoop, calls=%fused_computation.36 | loop fusion | flops 5275648 | bytes 4130816 | tf_op jit(solution)/shard_map/reduce_sum | solution.py:172
  (75 shorter events, 12.9 us)
Async XLA Ops:
  7.2 136.6 %copy-start = (bf16[256,3584]{1,0:T(8,128)(2,1)S(1)}, bf16[256,3584]{1,0:T(8,128)(2,1)}, u32[]{:S(2)}) copy-start(bf16[256,3584]{1,0:T(8,128)(2,1)} %param.20) | copy-start | bytes 5505028
  7.2 37.7 %all-gather.3.cloned.1.call-start = ((), (), s32[]{:S(2)}) async-start(), calls=%async_computation.3 | async-start | bytes 4718592 | tf_op jit(solution)/shard_map/all_gather | solution.py:96
  7.9 70.8 %all-gather.5.cloned.1.call-start = ((), (), s32[]{:S(2)}) async-start(), calls=%async_computation.4 | async-start | bytes 4718592 | tf_op jit(solution)/shard_map/all_gather | solution.py:97
  8.7 231.9 %reduce-scatter.2.cloned.1.call-start = ((), (), s32[]{:S(2)}) async-start(), calls=%async_computation.5 | async-start | bytes 7798784 | tf_op jit(solution)/shard_map/reduce_scatter | solution.py:139
  56.7 34.0 %copy-start.6 = (bf16[1024,256]{1,0:T(8,128)(2,1)S(1)}, bf16[1024,256]{1,0:T(8,128)(2,1)}, u32[]{:S(2)}) copy-start(bf16[1024,256]{1,0:T(8,128)(2,1)} %param.16) | copy-start | bytes 1572868
  143.8 5.1 copy-start.4
  148.8 91.7 %copy-start.2 = (bf16[64,3584]{1,0:T(8,128)(2,1)S(1)}, bf16[64,3584]{1,0:T(8,128)(2,1)}, u32[]{:S(2)}) copy-start(bf16[64,3584]{1,0:T(8,128)(2,1)} %param.21) | copy-start | bytes 1376260
  148.9 93.0 %copy-start.3 = (f32[3584]{0:T(1024)S(1)}, f32[3584]{0:T(1024)}, u32[]{:S(2)}) copy-start(f32[3584]{0:T(1024)} %param.22) | copy-start | bytes 43012
  263.8 105.1 %slice-start = ((s8[7340032]{0:T(1024)(128)(4,1)}), s8[4194304]{0:T(1024)(128)(4,1)S(1)}, s32[]{:S(2)}) async-start(s8[7340032]{0:T(1024)(128)(4,1)} %bitcast.150), calls=%async_computation.6 | async-start | bytes 8388608
  358.7 10.1 %slice-start.1 = ((s8[7340032]{0:T(1024)(128)(4,1)}), s8[3145728]{0:T(1024)(128)(4,1)S(1)}, s32[]{:S(2)}) async-start(s8[7340032]{0:T(1024)(128)(4,1)} %bitcast.150), calls=%async_computation.7 | async-start | bytes 6291456
  395.8 6.1 %copy-start.5 = (f32[64,8]{0,1:T(8,128)S(1)}, f32[64,8]{0,1:T(8,128)}, u32[]{:S(2)}) copy-start(f32[64,8]{0,1:T(8,128)} %param.24) | copy-start | bytes 6148
  395.8 95.6 %all-to-all-start.1 = ((bf16[128,8,3584]{2,1,0:T(8,128)(2,1)}), bf16[128,8,3584]{2,1,0:T(8,128)(2,1)}, u32[]{:S(2)}, u32[]{:S(2)}) async-start(bf16[128,8,3584]{2,1,0:T(8,128)(2,1)} %copy.65), calls=%async_computation.2 | async-start | bytes 14680064 | tf_op jit(solution)/shard_map/all_to_all | solution.py:169
  491.3 17.9 %copy-start.1 = (bf16[256,3584]{1,0:T(8,128)(2,1)S(1)}, bf16[256,3584]{1,0:T(8,128)(2,1)}, u32[]{:S(2)}) copy-start(bf16[256,3584]{1,0:T(8,128)(2,1)} %param.20) | copy-start | bytes 5505028
Sparse Core Ops, SparseCore 0:
  9.7 35.0 all-gather.2
  46.6 32.1 all-gather.4
  149.0 91.5 reduce-scatter.1
where the time goes:
time: 524 us; the launch traced here: 516 us
  waiting for transfers between devices  239 us (46%)
  blocking collectives  94.9 us (18%)
  local copies, waits for them, and re-layouts  75 us (14%)
  matrix products  50.6 us (10%)
  loops' own time  20.3 us (4%)
  other arithmetic  16.1 us (3%)
  between operations  14.4 us (3%)
  starting transfers between devices  6.17 us (1%)
    all_to_all x1, blocking collectives, per_device(): lax.all_to_all(senders, ('seq', 'exp'), split_axis=0, concat_axis=0, tile...  94.9 us
    reduce_scatter x1, waiting for transfers between devices, per_device(): lax.psum_scatter(jnp.dot(attn, o_proj, preferred_element_type=jnp.float32...  90.5 us
    all_to_all x1, waiting for transfers between devices, per_device(): lax.all_to_all(produced, ('seq', 'exp'), split_axis=0, concat_axis=0, til...  89.4 us
    all_gather x1, waiting for transfers between devices, per_device(): key_piece = lax.all_gather(keys, 'seq', axis=0, tiled=True)  35.4 us
    all_gather x1, waiting for transfers between devices, per_device(): value_piece = lax.all_gather(values, 'seq', axis=0, tiled=True)  22 us
    scatter x1, local copies, waits for them, and re-layouts, per_device(): senders = jnp.zeros((n_experts * cap, width), jnp.bfloat16).at[slots].set...  20.7 us
    another operation x1, loops' own time, per_device(): lax.scan(visit, start_state, (key_blocks, value_blocks, jnp.arange(block_...  19 us
    gather x1, local copies, waits for them, and re-layouts, per_device(): picked_rows = returned.reshape(n_experts * cap, width)[slots]  12.1 us
  transfers between devices with their start and end apart: 4, of which 4 were waited for; matrix products, arithmetic and copies ran while one was open for 3% of the time, Pallas kernels for 0%

commit v1 on v0

--- a/solution.py
+++ b/solution.py
@@ -3,6 +3,8 @@
 import jax
 import jax.numpy as jnp
 from jax import lax
+from jax.experimental import pallas as pl
+from jax.experimental.pallas import tpu as pltpu
 from jax.sharding import PartitionSpec as P
 
 HD = 128
@@ -54,17 +56,93 @@
     return result.astype(jnp.bfloat16)
 
 
-def expert_rows(received, w_gate, w_up, w_down):
-    n_here = w_gate.shape[0]
-    slot_shape = received.shape
-    grouped = received.reshape(slot_shape[0] // n_here, n_here, slot_shape[1], slot_shape[2])
-    gate_proj = jnp.einsum("sxcd,xdf->sxcf", grouped, w_gate, preferred_element_type=jnp.float32)
-    up_proj = jnp.einsum("sxcd,xdf->sxcf", grouped, w_up, preferred_element_type=jnp.float32)
-    hidden = (jax.nn.silu(gate_proj) * up_proj).astype(jnp.bfloat16)
-    result = jnp.einsum(
-        "sxcf,xfd->sxcd", hidden, w_down, preferred_element_type=jnp.float32
-    ).astype(jnp.bfloat16)
-    return result.reshape(slot_shape)
+def expert_kernel(n_ff, rows_ref, gate_ref, up_ref, down_ref, out_ref, hidden_ref):
+    step = pl.program_id(0)
+    n_rows = rows_ref.shape[0]
+    ff_tile = gate_ref.shape[2]
+    row_tile = 256
+
+    @pl.when(step < n_ff)
+    def _():
+        @pl.loop(0, n_rows // row_tile)
+        def _(i):
+            at = pl.ds(pl.multiple_of(i * row_tile, row_tile), row_tile)
+            rows = rows_ref[at, :]
+            gate = jnp.dot(rows, gate_ref[0], preferred_element_type=jnp.float32)
+            up = jnp.dot(rows, up_ref[0], preferred_element_type=jnp.float32)
+            hidden = gate / (1.0 + jnp.exp(-gate)) * up
+            cols = pl.ds(pl.multiple_of(step * ff_tile, ff_tile), ff_tile)
+            hidden_ref[at, cols] = hidden.astype(jnp.bfloat16)
+
+    @pl.when(step >= n_ff)
+    def _():
+        @pl.loop(0, n_rows // row_tile)
+        def _(i):
+            at = pl.ds(pl.multiple_of(i * row_tile, row_tile), row_tile)
+            out_ref[at, :] = jnp.dot(
+                hidden_ref[at, :], down_ref[0], preferred_element_type=jnp.float32
+            ).astype(jnp.bfloat16)
+
+
+def expert_rows(rows, w_gate, w_up, w_down):
+    n_rows, width = rows.shape
+    ff = w_gate.shape[2]
+    ff_tile, out_tile = 256, 512
+    n_ff, n_out = ff // ff_tile, width // out_tile
+
+    def ff_at(i):
+        return (0, 0, jnp.minimum(i, n_ff - 1))
+
+    def out_at(i):
+        return jnp.maximum(i - n_ff, 0)
+
+    return pl.pallas_call(
+        lambda *refs: expert_kernel(n_ff, *refs),
+        grid=(n_ff + n_out,),
+        in_specs=[
+            pl.BlockSpec((n_rows, width), lambda i: (0, 0)),
+            pl.BlockSpec((1, width, ff_tile), ff_at),
+            pl.BlockSpec((1, width, ff_tile), ff_at),
+            pl.BlockSpec((1, ff, out_tile), lambda i: (0, 0, out_at(i))),
+        ],
+        out_specs=pl.BlockSpec((n_rows, out_tile), lambda i: (0, out_at(i))),
+        out_shape=jax.ShapeDtypeStruct((n_rows, width), jnp.bfloat16),
+        scratch_shapes=[pltpu.VMEM((n_rows, ff), jnp.bfloat16)],
+        compiler_params=pltpu.CompilerParams(vmem_limit_bytes=44 * 1024 * 1024),
+        cost_estimate=pl.CostEstimate(
+            flops=6 * n_rows * width * ff,
+            bytes_accessed=2 * (2 * n_rows * width + 3 * width * ff),
+            transcendentals=n_rows * ff,
+        ),
+        name="experts",
+    )(rows, w_gate, w_up, w_down)
+
+
+def slot_tables(routes, route_weights, n_experts, cap):
+    n_tok = routes.shape[0]
+    expert_ids = lax.broadcasted_iota(jnp.int32, (n_experts, n_tok), 0)
+    hit = jnp.zeros((n_experts, n_tok), jnp.bool_)
+    weight = jnp.zeros((n_experts, n_tok), jnp.float32)
+    for k in range(routes.shape[1]):
+        match = routes[:, k][None, :] == expert_ids
+        hit = jnp.logical_or(hit, match)
+        weight = weight + jnp.where(match, route_weights[:, k][None, :], 0.0)
+    ahead = lax.broadcasted_iota(jnp.int32, (n_tok, n_tok), 0) < lax.broadcasted_iota(
+        jnp.int32, (n_tok, n_tok), 1
+    )
+    rank = jnp.dot(
+        hit.astype(jnp.bfloat16), ahead.astype(jnp.bfloat16), preferred_element_type=jnp.float32
+    ).astype(jnp.int32)
+    slot_ids = lax.broadcasted_iota(jnp.int32, (n_experts, cap, n_tok), 1)
+    taken = jnp.logical_and(hit[:, None, :], rank[:, None, :] == slot_ids)
+    place = taken.astype(jnp.bfloat16).reshape(n_experts * cap, n_tok)
+    high = weight.astype(jnp.bfloat16)
+    low = (weight - high.astype(jnp.float32)).astype(jnp.bfloat16)
+    zero = jnp.zeros((), jnp.bfloat16)
+    mix = jnp.concatenate(
+        [jnp.where(taken, high[:, None, :], zero), jnp.where(taken, low[:, None, :], zero)], axis=2
+    ).reshape(n_experts * cap, 2 * n_tok)
+    return place, mix
 
 
 def per_device(
@@ -148,28 +226,30 @@
     width = moe_in.shape[1]
     n_experts = w_gate.shape[0] * lax.axis_size("seq") * lax.axis_size("exp")
     cap = 2 * tok_moe * ROUTE_K // n_experts
-    flat_routes = routes.reshape(-1)
-    expert_ids = jnp.arange(n_experts, dtype=jnp.int32)
-    onehot = (flat_routes[:, None] == expert_ids[None, :]).astype(jnp.int32)
-    ranks = jnp.sum((jnp.cumsum(onehot, axis=0) - 1) * onehot, axis=1)
-    slots = flat_routes * cap + ranks
-    token_of = jnp.arange(flat_routes.shape[0], dtype=jnp.int32) // ROUTE_K
-    senders = (
-        jnp.zeros((n_experts * cap, width), jnp.bfloat16)
-        .at[slots]
-        .set(moe_in[token_of])
-        .reshape(n_experts, cap, width)
-    )
-    produced = expert_rows(
-        lax.all_to_all(senders, ("seq", "exp"), split_axis=0, concat_axis=0, tiled=True),
-        w_gate,
-        w_up,
-        w_down,
-    )
-    returned = lax.all_to_all(produced, ("seq", "exp"), split_axis=0, concat_axis=0, tiled=True)
-    picked_rows = returned.reshape(n_experts * cap, width)[slots]
-    weighted = picked_rows.astype(jnp.float32) * route_weights.reshape(-1)[:, None]
-    moe_out = jnp.sum(weighted.reshape(tok_moe, ROUTE_K, width), axis=1).astype(jnp.bfloat16)
+    place, mix = slot_tables(routes, route_weights, n_experts, cap)
+    senders = jnp.dot(place, moe_in, preferred_element_type=jnp.float32).astype(jnp.bfloat16)
+    received = lax.all_to_all(
+        senders.reshape(n_experts, cap, width),
+        ("seq", "exp"),
+        split_axis=0,
+        concat_axis=0,
+        tiled=True,
+    )
+    produced = expert_rows(received.reshape(n_experts * cap, width), w_gate, w_up, w_down)
+    returned = lax.all_to_all(
+        produced.reshape(n_experts, cap, width),
+        ("seq", "exp"),
+        split_axis=0,
+        concat_axis=0,
+        tiled=True,
+    )
+    halves = lax.dot_general(
+        mix,
+        returned.reshape(n_experts * cap, width),
+        (((0,), (0,)), ((), ())),
+        preferred_element_type=jnp.float32,
+    )
+    moe_out = (halves[:tok_moe] + halves[tok_moe:]).astype(jnp.bfloat16)
     return (summed, moe_out)
 
 

time: 524 us -> 491 us (0.937); the launches traced: 516 us -> 489 us
  local copies, waits for them, and re-layouts: 75 us -> 37.8 us
  Pallas kernels: 0 us -> 36.5 us
  matrix products: 50.6 us -> 32.2 us
  other arithmetic: 16.1 us -> 9.85 us
    pallas_call x0 -> x1, Pallas kernels: none -> 36.5 us  [expert_rows(): pl.pallas_call(lambda *refs: expert_kernel(n_ff, *refs), grid=(n_ff + n_o...]
    scatter x1 -> x0, local copies, waits for them, and re-layouts: 20.7 us -> none  [per_device(): senders = jnp.zeros((n_experts * cap, width), jnp.bfloat16).at[slots].set...]
    dot_general x3, matrix products: 30 us -> 11.6 us  [the longest x1 7.59 us: per_device(): lax.dot_general(mix, returned.reshape(n_experts * cap, width), (((0,), (0...]
    gather x1 -> x0, local copies, waits for them, and re-layouts: 12.1 us -> none  [per_device(): picked_rows = returned.reshape(n_experts * cap, width)[slots]]
    convert_element_type x1 -> x0, local copies, waits for them, and re-layouts: 7.04 us -> none  [expert_rows(): result = jnp.einsum('sxcf,xfd->sxcd', hidden, w_down, preferred_element_t...]
    reduce_sum x2 -> x0, other arithmetic: 6.05 us -> none  [the longest x1 5.82 us: per_device(): jnp.sum(weighted.reshape(tok_moe, ROUTE_K, width), axis=1)]
where the time goes in v1:
time: 491 us; the launch traced here: 489 us
  waiting for transfers between devices  239 us (49%)
  blocking collectives  94.6 us (19%)
  local copies, waits for them, and re-layouts  37.8 us (8%)
  Pallas kernels  36.5 us (7%)
  matrix products  32.2 us (7%)
  loops' own time  19.5 us (4%)
  between operations  14 us (3%)
  other arithmetic  9.85 us (2%)
  starting transfers between devices  6.17 us (1%)
    all_to_all x1, blocking collectives, per_device(): lax.all_to_all(senders.reshape(n_experts, cap, width), ('seq', 'exp'), sp...  94.6 us
    reduce_scatter x1, waiting for transfers between devices, per_device(): lax.psum_scatter(jnp.dot(attn, o_proj, preferred_element_type=jnp.float32...  90.9 us
    all_to_all x1, waiting for transfers between devices, per_device(): lax.all_to_all(produced.reshape(n_experts, cap, width), ('seq', 'exp'), s...  89.2 us
    pallas_call x1, Pallas kernels, expert_rows(): pl.pallas_call(lambda *refs: expert_kernel(n_ff, *refs), grid=(n_ff + n_o...  36.5 us
    all_gather x1, waiting for transfers between devices, per_device(): key_piece = lax.all_gather(keys, 'seq', axis=0, tiled=True)  35.4 us
    all_gather x1, waiting for transfers between devices, per_device(): value_piece = lax.all_gather(values, 'seq', axis=0, tiled=True)  22 us
    another operation x1, loops' own time, per_device(): lax.scan(visit, start_state, (key_blocks, value_blocks, jnp.arange(block_...  18.2 us
    while x3, local copies, waits for them, and re-layouts, per_device(): lax.scan(visit, start_state, (key_blocks, value_blocks, jnp.arange(block_...  11.3 us
  transfers between devices with their start and end apart: 4, of which 4 were waited for; matrix products, arithmetic and copies ran while one was open for 3% of the time, Pallas kernels for 0%

profile of v1, /device:TPU:5, one launch (start us, length us, event | category | flops | bytes accessed | tf_op | source)
XLA Modules:
  0.0 489.4 jit_solution(12933596659608805883)
XLA Ops:
  7.2 0.7 all-gather.3.cloned.1.call-update
  8.0 0.7 all-gather.5.cloned.1.call-update
  8.7 0.8 fusion.56
  9.5 35.4 %all-gather.3.cloned.1.call-done = bf16[8192,256]{1,0:T(8,128)(2,1)} async-done(((bf16[1024,256]{1,0:T(8,128)(2,1)}), bf16[8192,256]{1,0:T(8,128)(2,1)}) %all-gather.3.cloned.1.call-update) | async-done | bytes 4194320 | tf_op jit(solution)/shard_map/all_gather | solution.py:174
  44.9 6.9 %reshape.648 = bf16[8,1024,2,128]{3,2,1,0:T(2,128)(2,1)} reshape(bf16[8192,256]{1,0:T(8,128)(2,1)} %all-gather.3.cloned.1.call-done) | data formatting | bytes 8388608 | tf_op jit(solution)/shard_map/reshape | solution.py:177
  51.7 5.0 %copy.44 = bf16[8,1024,2,128]{3,1,2,0:T(8,128)(2,1)} copy(bf16[8,1024,2,128]{3,2,1,0:T(2,128)(2,1)} %reshape.648) | data formatting | bytes 8388608 | tf_op jit(solution)/shard_map/while | solution.py:212
  56.7 22.0 %all-gather.5.cloned.1.call-done = bf16[8192,256]{1,0:T(8,128)(2,1)} async-done(((bf16[1024,256]{1,0:T(8,128)(2,1)}), bf16[8192,256]{1,0:T(8,128)(2,1)}) %all-gather.5.cloned.1.call-update) | async-done | bytes 4194320 | tf_op jit(solution)/shard_map/all_gather | solution.py:175
  78.7 6.9 %reshape.649 = bf16[8,1024,2,128]{3,2,1,0:T(2,128)(2,1)} reshape(bf16[8192,256]{1,0:T(8,128)(2,1)} %all-gather.5.cloned.1.call-done) | data formatting | bytes 8388608 | tf_op jit(solution)/shard_map/reshape | solution.py:178
  85.6 5.0 %copy.45 = bf16[8,1024,2,128]{3,1,2,0:T(8,128)(2,1)} copy(bf16[8,1024,2,128]{3,2,1,0:T(2,128)(2,1)} %reshape.649) | data formatting | bytes 8388608 | tf_op jit(solution)/shard_map/while | solution.py:212
  90.7 49.6 %while.16 = (s32[]{:T(128)}, f32[1,2,1024]{2,1,0:T(2,128)S(1)}, f32[1,2,1024]{2,1,0:T(2,128)S(1)}, f32[1,1024,2,128]{3,1,2,0:T(8,128)S(1)}, s32[8]{0:T(128)S(1)}...) while((s32[]{:T(128)}, f32[1,2,1024]{2,1,0:T(2,128)S(1)}, ...), condition=%wide.region_6.7_spmd, body=%wide.region_1.6_spmd.sunk | while | flops 1104683008 | bytes 33154376 | solution.py:212
  93.0 0.6 dynamic_slice.43
  94.2 11.0 %conditional.2 = (f32[1,2,1024]{2,1,0:T(2,128)S(1)}, f32[1,2,1024]{2,1,0:T(2,128)S(1)}, f32[1,1024,2,128]{3,1,2,0:T(8,128)S(1)}) conditional(s32[]{:T(128)} %bitcast.119, (f32[2,1024]{1,0:T(2,128)S(1)}, f32[2,1024]{1,0:T(2,128)S(1)}, f32[1024,2,128]{2,0,1:T(8,128)S(1)}) %tuple.92, (s32[]{:T(128)}, s32[]{:T(128)}, bf16[8,1024,2,128]{3,1,2,0:T(8,128)(2,1)}, ...), branch_computations={%region_2.2_spmd, %region_3.5_spmd} | conditional | flops 1104683008 | bytes 33154084 | solution.py:203
  95.1 2.9 fusion
  98.0 2.3 fusion.2
  100.3 4.9 add_bitcast_fusion
  108.6 11.0 %conditional.2 = (f32[1,2,1024]{2,1,0:T(2,128)S(1)}, f32[1,2,1024]{2,1,0:T(2,128)S(1)}, f32[1,1024,2,128]{3,1,2,0:T(8,128)S(1)}) conditional(s32[]{:T(128)} %bitcast.119, (f32[2,1024]{1,0:T(2,128)S(1)}, f32[2,1024]{1,0:T(2,128)S(1)}, f32[1024,2,128]{2,0,1:T(8,128)S(1)}) %tuple.92, (s32[]{:T(128)}, s32[]{:T(128)}, bf16[8,1024,2,128]{3,1,2,0:T(8,128)(2,1)}, ...), branch_computations={%region_2.2_spmd, %region_3.5_spmd} | conditional | flops 1104683008 | bytes 33154084 | solution.py:203
  109.5 2.9 fusion
  112.4 2.3 fusion.2
  114.7 4.9 add_bitcast_fusion
  140.3 1.3 copy.46
  141.6 1.3 divide_convert_fusion.1
  143.0 5.0 %convolution_convert_fusion.1 = bf16[1024,3584]{1,0:T(8,128)(2,1)} fusion(bf16[1024,256]{0,1:T(8,128)(2,1)S(1)} %bitcast.128, bf16[256,3584]{1,0:T(8,128)(2,1)S(1)} %copy-done), kind=kOutput, calls=%fused_computation.31 | convolution fusion | flops 1882718208 | bytes 9699328 | tf_op jit(solution)/shard_map/dot_general | solution.py:218
  148.8 90.9 %reduce-scatter.2.cloned.1.call-done = bf16[64,3584]{1,0:T(8,128)(2,1)} async-done(((bf16[1024,3584]{1,0:T(8,128)(2,1)}), bf16[64,3584]{1,0:T(8,128)(2,1)}) %reduce-scatter.2.cloned.1.call-update) | async-done | bytes 458768 | tf_op jit(solution)/shard_map/reduce_scatter | solution.py:217
  239.7 1.3 multiply_reduce_fusion
  241.0 3.7 fusion.30
  244.7 94.6 %all_to_all.10 = bf16[128,8,3584]{2,1,0:T(8,128)(2,1)} all-to-all(bf16[128,8,3584]{2,1,0:T(8,128)(2,1)S(1)} %fusion.30), channel_id=1, replica_groups=mesh['seq'=8,'exp'=16] {'seq','exp'}, dimensions={0} | all-to-all | bytes 14680064 | tf_op jit(solution)/shard_map/all_to_all | solution.py:231
  339.3 36.5 %experts.1 = bf16[1024,3584]{1,0:T(8,128)(2,1)S(1)} custom-call(bf16[1024,3584]{1,0:T(8,128)(2,1)} %bitcast.124, bf16[1,3584,1024]{2,1,0:T(8,128)(2,1)} %refs_1_.1, bf16[1,3584,1024]{2,1,0:T(8,128)(2,1)} %refs_2_.1, bf16[1,1024,3584]{2,1,0:T(8,128)(2,1)} %refs_3_.1), custom_call_target="tpu_custom_call" | custom-call | flops 22548578304 | bytes 36700160 | tf_op jit(solution)/shard_map/experts/pallas_call | solution.py:99
  375.8 3.0 copy-done.1
  378.8 6.1 %all-to-all-start.1 = ((bf16[128,8,3584]{2,1,0:T(8,128)(2,1)}), bf16[128,8,3584]{2,1,0:T(8,128)(2,1)}, u32[]{:S(2)}, u32[]{:S(2)}) async-start(bf16[128,8,3584]{2,1,0:T(8,128)(2,1)} %bitcast.123), calls=%async_computation.2 | async-start | bytes 14680064 | tf_op jit(solution)/shard_map/all_to_all | solution.py:239
  385.2 89.2 %all-to-all-done.1 = bf16[128,8,3584]{2,1,0:T(8,128)(2,1)} async-done(((bf16[128,8,3584]{2,1,0:T(8,128)(2,1)}), bf16[128,8,3584]{2,1,0:T(8,128)(2,1)}, u32[]{:S(2)}, u32[]{:S(2)}) %all-to-all-start.1) | async-done | bytes 7340064 | tf_op jit(solution)/shard_map/all_to_all | solution.py:239
  474.4 7.6 %fusion.31 = f32[128,3584]{1,0:T(8,128)S(1)} fusion(bf16[128,8,3584]{2,1,0:T(8,128)(2,1)} %all-to-all-done.1, bf16[128,8,64]{0,2,1:T(8,128)(2,1)S(1)} %get-tuple-element.286, bf16[128,8,64]{0,2,1:T(8,128)(2,1)S(1)} %get-tuple-element.285), kind=kOutput, calls=%fused_computation.35 | convolution fusion | flops 940048384 | bytes 9437184 | tf_op jit(solution)/shard_map/dot_general | solution.py:246
  482.0 0.9 fusion.34
  (57 shorter events, 10.8 us)
Async XLA Ops:
  7.2 135.8 %copy-start = (bf16[256,3584]{1,0:T(8,128)(2,1)S(1)}, bf16[256,3584]{1,0:T(8,128)(2,1)}, u32[]{:S(2)}) copy-start(bf16[256,3584]{1,0:T(8,128)(2,1)} %param.20) | copy-start | bytes 5505028
  7.2 37.7 %all-gather.3.cloned.1.call-start = ((), (), s32[]{:S(2)}) async-start(), calls=%async_computation.3 | async-start | bytes 4718592 | tf_op jit(solution)/shard_map/all_gather | solution.py:174
  7.9 70.8 %all-gather.5.cloned.1.call-start = ((), (), s32[]{:S(2)}) async-start(), calls=%async_computation.4 | async-start | bytes 4718592 | tf_op jit(solution)/shard_map/all_gather | solution.py:175
  8.7 231.0 %reduce-scatter.2.cloned.1.call-start = ((), (), s32[]{:S(2)}) async-start(), calls=%async_computation.5 | async-start | bytes 7798784 | tf_op jit(solution)/shard_map/reduce_scatter | solution.py:217
  56.7 34.0 %copy-start.6 = (bf16[1024,256]{1,0:T(8,128)(2,1)S(1)}, bf16[1024,256]{1,0:T(8,128)(2,1)}, u32[]{:S(2)}) copy-start(bf16[1024,256]{1,0:T(8,128)(2,1)} %param.16) | copy-start | bytes 1572868
  142.9 5.1 %copy-start.4 = (s32[64,8]{0,1:T(8,128)S(1)}, s32[64,8]{0,1:T(8,128)}, u32[]{:S(2)}) copy-start(s32[64,8]{0,1:T(8,128)} %param.23) | copy-start | bytes 6148
  142.9 96.8 %copy-start.2 = (bf16[64,3584]{1,0:T(8,128)(2,1)S(1)}, bf16[64,3584]{1,0:T(8,128)(2,1)}, u32[]{:S(2)}) copy-start(bf16[64,3584]{1,0:T(8,128)(2,1)} %param.21) | copy-start | bytes 1376260
  148.0 93.0 %copy-start.3 = (f32[3584]{0:T(1024)S(1)}, f32[3584]{0:T(1024)}, u32[]{:S(2)}) copy-start(f32[3584]{0:T(1024)} %param.22) | copy-start | bytes 43012
  375.8 3.0 copy-start.1
  378.8 6.1 %copy-start.5 = (f32[64,8]{0,1:T(8,128)S(1)}, f32[64,8]{0,1:T(8,128)}, u32[]{:S(2)}) copy-start(f32[64,8]{0,1:T(8,128)} %param.24) | copy-start | bytes 6148
  378.8 95.6 %all-to-all-start.1 = ((bf16[128,8,3584]{2,1,0:T(8,128)(2,1)}), bf16[128,8,3584]{2,1,0:T(8,128)(2,1)}, u32[]{:S(2)}, u32[]{:S(2)}) async-start(bf16[128,8,3584]{2,1,0:T(8,128)(2,1)} %bitcast.123), calls=%async_computation.2 | async-start | bytes 14680064 | tf_op jit(solution)/shard_map/all_to_all | solution.py:239
Sparse Core Ops, SparseCore 0:
  9.7 35.0 all-gather.2
  46.6 32.1 all-gather.4
  148.2 91.5 reduce-scatter.1

commit v2 on v1

v2 whole, which is shorter than its diff:
```python
import math

import jax
import jax.numpy as jnp
from jax import lax
from jax.experimental import pallas as pl
from jax.experimental.pallas import tpu as pltpu
from jax.sharding import PartitionSpec as P

HD = 128
BLOCK = 1024
ROUTE_K = 8


NEG_FILL = -1e30
SCALE = math.log2(math.e) / math.sqrt(HD)
Q_TILE = 256
CORES = 2
SIDE = 4


def dot_t(a, b):
    return lax.dot_general(a, b, (((1,), (1,)), ((), ())), preferred_element_type=jnp.float32)


def own_kernel(q_ref, k_ref, v_ref, top_ref, sum_ref, acc_ref):
    for i in range(q_ref.shape[0] // Q_TILE):
        at = pl.ds(i * Q_TILE, Q_TILE)
        seen = pl.ds(0, (i + 1) * Q_TILE)
        scores = dot_t(q_ref[at, :], k_ref[seen, :])
        query_pos = lax.broadcasted_iota(jnp.int32, scores.shape, 0) + i * Q_TILE
        key_pos = lax.broadcasted_iota(jnp.int32, scores.shape, 1)
        scores = jnp.where(key_pos <= query_pos, scores, NEG_FILL)
        top = jnp.max(scores, axis=1, keepdims=True)
        weights = jnp.exp2((scores - top) * SCALE)
        top_ref[at, :] = jnp.broadcast_to(top, (Q_TILE, HD))
        sum_ref[at, :] = jnp.broadcast_to(jnp.sum(weights, axis=1, keepdims=True), (Q_TILE, HD))
        acc_ref[at, :] = jnp.dot(
            weights.astype(jnp.bfloat16), v_ref[seen, :], preferred_element_type=jnp.float32
        )


def attend_own(queries, keys, values):
    n, width = queries.shape
    spec = pl.BlockSpec((n, HD), lambda h: (0, h))
    state = jax.ShapeDtypeStruct((n, width), jnp.float32)
    return pl.pallas_call(
        own_kernel,
        grid=(width // HD,),
        in_specs=[spec] * 3,
        out_specs=[spec] * 3,
        out_shape=[state] * 3,
        compiler_params=pltpu.CompilerParams(vmem_limit_bytes=32 * 1024 * 1024),
        cost_estimate=pl.CostEstimate(
            flops=8 * n * n * width, bytes_accessed=18 * n * width, transcendentals=n * n
        ),
        name="attend_own",
    )(queries, keys, values)


def far_kernel(code_ref, q_ref, top_ref, sum_ref, acc_ref, *refs):
    near, swapped, out_ref = refs[:-6], refs[-6], refs[-5]
    held, tops, sums, accs = refs[-4:]
    tops[...] = top_ref[...]
    sums[...] = sum_ref[...]
    accs[...] = acc_ref[...]
    for j in range(swapped.shape[0]):
        code = code_ref[j]
        for s in range(len(near)):

            @pl.when(code == s + 1)
            def _(s=s):
                held[...] = near[s][...]

        @pl.when(code == len(near) + 1)
        def _(j=j):
            held[...] = swapped[j]

        @pl.when(code > 0)
        def _():
            for i in range(q_ref.shape[0] // Q_TILE):
                at = pl.ds(i * Q_TILE, Q_TILE)
                scores = dot_t(q_ref[at, :], held[:, :HD])
                old = tops[at, :]
                top = jnp.maximum(old, jnp.max(scores, axis=1, keepdims=True))
                weights = jnp.exp2((scores - top[:, :1]) * SCALE)
                fade = jnp.exp2((old - top) * SCALE)
                tops[at, :] = top
                sums[at, :] = sums[at, :] * fade + jnp.sum(weights, axis=1, keepdims=True)
                accs[at, :] = accs[at, :] * fade + jnp.dot(
                    weights.astype(jnp.bfloat16), held[:, HD:], preferred_element_type=jnp.float32
                )

    out_ref[...] = (accs[...] / sums[...]).astype(jnp.bfloat16)


def attend_far(codes, queries, state, near, swapped, head):
    n = queries.shape[0]
    spec = pl.BlockSpec((n, HD), lambda i: (0, head))
    block = pl.BlockSpec((n, 2 * HD), lambda i: (0, 0))
    return pl.pallas_call(
        far_kernel,
        grid=(1,),
        in_specs=[pl.BlockSpec(memory_space=pltpu.SMEM)]
        + [spec] * 4
        + [block] * len(near)
        + [pl.BlockSpec(swapped.shape, lambda i: (0, 0, 0))],
        out_specs=pl.BlockSpec((n, HD), lambda i: (0, 0)),
        out_shape=jax.ShapeDtypeStruct((n, HD), jnp.bfloat16),
        scratch_shapes=[pltpu.VMEM((n, 2 * HD), jnp.bfloat16)]
        + [pltpu.VMEM((n, HD), jnp.float32)] * 3,
        compiler_params=pltpu.CompilerParams(vmem_limit_bytes=40 * 1024 * 1024),
        cost_estimate=pl.CostEstimate(
            flops=16 * n * n * HD, bytes_accessed=24 * n * HD, transcendentals=2 * n * n
        ),
        name="attend_far",
    )(codes, queries, *state, *near, swapped)


def project_kernel(n, *refs):
    out_ref = refs[-1]
    total = jnp.dot(refs[0][...], refs[n][...], preferred_element_type=jnp.float32)
    for i in range(1, n):
        total += jnp.dot(refs[i][...], refs[n + i][...], preferred_element_type=jnp.float32)
    out_ref[...] = total.astype(jnp.bfloat16)


def project(rows, weights):
    n = len(rows)
    n_rows, depth = rows[0].shape
    width = weights[0].shape[1]
    tile = width // 2
    return pl.pallas_call(
        lambda *refs: project_kernel(n, *refs),
        grid=(width // tile,),
        in_specs=[pl.BlockSpec((n_rows, depth), lambda i: (0, 0))] * n
        + [pl.BlockSpec((depth, tile), lambda i: (0, i))] * n,
        out_specs=pl.BlockSpec((n_rows, tile), lambda i: (0, i)),
        out_shape=jax.ShapeDtypeStruct((n_rows, width), jnp.bfloat16),
        compiler_params=pltpu.CompilerParams(vmem_limit_bytes=32 * 1024 * 1024),
        cost_estimate=pl.CostEstimate(
            flops=2 * n * n_rows * depth * width,
            bytes_accessed=2 * n * (n_rows * depth + depth * width) + 2 * n_rows * width,
            transcendentals=0,
        ),
        name="project",
    )(*rows, *weights)


def chip_perm(far):
    return [
        (z * CORES + c, (z + far) * CORES + c) for z in range(SIDE - far) for c in range(CORES)
    ]


def ring_x(array, far):
    perm = [(x * SIDE + y, (x + far) % SIDE * SIDE + y) for x in range(SIDE) for y in range(SIDE)]
    return lax.ppermute(array, "exp", perm)


def ring_y(array, far):
    perm = [(x * SIDE + y, x * SIDE + (y + far) % SIDE) for x in range(SIDE) for y in range(SIDE)]
    return lax.ppermute(array, "exp", perm)


def swap_cores(array):
    perm = [(i, i ^ 1) for i in range(SIDE * CORES)]
    return lax.ppermute(array, "seq", perm)


def attend(queries, keys, values, gates):
    me = lax.axis_index("seq")
    chip, core = me // CORES, me % CORES
    wanted = gates[me, 1:]
    codes = jnp.where(
        wanted == me, 0, jnp.where(wanted % CORES == core, chip - wanted // CORES, SIDE)
    ).astype(jnp.int32)
    partner_far = chip - gates[me ^ 1, 1:] // CORES
    state = attend_own(queries, keys, values)
    outs = []
    for head in range(queries.shape[1] // HD):
        cols = slice(head * HD, (head + 1) * HD)
        own = jnp.concatenate([keys[:, cols], values[:, cols]], axis=1)
        near = [lax.ppermute(own, "seq", chip_perm(far)) for far in range(1, SIDE)]
        asked = []
        for j in range(wanted.shape[0]):
            block = own
            for far in range(1, SIDE):
                block = jnp.where(partner_far[j] == far, near[far - 1], block)
            asked.append(block)
        swapped = swap_cores(jnp.stack(asked))
        outs.append(attend_far(codes, queries, state, near, swapped, head))
    return jnp.concatenate(outs, axis=1)


def projected(attn, o_proj, tok_moe):
    at = lax.axis_index("exp")
    x, y = at // SIDE, at % SIDE
    half = o_proj.shape[1] // 2
    width = attn.shape[1]
    grid = attn.reshape(SIDE, SIDE, tok_moe, width)
    out = []
    for ring, other, mine, theirs, cols, axis in (
        (ring_x, ring_y, x, y, slice(0, half), 0),
        (ring_y, ring_x, y, x, slice(half, None), 1),
    ):
        shard = o_proj[:, cols]
        weights = [shard] + [ring(shard, far) for far in range(1, SIDE)]
        rows = []
        for far in range(SIDE):
            piece = lax.dynamic_index_in_dim(grid, (mine + far) % SIDE, axis, keepdims=False)
            piece = piece.reshape(SIDE * tok_moe, width)
            rows.append(ring(piece, far) if far else piece)
        partial = project(rows, weights).reshape(SIDE, tok_moe, half)
        total = lax.dynamic_index_in_dim(partial, theirs, 0, keepdims=False).astype(jnp.float32)
        for far in range(1, SIDE):
            piece = lax.dynamic_index_in_dim(partial, (theirs + far) % SIDE, 0, keepdims=False)
            total = total + other(piece, far).astype(jnp.float32)
        out.append(total.astype(jnp.bfloat16))
    return jnp.concatenate(out, axis=1)


def expert_kernel(n_ff, rows_ref, gate_ref, up_ref, down_ref, out_ref, hidden_ref):
    step = pl.program_id(0)
    ff_tile = gate_ref.shape[2]

    @pl.when(step < n_ff)
    def _():
        rows = rows_ref[...]
        gate = jnp.dot(rows, gate_ref[0], preferred_element_type=jnp.float32)
        up = jnp.dot(rows, up_ref[0], preferred_element_type=jnp.float32)
        hidden = gate / (1.0 + jnp.exp(-gate)) * up
        cols = pl.ds(pl.multiple_of(step * ff_tile, ff_tile), ff_tile)
        hidden_ref[:, cols] = hidden.astype(jnp.bfloat16)

    @pl.when(step >= n_ff)
    def _():
        out_ref[...] = jnp.dot(
            hidden_ref[...], down_ref[0], preferred_element_type=jnp.float32
        ).astype(jnp.bfloat16)


def expert_rows(rows, w_gate, w_up, w_down):
    n_rows, width = rows.shape
    ff = w_gate.shape[2]
    ff_tile, out_tile = 256, 512
    n_ff, n_out = ff // ff_tile, width // out_tile

    def ff_at(i):
        return (0, 0, jnp.minimum(i, n_ff - 1))

    def out_at(i):
        return jnp.maximum(i - n_ff, 0)

    return pl.pallas_call(
        lambda *refs: expert_kernel(n_ff, *refs),
        grid=(n_ff + n_out,),
        in_specs=[
            pl.BlockSpec((n_rows, width), lambda i: (0, 0)),
            pl.BlockSpec((1, width, ff_tile), ff_at),
            pl.BlockSpec((1, width, ff_tile), ff_at),
            pl.BlockSpec((1, ff, out_tile), lambda i: (0, 0, out_at(i))),
        ],
        out_specs=pl.BlockSpec((n_rows, out_tile), lambda i: (0, out_at(i))),
        out_shape=jax.ShapeDtypeStruct((n_rows, width), jnp.bfloat16),
        scratch_shapes=[pltpu.VMEM((n_rows, ff), jnp.bfloat16)],
        compiler_params=pltpu.CompilerParams(vmem_limit_bytes=44 * 1024 * 1024),
        cost_estimate=pl.CostEstimate(
            flops=6 * n_rows * width * ff,
            bytes_accessed=2 * (2 * n_rows * width + 3 * width * ff),
            transcendentals=n_rows * ff,
        ),
        name="experts",
    )(rows, w_gate, w_up, w_down)


def slot_tables(routes, route_weights, n_experts, cap):
    n_tok = routes.shape[0]
    expert_ids = lax.broadcasted_iota(jnp.int32, (n_experts, n_tok), 0)
    hit = jnp.zeros((n_experts, n_tok), jnp.bool_)
    weight = jnp.zeros((n_experts, n_tok), jnp.float32)
    for k in range(routes.shape[1]):
        match = routes[:, k][None, :] == expert_ids
        hit = jnp.logical_or(hit, match)
        weight = weight + jnp.where(match, route_weights[:, k][None, :], 0.0)
    ahead = lax.broadcasted_iota(jnp.int32, (n_tok, n_tok), 0) < lax.broadcasted_iota(
        jnp.int32, (n_tok, n_tok), 1
    )
    rank = jnp.dot(
        hit.astype(jnp.bfloat16), ahead.astype(jnp.bfloat16), preferred_element_type=jnp.float32
    ).astype(jnp.int32)
    slot_ids = lax.broadcasted_iota(jnp.int32, (n_experts, cap, n_tok), 1)
    taken = jnp.logical_and(hit[:, None, :], rank[:, None, :] == slot_ids)
    place = taken.astype(jnp.bfloat16).reshape(n_experts * cap, n_tok)
    high = weight.astype(jnp.bfloat16)
    low = (weight - high.astype(jnp.float32)).astype(jnp.bfloat16)
    zero = jnp.zeros((), jnp.bfloat16)
    mix = jnp.concatenate(
        [jnp.where(taken, high[:, None, :], zero), jnp.where(taken, low[:, None, :], zero)], axis=2
    ).reshape(n_experts * cap, 2 * n_tok)
    return place, mix


def per_device(
    queries,
    keys,
    values,
    gates,
    o_proj,
    residual,
    norm_gain,
    routes,
    route_weights,
    w_gate,
    w_up,
    w_down,
):
    tok_moe = residual.shape[0]
    summed = projected(attend(queries, keys, values, gates), o_proj, tok_moe)
    residual_sum = residual.astype(jnp.float32) + summed.astype(jnp.float32)
    norm_scale = lax.rsqrt(jnp.mean(residual_sum * residual_sum, axis=-1, keepdims=True) + 1e-06)
    moe_in = (residual_sum * norm_scale * norm_gain).astype(jnp.bfloat16)
    width = moe_in.shape[1]
    n_experts = w_gate.shape[0] * lax.axis_size("seq") * lax.axis_size("exp")
    cap = 2 * tok_moe * ROUTE_K // n_experts
    place, mix = slot_tables(routes, route_weights, n_experts, cap)
    senders = jnp.dot(place, moe_in, preferred_element_type=jnp.float32).astype(jnp.bfloat16)
    received = lax.all_to_all(
        senders.reshape(n_experts, cap, width),
        ("seq", "exp"),
        split_axis=0,
        concat_axis=0,
        tiled=True,
    )
    produced = expert_rows(received.reshape(n_experts * cap, width), w_gate, w_up, w_down)
    returned = lax.all_to_all(
        produced.reshape(n_experts, cap, width),
        ("seq", "exp"),
        split_axis=0,
        concat_axis=0,
        tiled=True,
    )
    halves = lax.dot_general(
        mix,
        returned.reshape(n_experts * cap, width),
        (((0,), (0,)), ((), ())),
        preferred_element_type=jnp.float32,
    )
    moe_out = (halves[:tok_moe] + halves[tok_moe:]).astype(jnp.bfloat16)
    return (summed, moe_out)


def solution(mesh):
    in_specs = (
        P("seq", "exp"),
        P("seq", "exp"),
        P("seq", "exp"),
        P(),
        P("exp", None),
        P(("seq", "exp"), None),
        P(),
        P(("seq", "exp"), None),
        P(("seq", "exp"), None),
        P(("seq", "exp"), None, None),
        P(("seq", "exp"), None, None),
        P(("seq", "exp"), None, None),
    )
    out_specs = (P(("seq", "exp"), None), P(("seq", "exp"), None))
    return jax.shard_map(
        per_device, mesh=mesh, in_specs=in_specs, out_specs=out_specs, check_vma=False
    )
```

time: 491 us -> 389 us (0.79)
  waiting for transfers between devices: 239 us -> 142 us
  starting transfers between devices: 6.17 us -> 52.6 us
  matrix products: 32.2 us -> 10.4 us
  loops' own time: 19.5 us -> 0 us
  local copies, waits for them, and re-layouts: 37.8 us -> 21.4 us
  Pallas kernels: 36.5 us -> 48.7 us
  between operations: 14 us -> 5.06 us
  blocking collectives: 94.6 us -> 101 us
    reduce_scatter x1 -> x0, waiting for transfers between devices: 90.9 us -> none  [per_device(): lax.psum_scatter(jnp.dot(attn, o_proj, preferred_element_type=jnp.float32...]
    all_gather x2 -> x0, waiting for transfers between devices: 57.4 us -> none  [the longest x1 35.4 us: per_device(): key_piece = lax.all_gather(keys, 'seq', axis=0, tiled=True)]
    ppermute x0 -> x26, waiting for transfers between devices: none -> 52.4 us  [the longest x6 24.6 us: attend(): near = [lax.ppermute(own, 'seq', chip_perm(far)) for far in range(1, SIDE)]]
    ppermute x0 -> x26, starting transfers between devices: none -> 46.5 us  [the longest x6 18.6 us: attend(): near = [lax.ppermute(own, 'seq', chip_perm(far)) for far in range(1, SIDE)]]
    dot_general x5 -> x0, matrix products: 20.6 us -> none  [the longest x2 9.76 us: pair_partial(): jnp.einsum('hqk,khd->qhd', weights.astype(jnp.bfloat16), value_blk, prefe...]
    another operation x9 -> x0, loops' own time: 19.5 us -> none  [the longest x1 18.2 us: per_device(): lax.scan(visit, start_state, (key_blocks, value_blocks, jnp.arange(block_...]
    pallas_call x0 -> x5, Pallas kernels: none -> 18 us  [the longest x2 8.52 us: attend_far(): pl.pallas_call(far_kernel, grid=(1,), in_specs=[pl.BlockSpec(memory_space...]
    reshape x2 -> x0, local copies, waits for them, and re-layouts: 13.8 us -> none  [the longest x1 6.9 us: per_device(): key_blocks = key_piece.reshape(block_count, BLOCK, heads_here, HD)]
  transfers between devices with their start and end apart: 4 -> 27, of which waited for: 4 -> 14; matrix products, arithmetic and copies ran while one was open for 3% -> 3% of each run, Pallas kernels for 0% -> 5%
where the time goes in v2:
time: 389 us; the launch traced here: 388 us
  waiting for transfers between devices  142 us (37%)
  blocking collectives  101 us (26%)
  starting transfers between devices  52.6 us (14%)
  Pallas kernels  48.7 us (13%)
  local copies, waits for them, and re-layouts  21.4 us (6%)
  matrix products  10.4 us (3%)
  other arithmetic  7.68 us (2%)
  between operations  5.06 us (1%)
    all_to_all x1, blocking collectives, per_device(): lax.all_to_all(senders.reshape(n_experts, cap, width), ('seq', 'exp'), sp...  101 us
    all_to_all x1, waiting for transfers between devices, per_device(): lax.all_to_all(produced.reshape(n_experts, cap, width), ('seq', 'exp'), s...  89.2 us
    pallas_call x1, Pallas kernels, expert_rows(): pl.pallas_call(lambda *refs: expert_kernel(n_ff, *refs), grid=(n_ff + n_o...  30.6 us
    ppermute x6, waiting for transfers between devices, attend(): near = [lax.ppermute(own, 'seq', chip_perm(far)) for far in range(1, SIDE)]  24.6 us
    ppermute x6, starting transfers between devices, attend(): near = [lax.ppermute(own, 'seq', chip_perm(far)) for far in range(1, SIDE)]  18.6 us
    ppermute x9, waiting for transfers between devices, ring_x(): return lax.ppermute(array, 'exp', perm)  18.1 us
    unnamed x60, local copies, waits for them, and re-layouts  16.2 us
    ppermute x9, starting transfers between devices, ring_y(): return lax.ppermute(array, 'exp', perm)  15.6 us
  transfers between devices with their start and end apart: 27, of which 14 were waited for; matrix products, arithmetic and copies ran while one was open for 3% of the time, Pallas kernels for 5%

profile of v2, /device:TPU:5, one launch (start us, length us, event | category | flops | bytes accessed | tf_op | source)
XLA Modules:
  0.0 388.0 jit_solution(10892656788791550245)
XLA Ops:
  2.8 3.6 collective-permute-start
  6.4 5.2 %collective-permute-start.1 = (bf16[1024,256]{1,0:T(8,128)(2,1)}, bf16[1024,256]{1,0:T(8,128)(2,1)S(1)}, u32[]{:S(2)}, u32[]{:S(2)}) collective-permute-start(bf16[1024,256]{1,0:T(8,128)(2,1)} %pad_maximum_fusion.2), channel_id=1, source_target_pairs={{0,64},{16,80},{32,96},{48,112},{1,65},{17,81},{33,97},{49,113},{2... | collective-permute-start | bytes 1572872 | tf_op jit(solution)/shard_map/ppermute | solution.py:184
  13.8 1.4 collective-permute-start.4
  17.7 5.7 %collective-permute-start.6 = (bf16[1024,256]{1,0:T(8,128)(2,1)}, bf16[1024,256]{1,0:T(8,128)(2,1)S(1)}, u32[]{:S(2)}, u32[]{:S(2)}) collective-permute-start(bf16[1024,256]{1,0:T(8,128)(2,1)} %pad_maximum_fusion.3), channel_id=1, source_target_pairs={{0,96},{16,112},{1,97},{17,113},{2,98},{18,114},{3,99},{19,115},{4... | collective-permute-start | bytes 1572872 | tf_op jit(solution)/shard_map/ppermute | solution.py:184
  28.5 16.0 %collective-permute-done.2.refs_2_ = bf16[1024,256]{1,0:T(8,128)(2,1)S(1)} collective-permute-done((bf16[1024,256]{1,0:T(8,128)(2,1)}, bf16[1024,256]{1,0:T(8,128)(2,1)S(1)}, u32[]{:S(2)}, u32[]{:S(2)}) %collective-permute-start.2) | collective-permute-done | bytes 524320 | tf_op jit(solution)/shard_map/ppermute | solution.py:184
  44.5 1.5 select_bitcast_fusion.3
  47.7 3.4 collective-permute-done.5.refs_1_
  51.0 4.7 %collective-permute-done.6.refs_2_ = bf16[1024,256]{1,0:T(8,128)(2,1)S(1)} collective-permute-done((bf16[1024,256]{1,0:T(8,128)(2,1)}, bf16[1024,256]{1,0:T(8,128)(2,1)S(1)}, u32[]{:S(2)}, u32[]{:S(2)}) %collective-permute-start.6) | collective-permute-done | bytes 524320 | tf_op jit(solution)/shard_map/ppermute | solution.py:184
  63.5 3.8 attend_own.1
  78.4 4.2 %attend_far.2 = bf16[1024,128]{1,0:T(8,128)(2,1)S(1)} custom-call(s32[2]{0:T(128)S(1)} %compare_select_fusion.1.code_ref, bf16[1024,256]{1,0:T(8,128)(2,1)S(1)} %copy-done.14, f32[1024,256]{1,0:T(8,128)S(1)} %copy-done.16, f32[1024,256]{1,0:T(8,128)S(1)} %copy-done.18, f32[1024,256]{1,0:T(8,128)S(1)} %copy-done.20, ...), custom_call_target="tpu_custom_call" | custom-call | flops 2147483648 | bytes 3145728 | tf_op jit(solution)/shard_map/attend_far/pallas_call | solution.py:101
  82.6 2.7 collective-permute-start.21
  85.3 4.3 %attend_far.3 = bf16[1024,128]{1,0:T(8,128)(2,1)S(1)} custom-call(s32[2]{0:T(128)S(1)} %compare_select_fusion.1.code_ref, bf16[1024,256]{1,0:T(8,128)(2,1)S(1)} %copy-done.14, f32[1024,256]{1,0:T(8,128)S(1)} %copy-done.16, f32[1024,256]{1,0:T(8,128)S(1)} %copy-done.18, f32[1024,256]{1,0:T(8,128)S(1)} %copy-done.20, bf16[1024,256]{1,0:T(8,128)(2,1)S(1)} %copy-done.2, ...), custom_call_target="tpu_custom_call" | custom-call | flops 2147483648 | bytes 3145728 | tf_op jit(solution)/shard_map/attend_far/pallas_call | solution.py:101
  91.6 8.1 %collective-permute-done.12.refs_6_ = bf16[256,1792]{1,0:T(8,128)(2,1)} collective-permute-done((bf16[256,1792]{1,0:T(8,128)(2,1)S(1)}, bf16[256,1792]{1,0:T(8,128)(2,1)}, u32[]{:S(2)}, u32[]{:S(2)}) %collective-permute-start.12) | collective-permute-done | bytes 917536 | tf_op jit(solution)/shard_map/ppermute | solution.py:158
  101.2 1.4 collective-permute-start.8
  104.0 2.5 collective-permute-start.9
  109.9 2.9 collective-permute-start.18
  112.8 2.8 project.2
  117.3 8.1 %collective-permute-done.22.refs_7_ = bf16[256,1792]{1,0:T(8,128)(2,1)} collective-permute-done((bf16[256,1792]{1,0:T(8,128)(2,1)S(1)}, bf16[256,1792]{1,0:T(8,128)(2,1)}, u32[]{:S(2)}, u32[]{:S(2)}) %collective-permute-start.22) | collective-permute-done | bytes 917536 | tf_op jit(solution)/shard_map/ppermute | solution.py:163
  125.4 2.6 collective-permute-start.15
  128.0 2.0 collective-permute-start.16
  130.0 2.9 project.3
  134.0 2.0 collective-permute-start.24
  136.1 1.8 collective-permute-start.25
  137.9 1.6 collective-permute-done.16
  140.2 5.8 %collective-permute-done.24 = bf16[64,1792]{1,0:T(8,128)(2,1)S(1)} collective-permute-done((bf16[64,1792]{1,0:T(8,128)(2,1)S(1)}, bf16[64,1792]{1,0:T(8,128)(2,1)S(1)}, u32[]{:S(2)}, u32[]{:S(2)}) %collective-permute-start.24) | collective-permute-done | bytes 229408 | tf_op jit(solution)/shard_map/ppermute | solution.py:158
  147.2 2.5 fusion.2
  149.7 100.6 %all_to_all.10 = bf16[128,8,3584]{2,1,0:T(8,128)(2,1)} all-to-all(bf16[128,8,3584]{2,1,0:T(8,128)(2,1)S(1)} %fusion.2), channel_id=1, replica_groups=mesh['seq'=8,'exp'=16] {'seq','exp'}, dimensions={0} | all-to-all | bytes 14680064 | tf_op jit(solution)/shard_map/all_to_all | solution.py:328
  250.3 30.6 %experts.1 = bf16[1024,3584]{1,0:T(8,128)(2,1)S(1)} custom-call(bf16[1024,3584]{1,0:T(8,128)(2,1)} %bitcast.106, bf16[1,3584,1024]{2,1,0:T(8,128)(2,1)} %refs_1_.1, bf16[1,3584,1024]{2,1,0:T(8,128)(2,1)} %refs_2_.1, bf16[1,1024,3584]{2,1,0:T(8,128)(2,1)} %refs_3_.1), custom_call_target="tpu_custom_call" | custom-call | flops 22548578304 | bytes 36700160 | tf_op jit(solution)/shard_map/experts/pallas_call | solution.py:255
  281.0 3.0 copy-done
  284.0 6.1 %all-to-all-start.1 = ((bf16[128,8,3584]{2,1,0:T(8,128)(2,1)}), bf16[128,8,3584]{2,1,0:T(8,128)(2,1)}, u32[]{:S(2)}, u32[]{:S(2)}) async-start(bf16[128,8,3584]{2,1,0:T(8,128)(2,1)} %bitcast.99), calls=%async_computation.1 | async-start | bytes 14680064 | tf_op jit(solution)/shard_map/all_to_all | solution.py:336
  290.4 89.2 %all-to-all-done.1 = bf16[128,8,3584]{2,1,0:T(8,128)(2,1)} async-done(((bf16[128,8,3584]{2,1,0:T(8,128)(2,1)}), bf16[128,8,3584]{2,1,0:T(8,128)(2,1)}, u32[]{:S(2)}, u32[]{:S(2)}) %all-to-all-start.1) | async-done | bytes 7340064 | tf_op jit(solution)/shard_map/all_to_all | solution.py:336
  379.6 7.6 %fusion.3 = f32[128,3584]{1,0:T(8,128)S(1)} fusion(bf16[128,8,3584]{2,1,0:T(8,128)(2,1)} %all-to-all-done.1, bf16[128,8,64]{0,2,1:T(8,128)(2,1)S(1)} %get-tuple-element.39, bf16[128,8,64]{0,2,1:T(8,128)(2,1)S(1)} %get-tuple-element.38), kind=kOutput, calls=%fused_computation.4 | convolution fusion | flops 940048384 | bytes 9437184 | tf_op jit(solution)/shard_map/dot_general | solution.py:343
  (121 shorter events, 42.4 us)
Async XLA Ops:
  2.8 14.8 %collective-permute-start = (bf16[1024,256]{1,0:T(8,128)(2,1)}, bf16[1024,256]{1,0:T(8,128)(2,1)S(1)}, u32[]{:S(2)}, u32[]{:S(2)}) collective-permute-start(bf16[1024,256]{1,0:T(8,128)(2,1)} %pad_maximum_fusion.2), channel_id=1, source_target_pairs={{0,32},{16,48},{32,64},{48,80},{64,96},{80,112},{1,33},{17,49},{33... | collective-permute-start | bytes 1572872 | tf_op jit(solution)/shard_map/ppermute | solution.py:184
  6.4 22.1 %collective-permute-start.1 = (bf16[1024,256]{1,0:T(8,128)(2,1)}, bf16[1024,256]{1,0:T(8,128)(2,1)S(1)}, u32[]{:S(2)}, u32[]{:S(2)}) collective-permute-start(bf16[1024,256]{1,0:T(8,128)(2,1)} %pad_maximum_fusion.2), channel_id=1, source_target_pairs={{0,64},{16,80},{32,96},{48,112},{1,65},{17,81},{33,97},{49,113},{2... | collective-permute-start | bytes 1572872 | tf_op jit(solution)/shard_map/ppermute | solution.py:184
  11.6 32.9 %collective-permute-start.2 = (bf16[1024,256]{1,0:T(8,128)(2,1)}, bf16[1024,256]{1,0:T(8,128)(2,1)S(1)}, u32[]{:S(2)}, u32[]{:S(2)}) collective-permute-start(bf16[1024,256]{1,0:T(8,128)(2,1)} %pad_maximum_fusion.2), channel_id=1, source_target_pairs={{0,96},{16,112},{1,97},{17,113},{2,98},{18,114},{3,99},{19,115},{4... | collective-permute-start | bytes 1572872 | tf_op jit(solution)/shard_map/ppermute | solution.py:184
  13.8 46.5 %copy-start.27 = (s32[64,8]{0,1:T(8,128)S(1)}, s32[64,8]{0,1:T(8,128)}, u32[]{:S(2)}) copy-start(s32[64,8]{0,1:T(8,128)} %param.19) | copy-start | bytes 6148
  13.8 33.9 %collective-permute-start.4 = (bf16[1024,256]{1,0:T(8,128)(2,1)}, bf16[1024,256]{1,0:T(8,128)(2,1)S(1)}, u32[]{:S(2)}, u32[]{:S(2)}) collective-permute-start(bf16[1024,256]{1,0:T(8,128)(2,1)} %pad_maximum_fusion.3), channel_id=1, source_target_pairs={{0,32},{16,48},{32,64},{48,80},{64,96},{80,112},{1,33},{17,49},{33... | collective-permute-start | bytes 1572872 | tf_op jit(solution)/shard_map/ppermute | solution.py:184
  15.2 35.8 %collective-permute-start.5 = (bf16[1024,256]{1,0:T(8,128)(2,1)}, bf16[1024,256]{1,0:T(8,128)(2,1)S(1)}, u32[]{:S(2)}, u32[]{:S(2)}) collective-permute-start(bf16[1024,256]{1,0:T(8,128)(2,1)} %pad_maximum_fusion.3), channel_id=1, source_target_pairs={{0,64},{16,80},{32,96},{48,112},{1,65},{17,81},{33,97},{49,113},{2... | collective-permute-start | bytes 1572872 | tf_op jit(solution)/shard_map/ppermute | solution.py:184
  16.6 41.2 %copy-start.23 = (bf16[256,3584]{1,0:T(8,128)(2,1)S(1)}, bf16[256,3584]{1,0:T(8,128)(2,1)}, u32[]{:S(2)}) copy-start(bf16[256,3584]{1,0:T(8,128)(2,1)} %param.16) | copy-start | bytes 5505028
  17.7 38.0 %collective-permute-start.6 = (bf16[1024,256]{1,0:T(8,128)(2,1)}, bf16[1024,256]{1,0:T(8,128)(2,1)S(1)}, u32[]{:S(2)}, u32[]{:S(2)}) collective-permute-start(bf16[1024,256]{1,0:T(8,128)(2,1)} %pad_maximum_fusion.3), channel_id=1, source_target_pairs={{0,96},{16,112},{1,97},{17,113},{2,98},{18,114},{3,99},{19,115},{4... | collective-permute-start | bytes 1572872 | tf_op jit(solution)/shard_map/ppermute | solution.py:184
  47.1 23.2 %collective-permute-start.3 = (bf16[2,1024,256]{2,1,0:T(8,128)(2,1)}, bf16[2,1024,256]{2,1,0:T(8,128)(2,1)}, u32[]{:S(2)}, u32[]{:S(2)}) collective-permute-start(bf16[2,1024,256]{2,1,0:T(8,128)(2,1)} %pad_maximum_fusion), channel_id=1, source_target_pairs={{0,16},{16,0},{32,48},{48,32},{64,80},{80,64},{96,112},{112,96},{1... | collective-permute-start | bytes 3145736 | tf_op jit(solution)/shard_map/ppermute | solution.py:168
  57.2 25.4 %collective-permute-start.7 = (bf16[2,1024,256]{2,1,0:T(8,128)(2,1)}, bf16[2,1024,256]{2,1,0:T(8,128)(2,1)}, u32[]{:S(2)}, u32[]{:S(2)}) collective-permute-start(bf16[2,1024,256]{2,1,0:T(8,128)(2,1)} %pad_maximum_fusion.1), channel_id=1, source_target_pairs={{0,16},{16,0},{32,48},{48,32},{64,80},{80,64},{96,112},{112,96},{1... | collective-permute-start | bytes 3145736 | tf_op jit(solution)/shard_map/ppermute | solution.py:168
  57.9 31.8 %collective-permute-start.11 = (bf16[256,1792]{1,0:T(8,128)(2,1)S(1)}, bf16[256,1792]{1,0:T(8,128)(2,1)S(1)}, u32[]{:S(2)}, u32[]{:S(2)}) collective-permute-start(bf16[256,1792]{1,0:T(8,128)(2,1)S(1)} %get-tuple-element.18.refs_4_), channel_id=1, source_target_pairs={{0,4},{1,5},{2,6},{3,7},{4,8},{5,9},{6,10},{7,11},{8,12},{9,13},{1... | collective-permute-start | bytes 2752520 | tf_op jit(solution)/shard_map/ppermute | solution.py:158
  58.9 40.8 %collective-permute-start.12 = (bf16[256,1792]{1,0:T(8,128)(2,1)S(1)}, bf16[256,1792]{1,0:T(8,128)(2,1)}, u32[]{:S(2)}, u32[]{:S(2)}) collective-permute-start(bf16[256,1792]{1,0:T(8,128)(2,1)S(1)} %get-tuple-element.18.refs_4_), channel_id=1, source_target_pairs={{0,8},{1,9},{2,10},{3,11},{4,12},{5,13},{6,14},{7,15},{8,0},{9,1},... | collective-permute-start | bytes 2752520 | tf_op jit(solution)/shard_map/ppermute | solution.py:158
  59.4 41.8 %collective-permute-start.13 = (bf16[256,1792]{1,0:T(8,128)(2,1)S(1)}, bf16[256,1792]{1,0:T(8,128)(2,1)}, u32[]{:S(2)}, u32[]{:S(2)}) collective-permute-start(bf16[256,1792]{1,0:T(8,128)(2,1)S(1)} %get-tuple-element.18.refs_4_), channel_id=1, source_target_pairs={{0,12},{1,13},{2,14},{3,15},{4,0},{5,1},{6,2},{7,3},{8,4},{9,5},{1... | collective-permute-start | bytes 2752520 | tf_op jit(solution)/shard_map/ppermute | solution.py:158
  70.3 45.3 %collective-permute-start.20 = (bf16[256,1792]{1,0:T(8,128)(2,1)S(1)}, bf16[256,1792]{1,0:T(8,128)(2,1)}, u32[]{:S(2)}, u32[]{:S(2)}) collective-permute-start(bf16[256,1792]{1,0:T(8,128)(2,1)S(1)} %get-tuple-element.19.refs_4_), channel_id=1, source_target_pairs={{0,1},{1,2},{2,3},{3,0},{4,5},{5,6},{6,7},{7,4},{8,9},{9,10},{10,1... | collective-permute-start | bytes 2752520 | tf_op jit(solution)/shard_map/ppermute | solution.py:163
  82.6 33.6 %collective-permute-start.21 = (bf16[256,1792]{1,0:T(8,128)(2,1)S(1)}, bf16[256,1792]{1,0:T(8,128)(2,1)}, u32[]{:S(2)}, u32[]{:S(2)}) collective-permute-start(bf16[256,1792]{1,0:T(8,128)(2,1)S(1)} %get-tuple-element.19.refs_4_), channel_id=1, source_target_pairs={{0,2},{1,3},{2,0},{3,1},{4,6},{5,7},{6,4},{7,5},{8,10},{9,11},{10,... | collective-permute-start | bytes 2752520 | tf_op jit(solution)/shard_map/ppermute | solution.py:163
  89.8 35.6 %collective-permute-start.22 = (bf16[256,1792]{1,0:T(8,128)(2,1)S(1)}, bf16[256,1792]{1,0:T(8,128)(2,1)}, u32[]{:S(2)}, u32[]{:S(2)}) collective-permute-start(bf16[256,1792]{1,0:T(8,128)(2,1)S(1)} %get-tuple-element.19.refs_4_), channel_id=1, source_target_pairs={{0,3},{1,0},{2,1},{3,2},{4,7},{5,4},{6,5},{7,6},{8,11},{9,8},{10,9... | collective-permute-start | bytes 2752520 | tf_op jit(solution)/shard_map/ppermute | solution.py:163
  99.7 4.3 %collective-permute-start.10 = (bf16[256,256]{1,0:T(8,128)(2,1)S(1)}, bf16[256,256]{1,0:T(8,128)(2,1)S(1)}, u32[]{:S(2)}, u32[]{:S(2)}) collective-permute-start(bf16[256,256]{1,0:T(8,128)(2,1)S(1)} %bitcast.112), channel_id=1, source_target_pairs={{0,12},{1,13},{2,14},{3,15},{4,0},{5,1},{6,2},{7,3},{8,4},{9,5},{1... | collective-permute-start | bytes 393224 | tf_op jit(solution)/shard_map/ppermute | solution.py:158
  101.2 7.0 %collective-permute-start.8 = (bf16[256,256]{1,0:T(8,128)(2,1)}, bf16[256,256]{1,0:T(8,128)(2,1)S(1)}, u32[]{:S(2)}, u32[]{:S(2)}) collective-permute-start(bf16[256,256]{1,0:T(8,128)(2,1)} %bitcast.12), channel_id=1, source_target_pairs={{0,4},{1,5},{2,6},{3,7},{4,8},{5,9},{6,10},{7,11},{8,12},{9,13},{1... | collective-permute-start | bytes 393224 | tf_op jit(solution)/shard_map/ppermute | solution.py:158
  104.0 5.9 %collective-permute-start.9 = (bf16[256,256]{1,0:T(8,128)(2,1)}, bf16[256,256]{1,0:T(8,128)(2,1)S(1)}, u32[]{:S(2)}, u32[]{:S(2)}) collective-permute-start(bf16[256,256]{1,0:T(8,128)(2,1)} %bitcast.13), channel_id=1, source_target_pairs={{0,8},{1,9},{2,10},{3,11},{4,12},{5,13},{6,14},{7,15},{8,0},{9,1},... | collective-permute-start | bytes 393224 | tf_op jit(solution)/shard_map/ppermute | solution.py:158
  108.2 19.8 %collective-permute-start.17 = (bf16[256,256]{1,0:T(8,128)(2,1)S(1)}, bf16[256,256]{1,0:T(8,128)(2,1)S(1)}, u32[]{:S(2)}, u32[]{:S(2)}) collective-permute-start(bf16[256,256]{1,0:T(8,128)(2,1)S(1)} %bitcast.111), channel_id=1, source_target_pairs={{0,1},{1,2},{2,3},{3,0},{4,5},{5,6},{6,7},{7,4},{8,9},{9,10},{10,1... | collective-permute-start | bytes 393224 | tf_op jit(solution)/shard_map/ppermute | solution.py:163
  109.9 20.1 %collective-permute-start.18 = (bf16[256,256]{1,0:T(8,128)(2,1)S(1)}, bf16[256,256]{1,0:T(8,128)(2,1)S(1)}, u32[]{:S(2)}, u32[]{:S(2)}) collective-permute-start(bf16[256,256]{1,0:T(8,128)(2,1)S(1)} %bitcast.110), channel_id=1, source_target_pairs={{0,2},{1,3},{2,0},{3,1},{4,6},{5,7},{6,4},{7,5},{8,10},{9,11},{10,... | collective-permute-start | bytes 393224 | tf_op jit(solution)/shard_map/ppermute | solution.py:163
  112.8 34.0 %copy-start.24 = (bf16[64,3584]{1,0:T(8,128)(2,1)S(1)}, bf16[64,3584]{1,0:T(8,128)(2,1)}, u32[]{:S(2)}) copy-start(bf16[64,3584]{1,0:T(8,128)(2,1)} %param.17) | copy-start | bytes 1376260
  112.8 34.3 %copy-start.26 = (f32[3584]{0:T(1024)S(1)}, f32[3584]{0:T(1024)}, u32[]{:S(2)}) copy-start(f32[3584]{0:T(1024)} %param.18) | copy-start | bytes 43012
  115.6 14.4 %collective-permute-start.19 = (bf16[256,256]{1,0:T(8,128)(2,1)S(1)}, bf16[256,256]{1,0:T(8,128)(2,1)S(1)}, u32[]{:S(2)}, u32[]{:S(2)}) collective-permute-start(bf16[256,256]{1,0:T(8,128)(2,1)S(1)} %bitcast.109), channel_id=1, source_target_pairs={{0,3},{1,0},{2,1},{3,2},{4,7},{5,4},{6,5},{7,6},{8,11},{9,8},{10,9... | collective-permute-start | bytes 393224 | tf_op jit(solution)/shard_map/ppermute | solution.py:163
  116.2 19.9 %collective-permute-start.14 = (bf16[64,1792]{1,0:T(8,128)(2,1)S(1)}, bf16[64,1792]{1,0:T(8,128)(2,1)S(1)}, u32[]{:S(2)}, u32[]{:S(2)}) collective-permute-start(bf16[64,1792]{1,0:T(8,128)(2,1)S(1)} %get-tuple-element.20), channel_id=1, source_target_pairs={{0,1},{1,2},{2,3},{3,0},{4,5},{5,6},{6,7},{7,4},{8,9},{9,10},{10,1... | collective-permute-start | bytes 688136 | tf_op jit(solution)/shard_map/ppermute | solution.py:163
  125.4 12.5 %collective-permute-start.15 = (bf16[64,1792]{1,0:T(8,128)(2,1)S(1)}, bf16[64,1792]{1,0:T(8,128)(2,1)S(1)}, u32[]{:S(2)}, u32[]{:S(2)}) collective-permute-start(bf16[64,1792]{1,0:T(8,128)(2,1)S(1)} %get-tuple-element.22), channel_id=1, source_target_pairs={{0,2},{1,3},{2,0},{3,1},{4,6},{5,7},{6,4},{7,5},{8,10},{9,11},{10,... | collective-permute-start | bytes 688136 | tf_op jit(solution)/shard_map/ppermute | solution.py:163
  128.0 11.5 %collective-permute-start.16 = (bf16[64,1792]{1,0:T(8,128)(2,1)S(1)}, bf16[64,1792]{1,0:T(8,128)(2,1)S(1)}, u32[]{:S(2)}, u32[]{:S(2)}) collective-permute-start(bf16[64,1792]{1,0:T(8,128)(2,1)S(1)} %get-tuple-element.21), channel_id=1, source_target_pairs={{0,3},{1,0},{2,1},{3,2},{4,7},{5,4},{6,5},{7,6},{8,11},{9,8},{10,9... | collective-permute-start | bytes 688136 | tf_op jit(solution)/shard_map/ppermute | solution.py:163
  133.0 7.2 %collective-permute-start.23 = (bf16[64,1792]{1,0:T(8,128)(2,1)S(1)}, bf16[64,1792]{1,0:T(8,128)(2,1)S(1)}, u32[]{:S(2)}, u32[]{:S(2)}) collective-permute-start(bf16[64,1792]{1,0:T(8,128)(2,1)S(1)} %get-tuple-element.23), channel_id=1, source_target_pairs={{0,4},{1,5},{2,6},{3,7},{4,8},{5,9},{6,10},{7,11},{8,12},{9,13},{1... | collective-permute-start | bytes 688136 | tf_op jit(solution)/shard_map/ppermute | solution.py:158
  134.0 11.9 %collective-permute-start.24 = (bf16[64,1792]{1,0:T(8,128)(2,1)S(1)}, bf16[64,1792]{1,0:T(8,128)(2,1)S(1)}, u32[]{:S(2)}, u32[]{:S(2)}) collective-permute-start(bf16[64,1792]{1,0:T(8,128)(2,1)S(1)} %get-tuple-element.25), channel_id=1, source_target_pairs={{0,8},{1,9},{2,10},{3,11},{4,12},{5,13},{6,14},{7,15},{8,0},{9,1},... | collective-permute-start | bytes 688136 | tf_op jit(solution)/shard_map/ppermute | solution.py:158
  136.1 10.7 %collective-permute-start.25 = (bf16[64,1792]{1,0:T(8,128)(2,1)S(1)}, bf16[64,1792]{1,0:T(8,128)(2,1)S(1)}, u32[]{:S(2)}, u32[]{:S(2)}) collective-permute-start(bf16[64,1792]{1,0:T(8,128)(2,1)S(1)} %get-tuple-element.24), channel_id=1, source_target_pairs={{0,12},{1,13},{2,14},{3,15},{4,0},{5,1},{6,2},{7,3},{8,4},{9,5},{1... | collective-permute-start | bytes 688136 | tf_op jit(solution)/shard_map/ppermute | solution.py:158
  147.1 103.2 %copy-start.25 = (bf16[64,3584]{1,0:T(8,128)(2,1)}, bf16[64,3584]{1,0:T(8,128)(2,1)S(1)}, u32[]{:S(2)}) copy-start(bf16[64,3584]{1,0:T(8,128)(2,1)S(1)} %get-tuple-element.13) | copy-start | bytes 1376260
  284.0 95.6 %all-to-all-start.1 = ((bf16[128,8,3584]{2,1,0:T(8,128)(2,1)}), bf16[128,8,3584]{2,1,0:T(8,128)(2,1)}, u32[]{:S(2)}, u32[]{:S(2)}) async-start(bf16[128,8,3584]{2,1,0:T(8,128)(2,1)} %bitcast.99), calls=%async_computation.1 | async-start | bytes 14680064 | tf_op jit(solution)/shard_map/all_to_all | solution.py:336
  (24 other events, 125.4 us)

commit v3 on v2

v3 whole, which is shorter than its diff:
```python
import math

import jax
import jax.numpy as jnp
from jax import lax
from jax.experimental import pallas as pl
from jax.experimental.pallas import tpu as pltpu
from jax.sharding import PartitionSpec as P

HD = 128
BLOCK = 1024
ROUTE_K = 8


NEG_FILL = -1e30
SCALE = math.log2(math.e) / math.sqrt(HD)
Q_TILE = 128
CORES = 2
SIDE = 4


def dot_t(a, b):
    return lax.dot_general(a, b, (((1,), (1,)), ((), ())), preferred_element_type=jnp.float32)


def mix_values(weights, values):
    wide = jnp.concatenate([values, jnp.ones_like(values)], axis=1)
    both = jnp.dot(weights.astype(jnp.bfloat16), wide, preferred_element_type=jnp.float32)
    return both[:, :HD], both[:, HD:]


def attend_kernel(code_ref, q_ref, own_ref, *refs):
    near, swapped, out_ref = refs[:-6], refs[-6], refs[-5]
    held, tops, sums, accs = refs[-4:]
    n_tiles = q_ref.shape[0] // Q_TILE
    for i in range(n_tiles):
        at = pl.ds(i * Q_TILE, Q_TILE)
        seen = pl.ds(0, (i + 1) * Q_TILE)
        scores = dot_t(q_ref[at, :], own_ref[seen, :HD])
        query_pos = lax.broadcasted_iota(jnp.int32, scores.shape, 0) + i * Q_TILE
        key_pos = lax.broadcasted_iota(jnp.int32, scores.shape, 1)
        scores = jnp.where(key_pos <= query_pos, scores, NEG_FILL)
        top = jnp.max(scores, axis=1, keepdims=True)
        weights = jnp.exp2((scores - top) * SCALE)
        acc, amount = mix_values(weights, own_ref[seen, HD:])
        tops[at, :] = jnp.broadcast_to(top, (Q_TILE, HD))
        sums[at, :] = amount
        accs[at, :] = acc
    for j in range(swapped.shape[0]):
        code = code_ref[j]
        for s in range(len(near)):

            @pl.when(code == s + 1)
            def _(s=s):
                held[...] = near[s][...]

        @pl.when(code == len(near) + 1)
        def _(j=j):
            held[...] = swapped[j]

        @pl.when(code > 0)
        def _():
            for i in range(n_tiles):
                at = pl.ds(i * Q_TILE, Q_TILE)
                scores = dot_t(q_ref[at, :], held[:, :HD])
                old = tops[at, :]
                top = jnp.maximum(old, jnp.max(scores, axis=1, keepdims=True))
                weights = jnp.exp2((scores - top[:, :1]) * SCALE)
                fade = jnp.exp2((old - top) * SCALE)
                acc, amount = mix_values(weights, held[:, HD:])
                tops[at, :] = top
                sums[at, :] = sums[at, :] * fade + amount
                accs[at, :] = accs[at, :] * fade + acc

    out_ref[...] = (accs[...] / sums[...]).astype(jnp.bfloat16)


def attend_head(codes, queries, own, near, swapped, head, before):
    n = queries.shape[0]
    block = pl.BlockSpec((n, 2 * HD), lambda i: (0, 0))
    extra = [] if before is None else [before]
    return pl.pallas_call(
        lambda *refs: attend_kernel(*refs[len(extra) :]),
        grid=(1,),
        in_specs=[pl.BlockSpec(memory_space=pl.ANY)] * len(extra)
        + [
            pl.BlockSpec(memory_space=pltpu.SMEM),
            pl.BlockSpec((n, HD), lambda i: (0, head)),
        ]
        + [block] * (1 + len(near))
        + [pl.BlockSpec(swapped.shape, lambda i: (0, 0, 0))],
        out_specs=pl.BlockSpec((n, HD), lambda i: (0, head)),
        out_shape=jax.ShapeDtypeStruct(queries.shape, jnp.bfloat16),
        input_output_aliases={0: 0} if extra else {},
        scratch_shapes=[pltpu.VMEM((n, 2 * HD), jnp.bfloat16)]
        + [pltpu.VMEM((n, HD), jnp.float32)] * 3,
        compiler_params=pltpu.CompilerParams(vmem_limit_bytes=60 * 1024 * 1024),
        cost_estimate=pl.CostEstimate(
            flops=64 * n * n * HD, bytes_accessed=14 * n * HD, transcendentals=2 * n * n
        ),
        name="attend",
    )(*extra, codes, queries, own, *near, swapped)


def project_kernel(core_ref, *refs):
    rows, own, mine, theirs, out_ref = refs[:4], refs[4], refs[5:8], refs[8:11], refs[11]
    core = core_ref[0]
    first = pl.ds(pl.multiple_of(core * HD, HD), HD)
    second = pl.ds(pl.multiple_of((1 - core) * HD, HD), HD)
    total = jnp.dot(rows[0][...], own[...], preferred_element_type=jnp.float32)
    for row, left, right in zip(rows[1:], mine, theirs):
        total += jnp.dot(
            jnp.concatenate([row[:, first], row[:, second]], axis=1),
            jnp.concatenate([left[...], right[...]], axis=0),
            preferred_element_type=jnp.float32,
        )
    out_ref[...] = total.astype(jnp.bfloat16)


def project(core, rows, own, mine, theirs):
    n = len(mine)
    n_rows, depth = rows[0].shape
    width, tile = own.shape[1], 896
    return pl.pallas_call(
        project_kernel,
        grid=(width // tile,),
        in_specs=[pl.BlockSpec(memory_space=pltpu.SMEM)]
        + [pl.BlockSpec((n_rows, depth), lambda i: (0, 0))] * (1 + n)
        + [pl.BlockSpec((depth, tile), lambda i: (0, i))]
        + [pl.BlockSpec((HD, tile), lambda i: (0, i))] * n
        + [pl.BlockSpec((HD, tile), lambda i, k=k: (k, i)) for k in range(n)],
        out_specs=pl.BlockSpec((n_rows, tile), lambda i: (0, i)),
        out_shape=jax.ShapeDtypeStruct((n_rows, width), jnp.bfloat16),
        compiler_params=pltpu.CompilerParams(vmem_limit_bytes=32 * 1024 * 1024),
        cost_estimate=pl.CostEstimate(
            flops=6 * n * n_rows * depth * width,
            bytes_accessed=2 * n * (n_rows * depth + depth * width) + 2 * n_rows * width,
            transcendentals=0,
        ),
        name="project",
    )(core, *rows, own, *mine, *([theirs] * n))


def chip_perm(far):
    return [
        (z * CORES + c, (z + far) * CORES + c) for z in range(SIDE - far) for c in range(CORES)
    ]


def ring_x(array, far):
    perm = [(x * SIDE + y, (x + far) % SIDE * SIDE + y) for x in range(SIDE) for y in range(SIDE)]
    return lax.ppermute(array, "exp", perm)


def ring_y(array, far):
    perm = [(x * SIDE + y, x * SIDE + (y + far) % SIDE) for x in range(SIDE) for y in range(SIDE)]
    return lax.ppermute(array, "exp", perm)


def swap_cores(array):
    perm = [(i, i ^ 1) for i in range(SIDE * CORES)]
    return lax.ppermute(array, "seq", perm)


def after(array, *earlier):
    return lax.optimization_barrier((array, *earlier))[0]


def attend(queries, keys, values, gates, first_shards, last_shard):
    me = lax.axis_index("seq")
    chip, core = me // CORES, me % CORES
    wanted = gates[me, 1:]
    codes = jnp.where(
        wanted == me, 0, jnp.where(wanted % CORES == core, chip - wanted // CORES, SIDE)
    ).astype(jnp.int32)
    partner_far = (chip - gates[me ^ 1, 1:] // CORES)[:, None, None]
    owns = []
    for head in range(queries.shape[1] // HD):
        cols = slice(head * HD, (head + 1) * HD)
        owns.append(jnp.concatenate([keys[:, cols], values[:, cols]], axis=1))
    attn, near = None, None
    for head, own in enumerate(owns):
        if head == 0:
            near = [lax.ppermute(own, "seq", chip_perm(far)) for far in range(1, SIDE)]
            shards = first_shards(own)
            later = [after(own, shards[0]) for own in owns[1:]]
            near, shards, later = lax.optimization_barrier((near, shards, later))
        else:
            sent = later[head - 1]
            near = [
                lax.ppermute(after(sent, seen), "seq", chip_perm(far))
                for far, seen in enumerate(near, 1)
            ]
            if head == 1:
                shards = shards + [last_shard(shards[0])]
            near, attn, shards = lax.optimization_barrier((near, attn, shards))
        asked = own[None]
        for far in range(1, SIDE):
            asked = jnp.where(partner_far == far, near[far - 1][None], asked)
        swapped = swap_cores(asked)
        attn = attend_head(codes, queries, own, near, swapped, head, attn)
    return attn, [after(shard, swapped) for shard in shards]


def projected(queries, keys, values, gates, o_proj, tok_moe):
    at = lax.axis_index("exp")
    x, y = at // SIDE, at % SIDE
    order = (1, 3, 2)

    core = lax.axis_index("seq") % CORES
    share = (core * HD, 0), (HD, o_proj.shape[1])

    def first_shards(seen):
        part = lax.dynamic_slice(after(o_proj, seen), *share)
        return [ring_x(part, far) for far in order[:2]]

    def last_shard(seen):
        return ring_x(lax.dynamic_slice(after(o_proj, seen), *share), order[2])

    attn, mine = attend(queries, keys, values, gates, first_shards, last_shard)
    theirs = swap_cores(jnp.concatenate(mine, axis=0))
    n_rows, width = attn.shape[0] // SIDE, attn.shape[1]
    rows = []
    for far in (0,) + order:
        piece = lax.dynamic_slice(attn, ((x + far) % SIDE * n_rows, 0), (n_rows, width))
        rows.append(ring_x(piece, far) if far else piece)
    partial = project(core.reshape(1), rows, o_proj, mine, theirs)
    total = None
    for far in (0,) + order:
        start = (y + far) % SIDE * tok_moe
        piece = lax.dynamic_slice(partial, (start, 0), (tok_moe, partial.shape[1]))
        if far:
            piece = ring_y(piece, far)
        piece = piece.astype(jnp.float32)
        total = piece if total is None else total + piece
    return total.astype(jnp.bfloat16)


def expert_kernel(n_ff, rows_ref, gate_ref, up_ref, down_ref, out_ref, hidden_ref):
    step = pl.program_id(0)
    ff_tile = gate_ref.shape[2]

    @pl.when(step < n_ff)
    def _():
        rows = rows_ref[...]
        gate = jnp.dot(rows, gate_ref[0], preferred_element_type=jnp.float32)
        up = jnp.dot(rows, up_ref[0], preferred_element_type=jnp.float32)
        hidden = gate / (1.0 + jnp.exp(-gate)) * up
        cols = pl.ds(pl.multiple_of(step * ff_tile, ff_tile), ff_tile)
        hidden_ref[:, cols] = hidden.astype(jnp.bfloat16)

    @pl.when(step >= n_ff)
    def _():
        out_ref[...] = jnp.dot(
            hidden_ref[...], down_ref[0], preferred_element_type=jnp.float32
        ).astype(jnp.bfloat16)


def expert_rows(rows, w_gate, w_up, w_down):
    n_rows, width = rows.shape
    ff = w_gate.shape[2]
    ff_tile, out_tile = 256, 512
    n_ff, n_out = ff // ff_tile, width // out_tile

    def ff_at(i):
        return (0, 0, jnp.minimum(i, n_ff - 1))

    def out_at(i):
        return jnp.maximum(i - n_ff, 0)

    return pl.pallas_call(
        lambda *refs: expert_kernel(n_ff, *refs),
        grid=(n_ff + n_out,),
        in_specs=[
            pl.BlockSpec(memory_space=pltpu.VMEM),
            pl.BlockSpec((1, width, ff_tile), ff_at),
            pl.BlockSpec((1, width, ff_tile), ff_at),
            pl.BlockSpec((1, ff, out_tile), lambda i: (0, 0, out_at(i))),
        ],
        out_specs=pl.BlockSpec((n_rows, out_tile), lambda i: (0, out_at(i))),
        out_shape=pltpu.HBM((n_rows, width), jnp.bfloat16),
        scratch_shapes=[pltpu.VMEM((n_rows, ff), jnp.bfloat16)],
        compiler_params=pltpu.CompilerParams(vmem_limit_bytes=32 * 1024 * 1024),
        cost_estimate=pl.CostEstimate(
            flops=6 * n_rows * width * ff,
            bytes_accessed=2 * (2 * n_rows * width + 3 * width * ff),
            transcendentals=n_rows * ff,
        ),
        name="experts",
    )(rows, w_gate, w_up, w_down)


def slot_tables(routes, route_weights, n_experts, cap):
    n_tok, n_slots = routes.shape[0], n_experts * cap
    hit = jnp.zeros((n_tok, n_experts), jnp.bool_)
    weight = jnp.zeros((n_tok, n_experts), jnp.float32)
    expert_ids = lax.broadcasted_iota(jnp.int32, (n_tok, n_experts), 1)
    for k in range(routes.shape[1]):
        match = routes[:, k : k + 1] == expert_ids
        hit = jnp.logical_or(hit, match)
        weight = weight + jnp.where(match, route_weights[:, k : k + 1], 0.0)
    square = (n_tok, n_tok)
    ahead = lax.broadcasted_iota(jnp.int32, square, 0) > lax.broadcasted_iota(jnp.int32, square, 1)
    rank = jnp.dot(
        ahead.astype(jnp.bfloat16), hit.astype(jnp.bfloat16), preferred_element_type=jnp.float32
    )
    place = jnp.where(hit, rank, float(2 * n_tok)).astype(jnp.bfloat16)
    high = weight.astype(jnp.bfloat16)
    low = (weight - high.astype(jnp.float32)).astype(jnp.bfloat16)
    spread = lax.broadcasted_iota(jnp.int32, (n_experts, n_slots), 0) == (
        lax.broadcasted_iota(jnp.int32, (n_experts, n_slots), 1) // cap
    )
    wide = jnp.dot(
        jnp.concatenate([place, high, low], axis=0),
        spread.astype(jnp.bfloat16),
        preferred_element_type=jnp.float32,
    )
    slot_ids = lax.broadcasted_iota(jnp.int32, (n_tok, n_slots), 1) % cap
    taken = wide[:n_tok] == slot_ids.astype(jnp.float32)
    pick = taken.astype(jnp.bfloat16)
    mix = jnp.where(jnp.concatenate([taken, taken], axis=0), wide[n_tok:], 0.0)
    return pick.T, mix.astype(jnp.bfloat16)


def combine_kernel(mix_ref, rows_ref, out_ref):
    n_tok, tile = out_ref.shape
    cols = pl.ds(pl.multiple_of(pl.program_id(0) * tile, tile), tile)
    halves = jnp.dot(mix_ref[...], rows_ref[:, cols], preferred_element_type=jnp.float32)
    out_ref[...] = (halves[:n_tok] + halves[n_tok:]).astype(jnp.bfloat16)


def combine(mix, rows):
    n_rows, width = rows.shape
    n_tok, tile = mix.shape[0] // 2, 896
    return pl.pallas_call(
        combine_kernel,
        grid=(width // tile,),
        in_specs=[pl.BlockSpec(memory_space=pltpu.VMEM)] * 2,
        out_specs=pl.BlockSpec((n_tok, tile), lambda i: (0, i)),
        out_shape=jax.ShapeDtypeStruct((n_tok, width), jnp.bfloat16),
        compiler_params=pltpu.CompilerParams(vmem_limit_bytes=24 * 1024 * 1024),
        cost_estimate=pl.CostEstimate(
            flops=4 * n_tok * n_rows * width, bytes_accessed=2 * n_rows * width, transcendentals=0
        ),
        name="combine",
    )(mix, rows)


def per_device(
    queries,
    keys,
    values,
    gates,
    o_proj,
    residual,
    norm_gain,
    routes,
    route_weights,
    w_gate,
    w_up,
    w_down,
):
    tok_moe = residual.shape[0]
    summed = projected(queries, keys, values, gates, o_proj, tok_moe)
    residual_sum = residual.astype(jnp.float32) + summed.astype(jnp.float32)
    norm_scale = lax.rsqrt(jnp.mean(residual_sum * residual_sum, axis=-1, keepdims=True) + 1e-06)
    moe_in = (residual_sum * norm_scale * norm_gain).astype(jnp.bfloat16)
    width = moe_in.shape[1]
    n_experts = w_gate.shape[0] * lax.axis_size("seq") * lax.axis_size("exp")
    cap = 2 * tok_moe * ROUTE_K // n_experts
    place, mix = slot_tables(routes, route_weights, n_experts, cap)
    senders = jnp.dot(place, moe_in, preferred_element_type=jnp.float32).astype(jnp.bfloat16)
    received = lax.all_to_all(
        senders.reshape(n_experts, cap, width),
        ("seq", "exp"),
        split_axis=0,
        concat_axis=0,
        tiled=True,
    )
    produced = expert_rows(received.reshape(n_experts * cap, width), w_gate, w_up, w_down)
    returned = lax.all_to_all(
        produced.reshape(n_experts, cap, width),
        ("seq", "exp"),
        split_axis=0,
        concat_axis=0,
        tiled=True,
    )
    moe_out = combine(mix, returned.reshape(n_experts * cap, width))
    return (summed, moe_out)


def solution(mesh):
    in_specs = (
        P("seq", "exp"),
        P("seq", "exp"),
        P("seq", "exp"),
        P(),
        P("exp", None),
        P(("seq", "exp"), None),
        P(),
        P(("seq", "exp"), None),
        P(("seq", "exp"), None),
        P(("seq", "exp"), None, None),
        P(("seq", "exp"), None, None),
        P(("seq", "exp"), None, None),
    )
    out_specs = (P(("seq", "exp"), None), P(("seq", "exp"), None))
    return jax.shard_map(
        per_device, mesh=mesh, in_specs=in_specs, out_specs=out_specs, check_vma=False
    )
```

time: 389 us -> 363 us (0.933)
  local copies, waits for them, and re-layouts: 21.4 us -> 8.23 us
  starting transfers between devices: 52.6 us -> 41.4 us
  matrix products: 10.4 us -> 3.28 us
  Pallas kernels: 48.7 us -> 53.6 us
  other arithmetic: 7.68 us -> 11.9 us
  between operations: 5.06 us -> 0.97 us
    unnamed x60 -> x36, local copies, waits for them, and re-layouts: 16.2 us -> 0.09 us
    ppermute x6 -> x3, waiting for transfers between devices: 24.6 us -> 9.24 us  [attend(): near = [lax.ppermute(own, 'seq', chip_perm(far)) for far in range(1, SIDE)]]
    ppermute x0 -> x3, waiting for transfers between devices: none -> 12.3 us  [attend(): lax.ppermute(after(sent, seen), 'seq', chip_perm(far))]
    ppermute x9 -> x3, starting transfers between devices: 15.6 us -> 5.05 us  [ring_y(): return lax.ppermute(array, 'exp', perm)]
    ppermute x0 -> x3, starting transfers between devices: none -> 10.4 us  [attend(): lax.ppermute(after(sent, seen), 'seq', chip_perm(far))]
    ppermute x9 -> x3, waiting for transfers between devices: 9.71 us -> 18.6 us  [ring_y(): return lax.ppermute(array, 'exp', perm)]
    ppermute x6 -> x3, starting transfers between devices: 18.6 us -> 11 us  [attend(): near = [lax.ppermute(own, 'seq', chip_perm(far)) for far in range(1, SIDE)]]
    dot_general x2, matrix products: 7.87 us -> 1.14 us  [the longest x1 0.86 us: slot_tables(): jnp.dot(ahead.astype(jnp.bfloat16), hit.astype(jnp.bfloat16), preferred_e...]
  transfers between devices with their start and end apart: 27 -> 19, of which waited for: 14 -> 12; matrix products, arithmetic and copies ran while one was open for 3% -> 3% of each run, Pallas kernels for 5% -> 4%
where the time goes in v3:
time: 363 us; the launch traced here: 362 us
  waiting for transfers between devices  144 us (40%)
  blocking collectives  98.2 us (27%)
  Pallas kernels  53.6 us (15%)
  starting transfers between devices  41.4 us (11%)
  other arithmetic  11.9 us (3%)
  local copies, waits for them, and re-layouts  8.23 us (2%)
    all_to_all x1, blocking collectives, per_device(): lax.all_to_all(senders.reshape(n_experts, cap, width), ('seq', 'exp'), sp...  98.2 us
    all_to_all x1, waiting for transfers between devices, per_device(): lax.all_to_all(produced.reshape(n_experts, cap, width), ('seq', 'exp'), s...  89.5 us
    pallas_call x1, Pallas kernels, expert_rows(): pl.pallas_call(lambda *refs: expert_kernel(n_ff, *refs), grid=(n_ff + n_o...  29.6 us
    ppermute x3, waiting for transfers between devices, ring_y(): return lax.ppermute(array, 'exp', perm)  18.6 us
    pallas_call x2, Pallas kernels, attend_head(): pl.pallas_call(lambda *refs: attend_kernel(*refs[len(extra):]), grid=(1,)...  13 us
    ppermute x6, waiting for transfers between devices, ring_x(): return lax.ppermute(array, 'exp', perm)  12.3 us
    ppermute x3, waiting for transfers between devices, attend(): lax.ppermute(after(sent, seen), 'seq', chip_perm(far))  12.3 us
    ppermute x3, starting transfers between devices, attend(): near = [lax.ppermute(own, 'seq', chip_perm(far)) for far in range(1, SIDE)]  11 us
  transfers between devices with their start and end apart: 19, of which 12 were waited for; matrix products, arithmetic and copies ran while one was open for 3% of the time, Pallas kernels for 4%

profile of v3, /device:TPU:5, one launch (start us, length us, event | category | flops | bytes accessed | tf_op | source)
XLA Modules:
  0.0 362.0 jit_solution(9267196652802168918)
XLA Ops:
  0.7 2.1 fusion.41
  3.6 2.2 constant_dynamic-slice_fusion.8
  7.3 6.5 %collective-permute-start.2 = (bf16[1024,256]{1,0:T(8,128)(2,1)}, bf16[1024,256]{1,0:T(8,128)(2,1)}, u32[]{:S(2)}, u32[]{:S(2)}) collective-permute-start(bf16[1024,256]{1,0:T(8,128)(2,1)} %pad_maximum_fusion.1.refs_2_), channel_id=1, source_target_pairs={{0,96},{16,112},{1,97},{17,113},{2,98},{18,114},{3,99},{19,115},{4... | collective-permute-start | bytes 1572872 | tf_op jit(solution)/shard_map/ppermute | solution.py:184
  13.7 2.1 collective-permute-start.1
  15.8 2.5 collective-permute-start
  20.3 7.0 %collective-permute-done.3.refs_5_ = bf16[128,3584]{1,0:T(8,128)(2,1)S(1)} collective-permute-done((bf16[128,3584]{1,0:T(8,128)(2,1)}, bf16[128,3584]{1,0:T(8,128)(2,1)S(1)}, u32[]{:S(2)}, u32[]{:S(2)}) %collective-permute-start.3) | collective-permute-done | bytes 917536 | tf_op jit(solution)/shard_map/ppermute | solution.py:152
  27.3 7.1 %collective-permute-done.2.refs_5_ = bf16[1024,256]{1,0:T(8,128)(2,1)} collective-permute-done((bf16[1024,256]{1,0:T(8,128)(2,1)}, bf16[1024,256]{1,0:T(8,128)(2,1)}, u32[]{:S(2)}, u32[]{:S(2)}) %collective-permute-start.2) | collective-permute-done | bytes 524320 | tf_op jit(solution)/shard_map/ppermute | solution.py:184
  34.4 2.1 collective-permute-done.refs_3_
  36.6 1.8 select_select_fusion.1
  38.3 2.2 collective-permute-start.8
  43.5 4.1 %collective-permute-start.5 = (bf16[1024,256]{1,0:T(8,128)(2,1)S(1)}, bf16[1024,256]{1,0:T(8,128)(2,1)S(1)}, u32[]{:S(2)}, u32[]{:S(2)}) collective-permute-start(bf16[1024,256]{1,0:T(8,128)(2,1)S(1)} %pad_maximum_fusion.2.refs_3_), channel_id=1, source_target_pairs={{0,32},{16,48},{32,64},{48,80},{64,96},{80,112},{1,33},{17,49},{33... | collective-permute-start | bytes 1572872 | tf_op jit(solution)/shard_map/ppermute | solution.py:191
  47.7 4.2 %collective-permute-start.6 = (bf16[1024,256]{1,0:T(8,128)(2,1)S(1)}, bf16[1024,256]{1,0:T(8,128)(2,1)}, u32[]{:S(2)}, u32[]{:S(2)}) collective-permute-start(bf16[1024,256]{1,0:T(8,128)(2,1)S(1)} %pad_maximum_fusion.2.refs_3_), channel_id=1, source_target_pairs={{0,64},{16,80},{32,96},{48,112},{1,65},{17,81},{33,97},{49,113},{2... | collective-permute-start | bytes 1572872 | tf_op jit(solution)/shard_map/ppermute | solution.py:191
  51.8 2.1 collective-permute-start.7
  53.9 6.4 %attend.2.refs_0_ = bf16[1024,256]{1,0:T(8,128)(2,1)} custom-call(s32[2]{0:T(128)} %compare_select_fusion.1.refs_0_.refs_1_, bf16[1024,256]{1,0:T(8,128)(2,1)} %refs_2_.2, bf16[1024,256]{1,0:T(8,128)(2,1)} %pad_maximum_fusion.1.refs_2_, bf16[1024,256]{1,0:T(8,128)(2,1)} %collective-permute-done.refs_3_, bf16[1024,256]{1,0:T(8,128)(2,1)} %collective-permute-done.1.refs_4_, ...), custom_call_target="tpu_custom_call" | custom-call | flops 8589934592 | bytes 1835008 | tf_op jit(solution)/shard_map/attend/pallas_call | solution.py:82
  60.3 9.5 %collective-permute-done.6.refs_5_ = bf16[1024,256]{1,0:T(8,128)(2,1)} collective-permute-done((bf16[1024,256]{1,0:T(8,128)(2,1)S(1)}, bf16[1024,256]{1,0:T(8,128)(2,1)}, u32[]{:S(2)}, u32[]{:S(2)}) %collective-permute-start.6) | collective-permute-done | bytes 524320 | tf_op jit(solution)/shard_map/ppermute | solution.py:191
  69.8 2.8 collective-permute-done.7.refs_6_
  74.7 2.4 collective-permute-done.10.refs_7_
  77.1 3.2 pad_maximum_fusion
  83.5 6.6 %attend.3 = bf16[1024,256]{1,0:T(8,128)(2,1)} custom-call(bf16[1024,256]{1,0:T(8,128)(2,1)} %attend.2.refs_0_, s32[2]{0:T(128)} %compare_select_fusion.1.refs_0_.refs_1_, bf16[1024,256]{1,0:T(8,128)(2,1)} %refs_2_.2, bf16[1024,256]{1,0:T(8,128)(2,1)} %copy-done.1, bf16[1024,256]{1,0:T(8,128)(2,1)} %copy-done.4, ...), custom_call_target="tpu_custom_call", output_to_operand_aliasing={{}: (0, {})} | custom-call | flops 8589934592 | bytes 1835008 | tf_op jit(solution)/shard_map/attend/pallas_call | solution.py:82
  90.2 1.8 constant_dynamic-slice_fusion.3
  95.5 3.3 collective-permute-done.13.refs_3_
  98.8 1.6 collective-permute-done.12.refs_2_
  100.9 5.2 %project.1 = bf16[256,3584]{1,0:T(8,128)(2,1)S(1)} custom-call(s32[1]{0:T(128)} %bitcast.core_ref, bf16[256,256]{1,0:T(8,128)(2,1)S(1)} %get-tuple-element.60.refs_0_, bf16[256,256]{1,0:T(8,128)(2,1)S(1)} %collective-permute-done.11.refs_1_, bf16[256,256]{1,0:T(8,128)(2,1)S(1)} %collective-permute-done.12.refs_2_, ...), custom_call_target="tpu_custom_call" | custom-call | flops 4227858432 | bytes 7733248 | tf_op jit(solution)/shard_map/project/pallas_call | solution.py:124
  107.6 2.6 collective-permute-start.17
  111.7 7.7 %collective-permute-done.15 = bf16[64,3584]{1,0:T(8,128)(2,1)S(1)} collective-permute-done((bf16[64,3584]{1,0:T(8,128)(2,1)S(1)}, bf16[64,3584]{1,0:T(8,128)(2,1)S(1)}, u32[]{:S(2)}, u32[]{:S(2)}) %collective-permute-start.15) | collective-permute-done | bytes 458784 | tf_op jit(solution)/shard_map/ppermute | solution.py:157
  119.4 10.9 %collective-permute-done.17 = bf16[64,3584]{1,0:T(8,128)(2,1)S(1)} collective-permute-done((bf16[64,3584]{1,0:T(8,128)(2,1)S(1)}, bf16[64,3584]{1,0:T(8,128)(2,1)S(1)}, u32[]{:S(2)}, u32[]{:S(2)}) %collective-permute-start.17) | collective-permute-done | bytes 458784 | tf_op jit(solution)/shard_map/ppermute | solution.py:157
  130.8 2.1 fusion
  133.0 98.2 %all_to_all.10 = bf16[128,8,3584]{2,1,0:T(8,128)(2,1)S(1)} all-to-all(bf16[128,8,3584]{2,1,0:T(8,128)(2,1)S(1)} %fusion), channel_id=1, replica_groups=mesh['seq'=8,'exp'=16] {'seq','exp'}, dimensions={0} | all-to-all | bytes 14680064 | tf_op jit(solution)/shard_map/all_to_all | solution.py:373
  231.2 29.6 %experts.1 = bf16[1024,3584]{1,0:T(8,128)(2,1)} custom-call(bf16[1024,3584]{1,0:T(8,128)(2,1)S(1)} %bitcast.39, bf16[1,3584,1024]{2,1,0:T(8,128)(2,1)S(1)} %bitcast.41, bf16[1,3584,1024]{2,1,0:T(8,128)(2,1)S(1)} %bitcast.43, bf16[1,1024,3584]{2,1,0:T(8,128)(2,1)} %refs_3_.1), custom_call_target="tpu_custom_call" | custom-call | flops 22548578304 | bytes 36700160 | tf_op jit(solution)/shard_map/experts/pallas_call | solution.py:271
  260.8 5.9 %all-to-all-start.1 = ((bf16[128,8,3584]{2,1,0:T(8,128)(2,1)}), bf16[128,8,3584]{2,1,0:T(8,128)(2,1)}, u32[]{:S(2)}, u32[]{:S(2)}) async-start(bf16[128,8,3584]{2,1,0:T(8,128)(2,1)} %bitcast.44), calls=%async_computation.1 | async-start | bytes 14680064 | tf_op jit(solution)/shard_map/all_to_all | solution.py:381
  266.8 89.5 %all-to-all-done.1 = bf16[128,8,3584]{2,1,0:T(8,128)(2,1)} async-done(((bf16[128,8,3584]{2,1,0:T(8,128)(2,1)}), bf16[128,8,3584]{2,1,0:T(8,128)(2,1)}, u32[]{:S(2)}, u32[]{:S(2)}) %all-to-all-start.1) | async-done | bytes 7340064 | tf_op jit(solution)/shard_map/all_to_all | solution.py:381
  356.3 5.7 %combine.1 = bf16[64,3584]{1,0:T(8,128)(2,1)} custom-call(bf16[128,1024]{1,0:T(8,128)(2,1)S(1)} %fusion.2.mix_ref, bf16[1024,3584]{1,0:T(8,128)(2,1)} %bitcast.20.rows_ref), custom_call_target="tpu_custom_call" | custom-call | flops 939524096 | bytes 7340032 | tf_op jit(solution)/shard_map/combine/pallas_call | solution.py:335
  (78 shorter events, 20.0 us)
Async XLA Ops:
  0.6 39.9 %copy-start = (bf16[256,3584]{1,0:T(8,128)(2,1)S(1)}, bf16[256,3584]{1,0:T(8,128)(2,1)}, u32[]{:S(2)}) copy-start(bf16[256,3584]{1,0:T(8,128)(2,1)} %refs_4_.1) | copy-start | bytes 5505028
  5.8 21.5 %collective-permute-start.3 = (bf16[128,3584]{1,0:T(8,128)(2,1)}, bf16[128,3584]{1,0:T(8,128)(2,1)S(1)}, u32[]{:S(2)}, u32[]{:S(2)}) collective-permute-start(bf16[128,3584]{1,0:T(8,128)(2,1)} %constant_dynamic-slice_fusion.8), channel_id=1, source_target_pairs={{0,4},{1,5},{2,6},{3,7},{4,8},{5,9},{6,10},{7,11},{8,12},{9,13},{1... | collective-permute-start | bytes 2752520 | tf_op jit(solution)/shard_map/ppermute | solution.py:152
  6.7 29.9 %collective-permute-start.4 = (bf16[128,3584]{1,0:T(8,128)(2,1)}, bf16[128,3584]{1,0:T(8,128)(2,1)}, u32[]{:S(2)}, u32[]{:S(2)}) collective-permute-start(bf16[128,3584]{1,0:T(8,128)(2,1)} %constant_dynamic-slice_fusion.8), channel_id=1, source_target_pairs={{0,12},{1,13},{2,14},{3,15},{4,0},{5,1},{6,2},{7,3},{8,4},{9,5},{1... | collective-permute-start | bytes 2752520 | tf_op jit(solution)/shard_map/ppermute | solution.py:152
  7.3 27.2 %collective-permute-start.2 = (bf16[1024,256]{1,0:T(8,128)(2,1)}, bf16[1024,256]{1,0:T(8,128)(2,1)}, u32[]{:S(2)}, u32[]{:S(2)}) collective-permute-start(bf16[1024,256]{1,0:T(8,128)(2,1)} %pad_maximum_fusion.1.refs_2_), channel_id=1, source_target_pairs={{0,96},{16,112},{1,97},{17,113},{2,98},{18,114},{3,99},{19,115},{4... | collective-permute-start | bytes 1572872 | tf_op jit(solution)/shard_map/ppermute | solution.py:184
  13.7 20.7 %collective-permute-start.1 = (bf16[1024,256]{1,0:T(8,128)(2,1)}, bf16[1024,256]{1,0:T(8,128)(2,1)}, u32[]{:S(2)}, u32[]{:S(2)}) collective-permute-start(bf16[1024,256]{1,0:T(8,128)(2,1)} %pad_maximum_fusion.1.refs_2_), channel_id=1, source_target_pairs={{0,64},{16,80},{32,96},{48,112},{1,65},{17,81},{33,97},{49,113},{2... | collective-permute-start | bytes 1572872 | tf_op jit(solution)/shard_map/ppermute | solution.py:184
  15.8 20.8 %collective-permute-start = (bf16[1024,256]{1,0:T(8,128)(2,1)}, bf16[1024,256]{1,0:T(8,128)(2,1)}, u32[]{:S(2)}, u32[]{:S(2)}) collective-permute-start(bf16[1024,256]{1,0:T(8,128)(2,1)} %pad_maximum_fusion.1.refs_2_), channel_id=1, source_target_pairs={{0,32},{16,48},{32,64},{48,80},{64,96},{80,112},{1,33},{17,49},{33... | collective-permute-start | bytes 1572872 | tf_op jit(solution)/shard_map/ppermute | solution.py:184
  20.3 52.4 %copy-start.1 = (bf16[1024,256]{1,0:T(8,128)(2,1)}, bf16[1024,256]{1,0:T(8,128)(2,1)S(1)}, u32[]{:S(2)}) copy-start(bf16[1024,256]{1,0:T(8,128)(2,1)S(1)} %pad_maximum_fusion.2.refs_3_) | copy-start | bytes 1572868
  38.3 15.6 %collective-permute-start.8 = (bf16[2,1024,256]{2,1,0:T(8,128)(2,1)S(1)}, bf16[2,1024,256]{2,1,0:T(8,128)(2,1)}, u32[]{:S(2)}, u32[]{:S(2)}) collective-permute-start(bf16[2,1024,256]{2,1,0:T(8,128)(2,1)S(1)} %select_select_fusion.1), channel_id=1, source_target_pairs={{0,16},{16,0},{32,48},{48,32},{64,80},{80,64},{96,112},{112,96},{1... | collective-permute-start | bytes 3145736 | tf_op jit(solution)/shard_map/ppermute | solution.py:162
  41.6 31.1 %collective-permute-start.9 = (bf16[128,3584]{1,0:T(8,128)(2,1)}, bf16[128,3584]{1,0:T(8,128)(2,1)}, u32[]{:S(2)}, u32[]{:S(2)}) collective-permute-start(bf16[128,3584]{1,0:T(8,128)(2,1)} %constant_dynamic-slice_fusion.7), channel_id=1, source_target_pairs={{0,8},{1,9},{2,10},{3,11},{4,12},{5,13},{6,14},{7,15},{8,0},{9,1},... | collective-permute-start | bytes 2752520 | tf_op jit(solution)/shard_map/ppermute | solution.py:152
  43.5 16.8 %collective-permute-start.5 = (bf16[1024,256]{1,0:T(8,128)(2,1)S(1)}, bf16[1024,256]{1,0:T(8,128)(2,1)S(1)}, u32[]{:S(2)}, u32[]{:S(2)}) collective-permute-start(bf16[1024,256]{1,0:T(8,128)(2,1)S(1)} %pad_maximum_fusion.2.refs_3_), channel_id=1, source_target_pairs={{0,32},{16,48},{32,64},{48,80},{64,96},{80,112},{1,33},{17,49},{33... | collective-permute-start | bytes 1572872 | tf_op jit(solution)/shard_map/ppermute | solution.py:191
  47.7 22.2 %collective-permute-start.6 = (bf16[1024,256]{1,0:T(8,128)(2,1)S(1)}, bf16[1024,256]{1,0:T(8,128)(2,1)}, u32[]{:S(2)}, u32[]{:S(2)}) collective-permute-start(bf16[1024,256]{1,0:T(8,128)(2,1)S(1)} %pad_maximum_fusion.2.refs_3_), channel_id=1, source_target_pairs={{0,64},{16,80},{32,96},{48,112},{1,65},{17,81},{33,97},{49,113},{2... | collective-permute-start | bytes 1572872 | tf_op jit(solution)/shard_map/ppermute | solution.py:191
  51.8 20.9 %collective-permute-start.7 = (bf16[1024,256]{1,0:T(8,128)(2,1)S(1)}, bf16[1024,256]{1,0:T(8,128)(2,1)}, u32[]{:S(2)}, u32[]{:S(2)}) collective-permute-start(bf16[1024,256]{1,0:T(8,128)(2,1)S(1)} %pad_maximum_fusion.2.refs_3_), channel_id=1, source_target_pairs={{0,96},{16,112},{1,97},{17,113},{2,98},{18,114},{3,99},{19,115},{4... | collective-permute-start | bytes 1572872 | tf_op jit(solution)/shard_map/ppermute | solution.py:191
  60.3 21.5 %copy-start.10 = (s32[64,8]{0,1:T(8,128)S(1)}, s32[64,8]{0,1:T(8,128)}, u32[]{:S(2)}) copy-start(s32[64,8]{0,1:T(8,128)} %param.19) | copy-start | bytes 6148
  60.3 21.5 %copy-start.11 = (f32[64,8]{0,1:T(8,128)S(1)}, f32[64,8]{0,1:T(8,128)}, u32[]{:S(2)}) copy-start(f32[64,8]{0,1:T(8,128)} %param.20) | copy-start | bytes 6148
  60.3 16.8 %copy-start.4 = (bf16[1024,256]{1,0:T(8,128)(2,1)}, bf16[1024,256]{1,0:T(8,128)(2,1)S(1)}, u32[]{:S(2)}) copy-start(bf16[1024,256]{1,0:T(8,128)(2,1)S(1)} %collective-permute-done.5.refs_4_) | copy-start | bytes 1572868
  74.1 3.0 collective-permute-start.10
  80.3 20.6 %collective-permute-start.14 = (bf16[384,3584]{1,0:T(8,128)(2,1)}, bf16[384,3584]{1,0:T(8,128)(2,1)}, u32[]{:S(2)}, u32[]{:S(2)}) collective-permute-start(bf16[384,3584]{1,0:T(8,128)(2,1)} %pad_maximum_fusion), channel_id=1, source_target_pairs={{0,16},{16,0},{32,48},{48,32},{64,80},{80,64},{96,112},{112,96},{1... | collective-permute-start | bytes 8257544 | tf_op jit(solution)/shard_map/ppermute | solution.py:162
  91.9 6.9 %collective-permute-start.13 = (bf16[256,256]{1,0:T(8,128)(2,1)}, bf16[256,256]{1,0:T(8,128)(2,1)S(1)}, u32[]{:S(2)}, u32[]{:S(2)}) collective-permute-start(bf16[256,256]{1,0:T(8,128)(2,1)} %get-tuple-element.57), channel_id=1, source_target_pairs={{0,8},{1,9},{2,10},{3,11},{4,12},{5,13},{6,14},{7,15},{8,0},{9,1},... | collective-permute-start | bytes 393224 | tf_op jit(solution)/shard_map/ppermute | solution.py:152
  93.5 6.9 %collective-permute-start.12 = (bf16[256,256]{1,0:T(8,128)(2,1)S(1)}, bf16[256,256]{1,0:T(8,128)(2,1)S(1)}, u32[]{:S(2)}, u32[]{:S(2)}) collective-permute-start(bf16[256,256]{1,0:T(8,128)(2,1)S(1)} %get-tuple-element.58), channel_id=1, source_target_pairs={{0,12},{1,13},{2,14},{3,15},{4,0},{5,1},{6,2},{7,3},{8,4},{9,5},{1... | collective-permute-start | bytes 393224 | tf_op jit(solution)/shard_map/ppermute | solution.py:152
  93.7 7.1 %collective-permute-start.11 = (bf16[256,256]{1,0:T(8,128)(2,1)S(1)}, bf16[256,256]{1,0:T(8,128)(2,1)S(1)}, u32[]{:S(2)}, u32[]{:S(2)}) collective-permute-start(bf16[256,256]{1,0:T(8,128)(2,1)S(1)} %get-tuple-element.59), channel_id=1, source_target_pairs={{0,4},{1,5},{2,6},{3,7},{4,8},{5,9},{6,10},{7,11},{8,12},{9,13},{1... | collective-permute-start | bytes 393224 | tf_op jit(solution)/shard_map/ppermute | solution.py:152
  100.9 10.8 %copy-start.7 = (s32[1024]{0:T(1024)S(1)}, s32[1024]{0:T(1024)}, u32[]{:S(2)}) copy-start(s32[1024]{0:T(1024)} %get-tuple-element.87) | copy-start | bytes 12292
  100.9 29.4 %copy-start.2 = (bf16[64,3584]{1,0:T(8,128)(2,1)S(1)}, bf16[64,3584]{1,0:T(8,128)(2,1)}, u32[]{:S(2)}) copy-start(bf16[64,3584]{1,0:T(8,128)(2,1)} %param.17) | copy-start | bytes 1376260
  106.1 24.7 %copy-start.6 = (f32[3584]{0:T(1024)S(1)}, f32[3584]{0:T(1024)}, u32[]{:S(2)}) copy-start(f32[3584]{0:T(1024)} %param.18) | copy-start | bytes 43012
  106.3 13.1 %collective-permute-start.15 = (bf16[64,3584]{1,0:T(8,128)(2,1)S(1)}, bf16[64,3584]{1,0:T(8,128)(2,1)S(1)}, u32[]{:S(2)}, u32[]{:S(2)}) collective-permute-start(bf16[64,3584]{1,0:T(8,128)(2,1)S(1)} %get-tuple-element.54), channel_id=1, source_target_pairs={{0,1},{1,2},{2,3},{3,0},{4,5},{5,6},{6,7},{7,4},{8,9},{9,10},{10,1... | collective-permute-start | bytes 1376264 | tf_op jit(solution)/shard_map/ppermute | solution.py:157
  107.6 22.7 %collective-permute-start.17 = (bf16[64,3584]{1,0:T(8,128)(2,1)S(1)}, bf16[64,3584]{1,0:T(8,128)(2,1)S(1)}, u32[]{:S(2)}, u32[]{:S(2)}) collective-permute-start(bf16[64,3584]{1,0:T(8,128)(2,1)S(1)} %get-tuple-element.55), channel_id=1, source_target_pairs={{0,2},{1,3},{2,0},{3,1},{4,6},{5,7},{6,4},{7,5},{8,10},{9,11},{10,... | collective-permute-start | bytes 1376264 | tf_op jit(solution)/shard_map/ppermute | solution.py:157
  110.2 20.1 %collective-permute-start.16 = (bf16[64,3584]{1,0:T(8,128)(2,1)S(1)}, bf16[64,3584]{1,0:T(8,128)(2,1)S(1)}, u32[]{:S(2)}, u32[]{:S(2)}) collective-permute-start(bf16[64,3584]{1,0:T(8,128)(2,1)S(1)} %get-tuple-element.56), channel_id=1, source_target_pairs={{0,3},{1,0},{2,1},{3,2},{4,7},{5,4},{6,5},{7,6},{8,11},{9,8},{10,9... | collective-permute-start | bytes 1376264 | tf_op jit(solution)/shard_map/ppermute | solution.py:157
  130.8 100.4 %copy-start.3 = (bf16[64,3584]{1,0:T(8,128)(2,1)}, bf16[64,3584]{1,0:T(8,128)(2,1)S(1)}, u32[]{:S(2)}) copy-start(bf16[64,3584]{1,0:T(8,128)(2,1)S(1)} %get-tuple-element.49) | copy-start | bytes 1376260
  130.8 100.4 %slice-start = ((s8[7340032]{0:T(1024)(128)(4,1)}), s8[4194304]{0:T(1024)(128)(4,1)S(1)}, s32[]{:S(2)}) async-start(s8[7340032]{0:T(1024)(128)(4,1)} %bitcast.40), calls=%async_computation.2 | async-start | bytes 8388608
  130.8 100.4 %slice-start.2 = ((s8[7340032]{0:T(1024)(128)(4,1)}), s8[4194304]{0:T(1024)(128)(4,1)S(1)}, s32[]{:S(2)}) async-start(s8[7340032]{0:T(1024)(128)(4,1)} %bitcast.42), calls=%async_computation.4 | async-start | bytes 8388608
  133.0 98.2 %slice-start.1 = ((s8[7340032]{0:T(1024)(128)(4,1)}), s8[3145728]{0:T(1024)(128)(4,1)S(1)}, s32[]{:S(2)}) async-start(s8[7340032]{0:T(1024)(128)(4,1)} %bitcast.40), calls=%async_computation.3 | async-start | bytes 6291456
  133.0 98.2 %slice-start.3 = ((s8[7340032]{0:T(1024)(128)(4,1)}), s8[3145728]{0:T(1024)(128)(4,1)S(1)}, s32[]{:S(2)}) async-start(s8[7340032]{0:T(1024)(128)(4,1)} %bitcast.42), calls=%async_computation.5 | async-start | bytes 6291456
  260.8 95.4 %all-to-all-start.1 = ((bf16[128,8,3584]{2,1,0:T(8,128)(2,1)}), bf16[128,8,3584]{2,1,0:T(8,128)(2,1)}, u32[]{:S(2)}, u32[]{:S(2)}) async-start(bf16[128,8,3584]{2,1,0:T(8,128)(2,1)} %bitcast.44), calls=%async_computation.1 | async-start | bytes 14680064 | tf_op jit(solution)/shard_map/all_to_all | solution.py:381
  (5 other events, 52.9 us)

commit v4 on v3

--- a/solution.py
+++ b/solution.py
@@ -29,23 +29,45 @@
     return both[:, :HD], both[:, HD:]
 
 
-def attend_kernel(code_ref, q_ref, own_ref, *refs):
-    near, swapped, out_ref = refs[:-6], refs[-6], refs[-5]
-    held, tops, sums, accs = refs[-4:]
-    n_tiles = q_ref.shape[0] // Q_TILE
-    for i in range(n_tiles):
+def own_kernel(q_ref, kv_ref, top_ref, sum_ref, acc_ref):
+    for i in range(q_ref.shape[0] // Q_TILE):
         at = pl.ds(i * Q_TILE, Q_TILE)
         seen = pl.ds(0, (i + 1) * Q_TILE)
-        scores = dot_t(q_ref[at, :], own_ref[seen, :HD])
+        scores = dot_t(q_ref[at, :], kv_ref[0, seen, :])
         query_pos = lax.broadcasted_iota(jnp.int32, scores.shape, 0) + i * Q_TILE
         key_pos = lax.broadcasted_iota(jnp.int32, scores.shape, 1)
         scores = jnp.where(key_pos <= query_pos, scores, NEG_FILL)
         top = jnp.max(scores, axis=1, keepdims=True)
         weights = jnp.exp2((scores - top) * SCALE)
-        acc, amount = mix_values(weights, own_ref[seen, HD:])
-        tops[at, :] = jnp.broadcast_to(top, (Q_TILE, HD))
-        sums[at, :] = amount
-        accs[at, :] = acc
+        acc, amount = mix_values(weights, kv_ref[1, seen, :])
+        top_ref[at, :] = jnp.broadcast_to(top, (Q_TILE, HD))
+        sum_ref[at, :] = amount
+        acc_ref[at, :] = acc
+
+
+def attend_own(queries, kv):
+    n, width = queries.shape
+    spec = pl.BlockSpec((n, HD), lambda h: (0, h))
+    return pl.pallas_call(
+        own_kernel,
+        grid=(width // HD,),
+        in_specs=[spec, pl.BlockSpec((2, n, HD), lambda h: (0, 0, h))],
+        out_specs=[spec] * 3,
+        out_shape=[jax.ShapeDtypeStruct((n, width), jnp.float32)] * 3,
+        compiler_params=pltpu.CompilerParams(vmem_limit_bytes=60 * 1024 * 1024),
+        cost_estimate=pl.CostEstimate(
+            flops=8 * n * n * width, bytes_accessed=18 * n * width, transcendentals=n * n
+        ),
+        name="attend_own",
+    )(queries, kv)
+
+
+def far_kernel(code_ref, q_ref, top_ref, sum_ref, acc_ref, *refs):
+    near, swapped, out_ref = refs[:-6], refs[-6], refs[-5]
+    held, tops, sums, accs = refs[-4:]
+    tops[...] = top_ref[...]
+    sums[...] = sum_ref[...]
+    accs[...] = acc_ref[...]
     for j in range(swapped.shape[0]):
         code = code_ref[j]
         for s in range(len(near)):
@@ -60,14 +82,14 @@
 
         @pl.when(code > 0)
         def _():
-            for i in range(n_tiles):
+            for i in range(q_ref.shape[0] // Q_TILE):
                 at = pl.ds(i * Q_TILE, Q_TILE)
-                scores = dot_t(q_ref[at, :], held[:, :HD])
+                scores = dot_t(q_ref[at, :], held[0])
                 old = tops[at, :]
                 top = jnp.maximum(old, jnp.max(scores, axis=1, keepdims=True))
                 weights = jnp.exp2((scores - top[:, :1]) * SCALE)
                 fade = jnp.exp2((old - top) * SCALE)
-                acc, amount = mix_values(weights, held[:, HD:])
+                acc, amount = mix_values(weights, held[1])
                 tops[at, :] = top
                 sums[at, :] = sums[at, :] * fade + amount
                 accs[at, :] = accs[at, :] * fade + acc
@@ -75,31 +97,55 @@
     out_ref[...] = (accs[...] / sums[...]).astype(jnp.bfloat16)
 
 
-def attend_head(codes, queries, own, near, swapped, head, before):
+def attend_far(codes, queries, state, near, swapped, head, before):
     n = queries.shape[0]
-    block = pl.BlockSpec((n, 2 * HD), lambda i: (0, 0))
+    spec = pl.BlockSpec((n, HD), lambda i: (0, head))
     extra = [] if before is None else [before]
     return pl.pallas_call(
-        lambda *refs: attend_kernel(*refs[len(extra) :]),
+        lambda *refs: far_kernel(*refs[len(extra) :]),
         grid=(1,),
         in_specs=[pl.BlockSpec(memory_space=pl.ANY)] * len(extra)
-        + [
-            pl.BlockSpec(memory_space=pltpu.SMEM),
-            pl.BlockSpec((n, HD), lambda i: (0, head)),
-        ]
-        + [block] * (1 + len(near))
-        + [pl.BlockSpec(swapped.shape, lambda i: (0, 0, 0))],
-        out_specs=pl.BlockSpec((n, HD), lambda i: (0, head)),
+        + [pl.BlockSpec(memory_space=pltpu.SMEM)]
+        + [spec] * 4
+        + [pl.BlockSpec((2, n, HD), lambda i: (0, 0, head))] * len(near)
+        + [pl.BlockSpec(swapped.shape, lambda i: (0, 0, 0, 0))],
+        out_specs=spec,
         out_shape=jax.ShapeDtypeStruct(queries.shape, jnp.bfloat16),
         input_output_aliases={0: 0} if extra else {},
-        scratch_shapes=[pltpu.VMEM((n, 2 * HD), jnp.bfloat16)]
+        scratch_shapes=[pltpu.VMEM((2, n, HD), jnp.bfloat16)]
         + [pltpu.VMEM((n, HD), jnp.float32)] * 3,
         compiler_params=pltpu.CompilerParams(vmem_limit_bytes=60 * 1024 * 1024),
         cost_estimate=pl.CostEstimate(
-            flops=64 * n * n * HD, bytes_accessed=14 * n * HD, transcendentals=2 * n * n
+            flops=48 * n * n * HD, bytes_accessed=24 * n * HD, transcendentals=2 * n * n
         ),
-        name="attend",
-    )(*extra, codes, queries, own, *near, swapped)
+        name="attend_far",
+    )(*extra, codes, queries, *state, *near, swapped)
+
+
+def choose_kernel(far_ref, *refs):
+    blocks, out_ref = refs[:-1], refs[-1]
+    for j in range(out_ref.shape[0]):
+        for far, block in enumerate(blocks):
+
+            @pl.when(far_ref[j] == far)
+            def _(j=j, block=block):
+                out_ref[j] = block[...]
+
+
+def choose(fars, blocks, head):
+    n = blocks[0].shape[1]
+    count = fars.shape[0]
+    return pl.pallas_call(
+        choose_kernel,
+        grid=(1,),
+        in_specs=[pl.BlockSpec(memory_space=pltpu.SMEM)]
+        + [pl.BlockSpec((2, n, HD), lambda i: (0, 0, head))] * len(blocks),
+        out_specs=pl.BlockSpec((count, 2, n, HD), lambda i: (0, 0, 0, 0)),
+        out_shape=jax.ShapeDtypeStruct((count, 2, n, HD), jnp.bfloat16),
+        compiler_params=pltpu.CompilerParams(vmem_limit_bytes=60 * 1024 * 1024),
+        cost_estimate=pl.CostEstimate(flops=0, bytes_accessed=24 * n * HD, transcendentals=0),
+        name="choose",
+    )(fars, *blocks)
 
 
 def project_kernel(core_ref, *refs):
@@ -128,17 +174,17 @@
         + [pl.BlockSpec((n_rows, depth), lambda i: (0, 0))] * (1 + n)
         + [pl.BlockSpec((depth, tile), lambda i: (0, i))]
         + [pl.BlockSpec((HD, tile), lambda i: (0, i))] * n
-        + [pl.BlockSpec((HD, tile), lambda i, k=k: (k, i)) for k in range(n)],
+        + [pl.BlockSpec((HD, tile), lambda i, k=k: (k, i)) for k in (0, 1, 0)],
         out_specs=pl.BlockSpec((n_rows, tile), lambda i: (0, i)),
         out_shape=jax.ShapeDtypeStruct((n_rows, width), jnp.bfloat16),
-        compiler_params=pltpu.CompilerParams(vmem_limit_bytes=32 * 1024 * 1024),
+        compiler_params=pltpu.CompilerParams(vmem_limit_bytes=60 * 1024 * 1024),
         cost_estimate=pl.CostEstimate(
             flops=6 * n * n_rows * depth * width,
             bytes_accessed=2 * n * (n_rows * depth + depth * width) + 2 * n_rows * width,
             transcendentals=0,
         ),
         name="project",
-    )(core, *rows, own, *mine, *([theirs] * n))
+    )(core, *rows, own, *mine, theirs[0], theirs[0], theirs[1])
 
 
 def chip_perm(far):
@@ -166,59 +212,41 @@
     return lax.optimization_barrier((array, *earlier))[0]
 
 
-def attend(queries, keys, values, gates, first_shards, last_shard):
+def attend(queries, keys, values, gates, share, send_share, early):
     me = lax.axis_index("seq")
     chip, core = me // CORES, me % CORES
     wanted = gates[me, 1:]
     codes = jnp.where(
         wanted == me, 0, jnp.where(wanted % CORES == core, chip - wanted // CORES, SIDE)
     ).astype(jnp.int32)
-    partner_far = (chip - gates[me ^ 1, 1:] // CORES)[:, None, None]
-    owns = []
-    for head in range(queries.shape[1] // HD):
-        cols = slice(head * HD, (head + 1) * HD)
-        owns.append(jnp.concatenate([keys[:, cols], values[:, cols]], axis=1))
-    attn, near = None, None
-    for head, own in enumerate(owns):
-        if head == 0:
-            near = [lax.ppermute(own, "seq", chip_perm(far)) for far in range(1, SIDE)]
-            shards = first_shards(own)
-            later = [after(own, shards[0]) for own in owns[1:]]
-            near, shards, later = lax.optimization_barrier((near, shards, later))
-        else:
-            sent = later[head - 1]
-            near = [
-                lax.ppermute(after(sent, seen), "seq", chip_perm(far))
-                for far, seen in enumerate(near, 1)
-            ]
-            if head == 1:
-                shards = shards + [last_shard(shards[0])]
-            near, attn, shards = lax.optimization_barrier((near, attn, shards))
-        asked = own[None]
-        for far in range(1, SIDE):
-            asked = jnp.where(partner_far == far, near[far - 1][None], asked)
-        swapped = swap_cores(asked)
-        attn = attend_head(codes, queries, own, near, swapped, head, attn)
-    return attn, [after(shard, swapped) for shard in shards]
-
-
-def projected(queries, keys, values, gates, o_proj, tok_moe):
+    partner_far = jnp.clip(chip - gates[me ^ 1, 1:] // CORES, 0, SIDE - 1).astype(jnp.int32)
+    kv = jnp.stack([keys, values])
+    near = [lax.ppermute(kv, "seq", chip_perm(far)) for far in range(1, SIDE)]
+    mine = [send_share(share, 1), send_share(share, 3)]
+    mine.append(send_share(after(share, *mine), 2))
+    state = attend_own(queries, kv)
+    joined = jnp.concatenate(mine[:2])
+    near, mine, joined, state, early = lax.optimization_barrier(
+        (near, mine, joined, state, early)
+    )
+    heads = range(queries.shape[1] // HD)
+    asked = [choose(partner_far, [kv, *near], head) for head in heads]
+    swapped = [swap_cores(block) for block in asked]
+    theirs = [swap_cores(after(part, asked[-1])) for part in (joined, mine[2])]
+    attn = None
+    for head in heads:
+        attn = attend_far(codes, queries, state, near, swapped[head], head, attn)
+    return attn, mine, theirs, early
+
+
+def projected(queries, keys, values, gates, o_proj, tok_moe, early):
     at = lax.axis_index("exp")
     x, y = at // SIDE, at % SIDE
     order = (1, 3, 2)
 
     core = lax.axis_index("seq") % CORES
-    share = (core * HD, 0), (HD, o_proj.shape[1])
-
-    def first_shards(seen):
-        part = lax.dynamic_slice(after(o_proj, seen), *share)
-        return [ring_x(part, far) for far in order[:2]]
-
-    def last_shard(seen):
-        return ring_x(lax.dynamic_slice(after(o_proj, seen), *share), order[2])
-
-    attn, mine = attend(queries, keys, values, gates, first_shards, last_shard)
-    theirs = swap_cores(jnp.concatenate(mine, axis=0))
+    share = lax.dynamic_slice(o_proj, (core * HD, 0), (HD, o_proj.shape[1]))
+    attn, mine, theirs, early = attend(queries, keys, values, gates, share, ring_x, early)
     n_rows, width = attn.shape[0] // SIDE, attn.shape[1]
     rows = []
     for far in (0,) + order:
@@ -233,7 +261,7 @@
             piece = ring_y(piece, far)
         piece = piece.astype(jnp.float32)
         total = piece if total is None else total + piece
-    return total.astype(jnp.bfloat16)
+    return total.astype(jnp.bfloat16), early
 
 
 def expert_kernel(n_ff, rows_ref, gate_ref, up_ref, down_ref, out_ref, hidden_ref):
@@ -360,15 +388,14 @@
     w_up,
     w_down,
 ):
-    tok_moe = residual.shape[0]
-    summed = projected(queries, keys, values, gates, o_proj, tok_moe)
+    tok_moe, width = residual.shape
+    n_experts = w_gate.shape[0] * lax.axis_size("seq") * lax.axis_size("exp")
+    cap = 2 * tok_moe * ROUTE_K // n_experts
+    tables = slot_tables(routes, route_weights, n_experts, cap)
+    summed, (place, mix) = projected(queries, keys, values, gates, o_proj, tok_moe, tables)
     residual_sum = residual.astype(jnp.float32) + summed.astype(jnp.float32)
     norm_scale = lax.rsqrt(jnp.mean(residual_sum * residual_sum, axis=-1, keepdims=True) + 1e-06)
     moe_in = (residual_sum * norm_scale * norm_gain).astype(jnp.bfloat16)
-    width = moe_in.shape[1]
-    n_experts = w_gate.shape[0] * lax.axis_size("seq") * lax.axis_size("exp")
-    cap = 2 * tok_moe * ROUTE_K // n_experts
-    place, mix = slot_tables(routes, route_weights, n_experts, cap)
     senders = jnp.dot(place, moe_in, preferred_element_type=jnp.float32).astype(jnp.bfloat16)
     received = lax.all_to_all(
         senders.reshape(n_experts, cap, width),

time: 363 us -> 350 us (0.964)
  waiting for transfers between devices: 144 us -> 48.7 us
  blocking collectives: 98.2 us -> 191 us
  starting transfers between devices: 41.4 us -> 26.7 us
  Pallas kernels: 53.6 us -> 60.6 us
  other arithmetic: 11.9 us -> 8.01 us
    all_to_all x0 -> x1, blocking collectives: none -> 90.6 us  [per_device(): lax.all_to_all(produced.reshape(n_experts, cap, width), ('seq', 'exp'), s...]
    all_to_all x1 -> x0, waiting for transfers between devices: 89.5 us -> none  [per_device(): lax.all_to_all(produced.reshape(n_experts, cap, width), ('seq', 'exp'), s...]
    ppermute x6 -> x3, starting transfers between devices: 21.4 us -> 10.5 us  [attend(): near = [lax.ppermute(kv, 'seq', chip_perm(far)) for far in range(1, SIDE)]]
    pallas_call x2 -> x5, Pallas kernels: 13 us -> 21.4 us  [the longest x2 9.99 us: attend_far(): pl.pallas_call(lambda *refs: far_kernel(*refs[len(extra):]), grid=(1,), i...]
    all_to_all x1 -> x0, starting transfers between devices: 5.91 us -> none  [per_device(): lax.all_to_all(produced.reshape(n_experts, cap, width), ('seq', 'exp'), s...]
    ppermute x6 -> x3, waiting for transfers between devices: 21.6 us -> 18.4 us  [attend(): near = [lax.ppermute(kv, 'seq', chip_perm(far)) for far in range(1, SIDE)]]
  transfers between devices with their start and end apart: 19 -> 16, of which waited for: 12 -> 8; matrix products, arithmetic and copies ran while one was open for 3% -> 3% of each run, Pallas kernels for 4% -> 5%
where the time goes in v4:
time: 350 us; the launch traced here: 348 us
  blocking collectives  191 us (55%)
  Pallas kernels  60.6 us (17%)
  waiting for transfers between devices  48.7 us (14%)
  starting transfers between devices  26.7 us (8%)
  local copies, waits for them, and re-layouts  9.05 us (3%)
  other arithmetic  8.01 us (2%)
    all_to_all x1, blocking collectives, per_device(): lax.all_to_all(senders.reshape(n_experts, cap, width), ('seq', 'exp'), sp...  100 us
    all_to_all x1, blocking collectives, per_device(): lax.all_to_all(produced.reshape(n_experts, cap, width), ('seq', 'exp'), s...  90.6 us
    pallas_call x1, Pallas kernels, expert_rows(): pl.pallas_call(lambda *refs: expert_kernel(n_ff, *refs), grid=(n_ff + n_o...  29.6 us
    ppermute x3, waiting for transfers between devices, ring_y(): return lax.ppermute(array, 'exp', perm)  20 us
    ppermute x3, waiting for transfers between devices, attend(): near = [lax.ppermute(kv, 'seq', chip_perm(far)) for far in range(1, SIDE)]  18.4 us
    ppermute x3, starting transfers between devices, attend(): near = [lax.ppermute(kv, 'seq', chip_perm(far)) for far in range(1, SIDE)]  10.5 us
    ppermute x6, waiting for transfers between devices, ring_x(): return lax.ppermute(array, 'exp', perm)  10.3 us
    pallas_call x2, Pallas kernels, attend_far(): pl.pallas_call(lambda *refs: far_kernel(*refs[len(extra):]), grid=(1,), i...  9.99 us
  transfers between devices with their start and end apart: 16, of which 8 were waited for; matrix products, arithmetic and copies ran while one was open for 3% of the time, Pallas kernels for 5%

profile of v4, /device:TPU:5, one launch (start us, length us, event | category | flops | bytes accessed | tf_op | source)
XLA Modules:
  0.0 347.5 jit_solution(7182490088067446377)
XLA Ops:
  0.7 2.2 constant_dynamic-slice_fusion.7
  4.3 1.3 pad_maximum_fusion.1.kv_ref.refs_0_
  5.6 5.7 %collective-permute-start.2 = (bf16[2,1024,256]{2,1,0:T(8,128)(2,1)S(1)}, bf16[2,1024,256]{2,1,0:T(8,128)(2,1)S(1)}, u32[]{:S(2)}, u32[]{:S(2)}) collective-permute-start(bf16[2,1024,256]{2,1,0:T(8,128)(2,1)S(1)} %pad_maximum_fusion.1.kv_ref.refs_0_), channel_id=1, source_target_pairs={{0,96},{16,112},{1,97},{17,113},{2,98},{18,114},{3,99},{19,115},{4... | collective-permute-start | bytes 3145736 | tf_op jit(solution)/shard_map/ppermute | solution.py:224
  11.4 1.4 collective-permute-start.1
  12.7 3.4 collective-permute-start
  18.7 5.7 %collective-permute-done.4.refs_6_ = bf16[128,3584]{1,0:T(8,128)(2,1)} collective-permute-done((bf16[128,3584]{1,0:T(8,128)(2,1)}, bf16[128,3584]{1,0:T(8,128)(2,1)}, u32[]{:S(2)}, u32[]{:S(2)}) %collective-permute-start.4) | collective-permute-done | bytes 917536 | tf_op jit(solution)/shard_map/ppermute | solution.py:198
  24.4 3.6 %collective-permute-start.5 = (bf16[128,3584]{1,0:T(8,128)(2,1)}, bf16[128,3584]{1,0:T(8,128)(2,1)}, u32[]{:S(2)}, u32[]{:S(2)}) collective-permute-start(bf16[128,3584]{1,0:T(8,128)(2,1)} %constant_dynamic-slice_fusion.7), channel_id=1, source_target_pairs={{0,8},{1,9},{2,10},{3,11},{4,12},{5,13},{6,14},{7,15},{8,0},{9,1},... | collective-permute-start | bytes 2752520 | tf_op jit(solution)/shard_map/ppermute | solution.py:198
  28.0 6.1 %attend_own.1 = (f32[1024,256]{1,0:T(8,128)}, f32[1024,256]{1,0:T(8,128)}, f32[1024,256]{1,0:T(8,128)}) custom-call(bf16[1024,256]{1,0:T(8,128)(2,1)} %refs_2_.2, bf16[2,1024,256]{2,1,0:T(8,128)(2,1)} %copy-done), custom_call_target="tpu_custom_call" | custom-call | flops 2147483648 | bytes 4718592 | tf_op jit(solution)/shard_map/attend_own/pallas_call | solution.py:51
  35.2 2.8 pad_maximum_fusion
  38.0 17.0 %collective-permute-done.2.refs_3_.refs_7_.refs_8_ = bf16[2,1024,256]{2,1,0:T(8,128)(2,1)S(1)} collective-permute-done((bf16[2,1024,256]{2,1,0:T(8,128)(2,1)S(1)}, bf16[2,1024,256]{2,1,0:T(8,128)(2,1)S(1)}, u32[]{:S(2)}, u32[]{:S(2)}) %collective-permute-start.2) | collective-permute-done | bytes 1048608 | tf_op jit(solution)/shard_map/ppermute | solution.py:224
  55.0 1.4 collective-permute-done.refs_1_.refs_5_.refs_6_
  56.4 2.6 choose.2
  59.0 2.2 collective-permute-start.6
  61.2 2.6 choose.3
  65.0 4.9 %attend_far.2.refs_0_ = bf16[1024,256]{1,0:T(8,128)(2,1)} custom-call(s32[2]{0:T(128)} %compare_select_fusion.1.refs_0_.refs_1_, bf16[1024,256]{1,0:T(8,128)(2,1)} %refs_2_.2, f32[1024,256]{1,0:T(8,128)} %get-tuple-element.24.refs_2_.refs_3_, f32[1024,256]{1,0:T(8,128)} %get-tuple-element.25.refs_3_.refs_4_, f32[1024,256]{1,0:T(8,128)} %get-tuple-element.26.refs_4_.refs_5_, ...), custom_call_target="tpu_custom_call" | custom-call | flops 6442450944 | bytes 3145728 | tf_op jit(solution)/shard_map/attend_far/pallas_call | solution.py:104
  71.0 5.1 %attend_far.3 = bf16[1024,256]{1,0:T(8,128)(2,1)} custom-call(bf16[1024,256]{1,0:T(8,128)(2,1)} %attend_far.2.refs_0_, s32[2]{0:T(128)} %compare_select_fusion.1.refs_0_.refs_1_, bf16[1024,256]{1,0:T(8,128)(2,1)} %refs_2_.2, f32[1024,256]{1,0:T(8,128)} %get-tuple-element.24.refs_2_.refs_3_, ...), custom_call_target="tpu_custom_call", output_to_operand_aliasing={{}: (0, {})} | custom-call | flops 6442450944 | bytes 3145728 | tf_op jit(solution)/shard_map/attend_far/pallas_call | solution.py:104
  76.1 1.8 constant_dynamic-slice_fusion.3
  79.1 2.1 collective-permute-start.9
  81.2 3.0 collective-permute-done.10.refs_3_
  84.3 1.5 collective-permute-done.8.refs_1_
  86.5 6.9 %project.1 = bf16[256,3584]{1,0:T(8,128)(2,1)} custom-call(s32[1]{0:T(128)} %bitcast.core_ref, bf16[256,256]{1,0:T(8,128)(2,1)} %get-tuple-element.52.refs_0_, bf16[256,256]{1,0:T(8,128)(2,1)} %copy-done.14, bf16[256,256]{1,0:T(8,128)(2,1)} %copy-done.13, bf16[256,256]{1,0:T(8,128)(2,1)} %copy-done.12, bf16[256,3584]{1,0:T(8,128)(2,1)} %refs_4_.1, ...), custom_call_target="tpu_custom_call" | custom-call | flops 4227858432 | bytes 7733248 | tf_op jit(solution)/shard_map/project/pallas_call | solution.py:170
  93.4 2.2 constant_dynamic-slice_fusion.2
  95.5 1.3 collective-permute-start.13
  96.8 2.6 collective-permute-start.15
  100.5 9.0 %collective-permute-done.13 = bf16[64,3584]{1,0:T(8,128)(2,1)S(1)} collective-permute-done((bf16[64,3584]{1,0:T(8,128)(2,1)}, bf16[64,3584]{1,0:T(8,128)(2,1)S(1)}, u32[]{:S(2)}, u32[]{:S(2)}) %collective-permute-start.13) | collective-permute-done | bytes 458784 | tf_op jit(solution)/shard_map/ppermute | solution.py:203
  109.5 11.0 %collective-permute-done.15 = bf16[64,3584]{1,0:T(8,128)(2,1)S(1)} collective-permute-done((bf16[64,3584]{1,0:T(8,128)(2,1)S(1)}, bf16[64,3584]{1,0:T(8,128)(2,1)S(1)}, u32[]{:S(2)}, u32[]{:S(2)}) %collective-permute-start.15) | collective-permute-done | bytes 458784 | tf_op jit(solution)/shard_map/ppermute | solution.py:203
  120.5 1.5 multiply_reduce_fusion
  122.1 2.1 fusion
  124.2 100.3 %all_to_all.10 = bf16[128,8,3584]{2,1,0:T(8,128)(2,1)S(1)} all-to-all(bf16[128,8,3584]{2,1,0:T(8,128)(2,1)S(1)} %fusion), channel_id=1, replica_groups=mesh['seq'=8,'exp'=16] {'seq','exp'}, dimensions={0} | all-to-all | bytes 14680064 | tf_op jit(solution)/shard_map/all_to_all | solution.py:400
  224.6 29.6 %experts.1 = bf16[1024,3584]{1,0:T(8,128)(2,1)} custom-call(bf16[1024,3584]{1,0:T(8,128)(2,1)S(1)} %bitcast.44, bf16[1,3584,1024]{2,1,0:T(8,128)(2,1)S(1)} %bitcast.46, bf16[1,3584,1024]{2,1,0:T(8,128)(2,1)S(1)} %bitcast.48, bf16[1,1024,3584]{2,1,0:T(8,128)(2,1)} %refs_3_.1), custom_call_target="tpu_custom_call" | custom-call | flops 22548578304 | bytes 36700160 | tf_op jit(solution)/shard_map/experts/pallas_call | solution.py:299
  254.2 90.6 %all_to_all.11 = bf16[128,8,3584]{2,1,0:T(8,128)(2,1)S(1)} all-to-all(bf16[128,8,3584]{2,1,0:T(8,128)(2,1)} %bitcast.49), channel_id=1, replica_groups=mesh['seq'=8,'exp'=16] {'seq','exp'}, dimensions={0} | all-to-all | bytes 14680064 | tf_op jit(solution)/shard_map/all_to_all | solution.py:408
  344.8 2.7 combine.1
  (71 shorter events, 10.5 us)
Async XLA Ops:
  0.6 15.6 %copy-start.8 = (s32[64,8]{0,1:T(8,128)S(1)}, s32[64,8]{0,1:T(8,128)}, u32[]{:S(2)}) copy-start(s32[64,8]{0,1:T(8,128)} %param.19) | copy-start | bytes 6148
  0.6 15.6 %copy-start.9 = (f32[64,8]{0,1:T(8,128)S(1)}, f32[64,8]{0,1:T(8,128)}, u32[]{:S(2)}) copy-start(f32[64,8]{0,1:T(8,128)} %param.20) | copy-start | bytes 6148
  0.7 15.6 %copy-start.10 = (s32[8,3]{0,1:T(4,128)S(1)}, s32[8,3]{0,1:T(4,128)}, u32[]{:S(2)}) copy-start(s32[8,3]{0,1:T(4,128)} %param.15) | copy-start | bytes 292
  2.9 21.5 %collective-permute-start.4 = (bf16[128,3584]{1,0:T(8,128)(2,1)}, bf16[128,3584]{1,0:T(8,128)(2,1)}, u32[]{:S(2)}, u32[]{:S(2)}) collective-permute-start(bf16[128,3584]{1,0:T(8,128)(2,1)} %constant_dynamic-slice_fusion.7), channel_id=1, source_target_pairs={{0,12},{1,13},{2,14},{3,15},{4,0},{5,1},{6,2},{7,3},{8,4},{9,5},{1... | collective-permute-start | bytes 2752520 | tf_op jit(solution)/shard_map/ppermute | solution.py:198
  3.1 21.3 %collective-permute-start.3 = (bf16[128,3584]{1,0:T(8,128)(2,1)}, bf16[128,3584]{1,0:T(8,128)(2,1)}, u32[]{:S(2)}, u32[]{:S(2)}) collective-permute-start(bf16[128,3584]{1,0:T(8,128)(2,1)} %constant_dynamic-slice_fusion.7), channel_id=1, source_target_pairs={{0,4},{1,5},{2,6},{3,7},{4,8},{5,9},{6,10},{7,11},{8,12},{9,13},{1... | collective-permute-start | bytes 2752520 | tf_op jit(solution)/shard_map/ppermute | solution.py:198
  5.6 22.4 %copy-start = (bf16[2,1024,256]{2,1,0:T(8,128)(2,1)}, bf16[2,1024,256]{2,1,0:T(8,128)(2,1)S(1)}, u32[]{:S(2)}) copy-start(bf16[2,1024,256]{2,1,0:T(8,128)(2,1)S(1)} %pad_maximum_fusion.1.kv_ref.refs_0_) | copy-start | bytes 3145732
  5.6 49.3 %collective-permute-start.2 = (bf16[2,1024,256]{2,1,0:T(8,128)(2,1)S(1)}, bf16[2,1024,256]{2,1,0:T(8,128)(2,1)S(1)}, u32[]{:S(2)}, u32[]{:S(2)}) collective-permute-start(bf16[2,1024,256]{2,1,0:T(8,128)(2,1)S(1)} %pad_maximum_fusion.1.kv_ref.refs_0_), channel_id=1, source_target_pairs={{0,96},{16,112},{1,97},{17,113},{2,98},{18,114},{3,99},{19,115},{4... | collective-permute-start | bytes 3145736 | tf_op jit(solution)/shard_map/ppermute | solution.py:224
  11.4 43.6 %collective-permute-start.1 = (bf16[2,1024,256]{2,1,0:T(8,128)(2,1)S(1)}, bf16[2,1024,256]{2,1,0:T(8,128)(2,1)S(1)}, u32[]{:S(2)}, u32[]{:S(2)}) collective-permute-start(bf16[2,1024,256]{2,1,0:T(8,128)(2,1)S(1)} %pad_maximum_fusion.1.kv_ref.refs_0_), channel_id=1, source_target_pairs={{0,64},{16,80},{32,96},{48,112},{1,65},{17,81},{33,97},{49,113},{2... | collective-permute-start | bytes 3145736 | tf_op jit(solution)/shard_map/ppermute | solution.py:224
  12.7 43.6 %collective-permute-start = (bf16[2,1024,256]{2,1,0:T(8,128)(2,1)S(1)}, bf16[2,1024,256]{2,1,0:T(8,128)(2,1)}, u32[]{:S(2)}, u32[]{:S(2)}) collective-permute-start(bf16[2,1024,256]{2,1,0:T(8,128)(2,1)S(1)} %pad_maximum_fusion.1.kv_ref.refs_0_), channel_id=1, source_target_pairs={{0,32},{16,48},{32,64},{48,80},{64,96},{80,112},{1,33},{17,49},{33... | collective-permute-start | bytes 3145736 | tf_op jit(solution)/shard_map/ppermute | solution.py:224
  24.4 32.0 %collective-permute-start.5 = (bf16[128,3584]{1,0:T(8,128)(2,1)}, bf16[128,3584]{1,0:T(8,128)(2,1)}, u32[]{:S(2)}, u32[]{:S(2)}) collective-permute-start(bf16[128,3584]{1,0:T(8,128)(2,1)} %constant_dynamic-slice_fusion.7), channel_id=1, source_target_pairs={{0,8},{1,9},{2,10},{3,11},{4,12},{5,13},{6,14},{7,15},{8,0},{9,1},... | collective-permute-start | bytes 2752520 | tf_op jit(solution)/shard_map/ppermute | solution.py:198
  55.0 1.4 copy-start.1
  55.0 1.4 copy-start.2
  59.0 4.9 %copy-start.4 = (bf16[256,3584]{1,0:T(8,128)(2,1)S(1)}, bf16[256,3584]{1,0:T(8,128)(2,1)}, u32[]{:S(2)}) copy-start(bf16[256,3584]{1,0:T(8,128)(2,1)} %pad_maximum_fusion) | copy-start | bytes 5505028
  59.0 6.0 %collective-permute-start.6 = (bf16[2,2,1024,128]{3,2,1,0:T(8,128)(2,1)}, bf16[2,2,1024,128]{3,2,1,0:T(8,128)(2,1)}, u32[]{:S(2)}, u32[]{:S(2)}) collective-permute-start(bf16[2,2,1024,128]{3,2,1,0:T(8,128)(2,1)} %choose.2), channel_id=1, source_target_pairs={{0,16},{16,0},{32,48},{48,32},{64,80},{80,64},{96,112},{112,96},{1... | collective-permute-start | bytes 3145736 | tf_op jit(solution)/shard_map/ppermute | solution.py:208
  63.8 6.1 %collective-permute-start.7 = (bf16[2,2,1024,128]{3,2,1,0:T(8,128)(2,1)}, bf16[2,2,1024,128]{3,2,1,0:T(8,128)(2,1)S(1)}, u32[]{:S(2)}, u32[]{:S(2)}) collective-permute-start(bf16[2,2,1024,128]{3,2,1,0:T(8,128)(2,1)} %choose.3), channel_id=1, source_target_pairs={{0,16},{16,0},{32,48},{48,32},{64,80},{80,64},{96,112},{112,96},{1... | collective-permute-start | bytes 3145736 | tf_op jit(solution)/shard_map/ppermute | solution.py:208
  64.0 21.9 %collective-permute-start.11 = (bf16[256,3584]{1,0:T(8,128)(2,1)S(1)}, bf16[256,3584]{1,0:T(8,128)(2,1)}, u32[]{:S(2)}, u32[]{:S(2)}) collective-permute-start(bf16[256,3584]{1,0:T(8,128)(2,1)S(1)} %copy-done.4), channel_id=1, source_target_pairs={{0,16},{16,0},{32,48},{48,32},{64,80},{80,64},{96,112},{112,96},{1... | collective-permute-start | bytes 5505032 | tf_op jit(solution)/shard_map/ppermute | solution.py:208
  64.9 16.3 %collective-permute-start.12 = (bf16[128,3584]{1,0:T(8,128)(2,1)}, bf16[128,3584]{1,0:T(8,128)(2,1)}, u32[]{:S(2)}, u32[]{:S(2)}) collective-permute-start(bf16[128,3584]{1,0:T(8,128)(2,1)} %collective-permute-done.5.refs_7_), channel_id=1, source_target_pairs={{0,16},{16,0},{32,48},{48,32},{64,80},{80,64},{96,112},{112,96},{1... | collective-permute-start | bytes 2752520 | tf_op jit(solution)/shard_map/ppermute | solution.py:208
  77.9 6.3 %collective-permute-start.10 = (bf16[256,256]{1,0:T(8,128)(2,1)S(1)}, bf16[256,256]{1,0:T(8,128)(2,1)S(1)}, u32[]{:S(2)}, u32[]{:S(2)}) collective-permute-start(bf16[256,256]{1,0:T(8,128)(2,1)S(1)} %get-tuple-element.49), channel_id=1, source_target_pairs={{0,8},{1,9},{2,10},{3,11},{4,12},{5,13},{6,14},{7,15},{8,0},{9,1},... | collective-permute-start | bytes 393224 | tf_op jit(solution)/shard_map/ppermute | solution.py:198
  79.1 5.2 %collective-permute-start.9 = (bf16[256,256]{1,0:T(8,128)(2,1)S(1)}, bf16[256,256]{1,0:T(8,128)(2,1)S(1)}, u32[]{:S(2)}, u32[]{:S(2)}) collective-permute-start(bf16[256,256]{1,0:T(8,128)(2,1)S(1)} %get-tuple-element.50), channel_id=1, source_target_pairs={{0,12},{1,13},{2,14},{3,15},{4,0},{5,1},{6,2},{7,3},{8,4},{9,5},{1... | collective-permute-start | bytes 393224 | tf_op jit(solution)/shard_map/ppermute | solution.py:198
  81.2 4.7 %collective-permute-start.8 = (bf16[256,256]{1,0:T(8,128)(2,1)S(1)}, bf16[256,256]{1,0:T(8,128)(2,1)S(1)}, u32[]{:S(2)}, u32[]{:S(2)}) collective-permute-start(bf16[256,256]{1,0:T(8,128)(2,1)S(1)} %get-tuple-element.51), channel_id=1, source_target_pairs={{0,4},{1,5},{2,6},{3,7},{4,8},{5,9},{6,10},{7,11},{8,12},{9,13},{1... | collective-permute-start | bytes 393224 | tf_op jit(solution)/shard_map/ppermute | solution.py:198
  84.1 1.7 copy-start.12
  84.3 1.6 copy-start.13
  86.5 34.0 %copy-start.5 = (bf16[64,3584]{1,0:T(8,128)(2,1)S(1)}, bf16[64,3584]{1,0:T(8,128)(2,1)}, u32[]{:S(2)}) copy-start(bf16[64,3584]{1,0:T(8,128)(2,1)} %param.17) | copy-start | bytes 1376260
  93.4 28.6 %copy-start.7 = (f32[3584]{0:T(1024)S(1)}, f32[3584]{0:T(1024)}, u32[]{:S(2)}) copy-start(f32[3584]{0:T(1024)} %param.18) | copy-start | bytes 43012
  95.5 14.0 %collective-permute-start.13 = (bf16[64,3584]{1,0:T(8,128)(2,1)}, bf16[64,3584]{1,0:T(8,128)(2,1)S(1)}, u32[]{:S(2)}, u32[]{:S(2)}) collective-permute-start(bf16[64,3584]{1,0:T(8,128)(2,1)} %get-tuple-element.46), channel_id=1, source_target_pairs={{0,1},{1,2},{2,3},{3,0},{4,5},{5,6},{6,7},{7,4},{8,9},{9,10},{10,1... | collective-permute-start | bytes 1376264 | tf_op jit(solution)/shard_map/ppermute | solution.py:203
  96.8 23.7 %collective-permute-start.15 = (bf16[64,3584]{1,0:T(8,128)(2,1)S(1)}, bf16[64,3584]{1,0:T(8,128)(2,1)S(1)}, u32[]{:S(2)}, u32[]{:S(2)}) collective-permute-start(bf16[64,3584]{1,0:T(8,128)(2,1)S(1)} %get-tuple-element.47), channel_id=1, source_target_pairs={{0,2},{1,3},{2,0},{3,1},{4,6},{5,7},{6,4},{7,5},{8,10},{9,11},{10,... | collective-permute-start | bytes 1376264 | tf_op jit(solution)/shard_map/ppermute | solution.py:203
  99.5 21.1 %collective-permute-start.14 = (bf16[64,3584]{1,0:T(8,128)(2,1)S(1)}, bf16[64,3584]{1,0:T(8,128)(2,1)S(1)}, u32[]{:S(2)}, u32[]{:S(2)}) collective-permute-start(bf16[64,3584]{1,0:T(8,128)(2,1)S(1)} %get-tuple-element.48), channel_id=1, source_target_pairs={{0,3},{1,0},{2,1},{3,2},{4,7},{5,4},{6,5},{7,6},{8,11},{9,8},{10,9... | collective-permute-start | bytes 1376264 | tf_op jit(solution)/shard_map/ppermute | solution.py:203
  122.0 2.2 copy-start.6
  122.0 102.5 %slice-start = ((s8[7340032]{0:T(1024)(128)(4,1)}), s8[4194304]{0:T(1024)(128)(4,1)S(1)}, s32[]{:S(2)}) async-start(s8[7340032]{0:T(1024)(128)(4,1)} %bitcast.45), calls=%async_computation.2 | async-start | bytes 8388608
  122.0 102.5 %slice-start.2 = ((s8[7340032]{0:T(1024)(128)(4,1)}), s8[4194304]{0:T(1024)(128)(4,1)S(1)}, s32[]{:S(2)}) async-start(s8[7340032]{0:T(1024)(128)(4,1)} %bitcast.47), calls=%async_computation.4 | async-start | bytes 8388608
  124.2 100.3 %slice-start.1 = ((s8[7340032]{0:T(1024)(128)(4,1)}), s8[3145728]{0:T(1024)(128)(4,1)S(1)}, s32[]{:S(2)}) async-start(s8[7340032]{0:T(1024)(128)(4,1)} %bitcast.45), calls=%async_computation.3 | async-start | bytes 6291456
  124.2 100.3 %slice-start.3 = ((s8[7340032]{0:T(1024)(128)(4,1)}), s8[3145728]{0:T(1024)(128)(4,1)S(1)}, s32[]{:S(2)}) async-start(s8[7340032]{0:T(1024)(128)(4,1)} %bitcast.47), calls=%async_computation.5 | async-start | bytes 6291456
  (3 other events, 2.6 us)

commit v5 on v4

--- a/solution.py
+++ b/solution.py
@@ -17,6 +17,7 @@
 Q_TILE = 128
 CORES = 2
 SIDE = 4
+ORDER = (1, 3, 2)
 
 
 def dot_t(a, b):
@@ -63,7 +64,7 @@
 
 
 def far_kernel(code_ref, q_ref, top_ref, sum_ref, acc_ref, *refs):
-    near, swapped, out_ref = refs[:-6], refs[-6], refs[-5]
+    near, swapped, outs = refs[: SIDE - 1], refs[SIDE - 1], refs[SIDE : 2 * SIDE]
     held, tops, sums, accs = refs[-4:]
     tops[...] = top_ref[...]
     sums[...] = sum_ref[...]
@@ -94,13 +95,17 @@
                 sums[at, :] = sums[at, :] * fade + amount
                 accs[at, :] = accs[at, :] * fade + acc
 
-    out_ref[...] = (accs[...] / sums[...]).astype(jnp.bfloat16)
+    n_rows = outs[0].shape[0]
+    for far, out_ref in zip((0, *ORDER), outs):
+        start = (code_ref[swapped.shape[0]] + far) % SIDE * n_rows
+        at = pl.ds(pl.multiple_of(start, n_rows), n_rows)
+        out_ref[...] = (accs[at, :] / sums[at, :]).astype(jnp.bfloat16)
 
 
 def attend_far(codes, queries, state, near, swapped, head, before):
-    n = queries.shape[0]
+    n, width = queries.shape
     spec = pl.BlockSpec((n, HD), lambda i: (0, head))
-    extra = [] if before is None else [before]
+    extra = [] if before is None else before
     return pl.pallas_call(
         lambda *refs: far_kernel(*refs[len(extra) :]),
         grid=(1,),
@@ -109,9 +114,9 @@
         + [spec] * 4
         + [pl.BlockSpec((2, n, HD), lambda i: (0, 0, head))] * len(near)
         + [pl.BlockSpec(swapped.shape, lambda i: (0, 0, 0, 0))],
-        out_specs=spec,
-        out_shape=jax.ShapeDtypeStruct(queries.shape, jnp.bfloat16),
-        input_output_aliases={0: 0} if extra else {},
+        out_specs=[pl.BlockSpec((n // SIDE, HD), lambda i: (0, head))] * SIDE,
+        out_shape=[jax.ShapeDtypeStruct((n // SIDE, width), jnp.bfloat16)] * SIDE,
+        input_output_aliases={i: i for i in range(len(extra))},
         scratch_shapes=[pltpu.VMEM((2, n, HD), jnp.bfloat16)]
         + [pltpu.VMEM((n, HD), jnp.float32)] * 3,
         compiler_params=pltpu.CompilerParams(vmem_limit_bytes=60 * 1024 * 1024),
@@ -148,9 +153,10 @@
     )(fars, *blocks)
 
 
-def project_kernel(core_ref, *refs):
-    rows, own, mine, theirs, out_ref = refs[:4], refs[4], refs[5:8], refs[8:11], refs[11]
-    core = core_ref[0]
+def project_kernel(spot_ref, *refs):
+    rows, own, mine, theirs = refs[:4], refs[4], refs[5:8], refs[8:11]
+    outs, held = refs[11:15], refs[15]
+    core = spot_ref[0]
     first = pl.ds(pl.multiple_of(core * HD, HD), HD)
     second = pl.ds(pl.multiple_of((1 - core) * HD, HD), HD)
     total = jnp.dot(rows[0][...], own[...], preferred_element_type=jnp.float32)
@@ -160,10 +166,15 @@
             jnp.concatenate([left[...], right[...]], axis=0),
             preferred_element_type=jnp.float32,
         )
-    out_ref[...] = total.astype(jnp.bfloat16)
-
-
-def project(core, rows, own, mine, theirs):
+    held[...] = total
+    n_rows = outs[0].shape[0]
+    for far, out_ref in zip((0, *ORDER), outs):
+        start = (spot_ref[1] + far) % SIDE * n_rows
+        at = pl.ds(pl.multiple_of(start, n_rows), n_rows)
+        out_ref[...] = held[at, :].astype(jnp.bfloat16)
+
+
+def project(spot, rows, own, mine, theirs):
     n = len(mine)
     n_rows, depth = rows[0].shape
     width, tile = own.shape[1], 896
@@ -175,8 +186,9 @@
         + [pl.BlockSpec((depth, tile), lambda i: (0, i))]
         + [pl.BlockSpec((HD, tile), lambda i: (0, i))] * n
         + [pl.BlockSpec((HD, tile), lambda i, k=k: (k, i)) for k in (0, 1, 0)],
-        out_specs=pl.BlockSpec((n_rows, tile), lambda i: (0, i)),
-        out_shape=jax.ShapeDtypeStruct((n_rows, width), jnp.bfloat16),
+        out_specs=[pl.BlockSpec((n_rows // SIDE, tile), lambda i: (0, i))] * SIDE,
+        out_shape=[jax.ShapeDtypeStruct((n_rows // SIDE, width), jnp.bfloat16)] * SIDE,
+        scratch_shapes=[pltpu.VMEM((n_rows, tile), jnp.float32)],
         compiler_params=pltpu.CompilerParams(vmem_limit_bytes=60 * 1024 * 1024),
         cost_estimate=pl.CostEstimate(
             flops=6 * n * n_rows * depth * width,
@@ -184,7 +196,7 @@
             transcendentals=0,
         ),
         name="project",
-    )(core, *rows, own, *mine, theirs[0], theirs[0], theirs[1])
+    )(spot, *rows, own, *mine, theirs[0], theirs[0], theirs[1])
 
 
 def chip_perm(far):
@@ -218,7 +230,8 @@
     wanted = gates[me, 1:]
     codes = jnp.where(
         wanted == me, 0, jnp.where(wanted % CORES == core, chip - wanted // CORES, SIDE)
-    ).astype(jnp.int32)
+    )
+    codes = jnp.append(codes, lax.axis_index("exp") // SIDE).astype(jnp.int32)
     partner_far = jnp.clip(chip - gates[me ^ 1, 1:] // CORES, 0, SIDE - 1).astype(jnp.int32)
     kv = jnp.stack([keys, values])
     near = [lax.ppermute(kv, "seq", chip_perm(far)) for far in range(1, SIDE)]
@@ -239,28 +252,16 @@
     return attn, mine, theirs, early
 
 
-def projected(queries, keys, values, gates, o_proj, tok_moe, early):
-    at = lax.axis_index("exp")
-    x, y = at // SIDE, at % SIDE
-    order = (1, 3, 2)
-
+def projected(queries, keys, values, gates, o_proj, early):
     core = lax.axis_index("seq") % CORES
     share = lax.dynamic_slice(o_proj, (core * HD, 0), (HD, o_proj.shape[1]))
-    attn, mine, theirs, early = attend(queries, keys, values, gates, share, ring_x, early)
-    n_rows, width = attn.shape[0] // SIDE, attn.shape[1]
-    rows = []
-    for far in (0,) + order:
-        piece = lax.dynamic_slice(attn, ((x + far) % SIDE * n_rows, 0), (n_rows, width))
-        rows.append(ring_x(piece, far) if far else piece)
-    partial = project(core.reshape(1), rows, o_proj, mine, theirs)
-    total = None
-    for far in (0,) + order:
-        start = (y + far) % SIDE * tok_moe
-        piece = lax.dynamic_slice(partial, (start, 0), (tok_moe, partial.shape[1]))
-        if far:
-            piece = ring_y(piece, far)
-        piece = piece.astype(jnp.float32)
-        total = piece if total is None else total + piece
+    pieces, mine, theirs, early = attend(queries, keys, values, gates, share, ring_x, early)
+    rows = [pieces[0]] + [ring_x(piece, far) for piece, far in zip(pieces[1:], ORDER)]
+    spot = jnp.stack([core, lax.axis_index("exp") % SIDE]).astype(jnp.int32)
+    sums = project(spot, rows, o_proj, mine, theirs)
+    total = sums[0].astype(jnp.float32)
+    for piece, far in zip(sums[1:], ORDER):
+        total = total + ring_y(piece, far).astype(jnp.float32)
     return total.astype(jnp.bfloat16), early
 
 
@@ -392,7 +393,7 @@
     n_experts = w_gate.shape[0] * lax.axis_size("seq") * lax.axis_size("exp")
     cap = 2 * tok_moe * ROUTE_K // n_experts
     tables = slot_tables(routes, route_weights, n_experts, cap)
-    summed, (place, mix) = projected(queries, keys, values, gates, o_proj, tok_moe, tables)
+    summed, (place, mix) = projected(queries, keys, values, gates, o_proj, tables)
     residual_sum = residual.astype(jnp.float32) + summed.astype(jnp.float32)
     norm_scale = lax.rsqrt(jnp.mean(residual_sum * residual_sum, axis=-1, keepdims=True) + 1e-06)
     moe_in = (residual_sum * norm_scale * norm_gain).astype(jnp.bfloat16)

time: 350 us -> 345 us (0.986)
  local copies, waits for them, and re-layouts: 9.05 us -> 5.1 us
    dynamic_slice x2 -> x0, local copies, waits for them, and re-layouts: 3.94 us -> none  [the longest x1 2.16 us: projected(): piece = lax.dynamic_slice(partial, (start, 0), (tok_moe, partial.shape[1]))]
  transfers between devices with their start and end apart: 16 -> 16, of which waited for: 8 -> 9; matrix products, arithmetic and copies ran while one was open for 3% -> 2% of each run, Pallas kernels for 5% -> 5%
where the time goes in v5:
time: 345 us; the launch traced here: 342 us
  blocking collectives  189 us (55%)
  Pallas kernels  60.5 us (18%)
  waiting for transfers between devices  48.5 us (14%)
  starting transfers between devices  26.8 us (8%)
  other arithmetic  8.71 us (3%)
  local copies, waits for them, and re-layouts  5.1 us (1%)
    all_to_all x1, blocking collectives, per_device(): lax.all_to_all(senders.reshape(n_experts, cap, width), ('seq', 'exp'), sp...  98.1 us
    all_to_all x1, blocking collectives, per_device(): lax.all_to_all(produced.reshape(n_experts, cap, width), ('seq', 'exp'), s...  90.6 us
    pallas_call x1, Pallas kernels, expert_rows(): pl.pallas_call(lambda *refs: expert_kernel(n_ff, *refs), grid=(n_ff + n_o...  29.7 us
    ppermute x3, waiting for transfers between devices, ring_y(): return lax.ppermute(array, 'exp', perm)  20.1 us
    ppermute x3, waiting for transfers between devices, attend(): near = [lax.ppermute(kv, 'seq', chip_perm(far)) for far in range(1, SIDE)]  18.4 us
    ppermute x3, starting transfers between devices, attend(): near = [lax.ppermute(kv, 'seq', chip_perm(far)) for far in range(1, SIDE)]  10.5 us
    pallas_call x2, Pallas kernels, attend_far(): pl.pallas_call(lambda *refs: far_kernel(*refs[len(extra):]), grid=(1,), i...  9.89 us
    ppermute x6, waiting for transfers between devices, ring_x(): return lax.ppermute(array, 'exp', perm)  9.62 us
  transfers between devices with their start and end apart: 16, of which 9 were waited for; matrix products, arithmetic and copies ran while one was open for 2% of the time, Pallas kernels for 5%

profile of v5, /device:TPU:5, one launch (start us, length us, event | category | flops | bytes accessed | tf_op | source)
XLA Modules:
  0.0 341.9 jit_solution(13472149689752850665)
XLA Ops:
  0.7 2.2 constant_dynamic-slice_fusion
  3.1 1.2 collective-permute-start.3
  4.3 1.3 pad_maximum_fusion.1.kv_ref.refs_0_
  5.6 5.7 %collective-permute-start.2 = (bf16[2,1024,256]{2,1,0:T(8,128)(2,1)S(1)}, bf16[2,1024,256]{2,1,0:T(8,128)(2,1)S(1)}, u32[]{:S(2)}, u32[]{:S(2)}) collective-permute-start(bf16[2,1024,256]{2,1,0:T(8,128)(2,1)S(1)} %pad_maximum_fusion.1.kv_ref.refs_0_), channel_id=1, source_target_pairs={{0,96},{16,112},{1,97},{17,113},{2,98},{18,114},{3,99},{19,115},{4... | collective-permute-start | bytes 3145736 | tf_op jit(solution)/shard_map/ppermute | solution.py:237
  11.4 1.4 collective-permute-start.1
  12.7 3.4 collective-permute-start
  18.7 5.7 %collective-permute-done.4.refs_6_ = bf16[128,3584]{1,0:T(8,128)(2,1)} collective-permute-done((bf16[128,3584]{1,0:T(8,128)(2,1)}, bf16[128,3584]{1,0:T(8,128)(2,1)}, u32[]{:S(2)}, u32[]{:S(2)}) %collective-permute-start.4) | collective-permute-done | bytes 917536 | tf_op jit(solution)/shard_map/ppermute | solution.py:210
  24.4 3.6 %collective-permute-start.5 = (bf16[128,3584]{1,0:T(8,128)(2,1)}, bf16[128,3584]{1,0:T(8,128)(2,1)}, u32[]{:S(2)}, u32[]{:S(2)}) collective-permute-start(bf16[128,3584]{1,0:T(8,128)(2,1)} %constant_dynamic-slice_fusion), channel_id=1, source_target_pairs={{0,8},{1,9},{2,10},{3,11},{4,12},{5,13},{6,14},{7,15},{8,0},{9,1},... | collective-permute-start | bytes 2752520 | tf_op jit(solution)/shard_map/ppermute | solution.py:210
  28.0 6.1 %attend_own.1 = (f32[1024,256]{1,0:T(8,128)}, f32[1024,256]{1,0:T(8,128)}, f32[1024,256]{1,0:T(8,128)}) custom-call(bf16[1024,256]{1,0:T(8,128)(2,1)} %refs_5_.1, bf16[2,1024,256]{2,1,0:T(8,128)(2,1)} %copy-done), custom_call_target="tpu_custom_call" | custom-call | flops 2147483648 | bytes 4718592 | tf_op jit(solution)/shard_map/attend_own/pallas_call | solution.py:52
  35.2 2.8 pad_maximum_fusion
  38.0 17.0 %collective-permute-done.2.refs_3_.refs_7_.refs_11_ = bf16[2,1024,256]{2,1,0:T(8,128)(2,1)S(1)} collective-permute-done((bf16[2,1024,256]{2,1,0:T(8,128)(2,1)S(1)}, bf16[2,1024,256]{2,1,0:T(8,128)(2,1)S(1)}, u32[]{:S(2)}, u32[]{:S(2)}) %collective-permute-start.2) | collective-permute-done | bytes 1048608 | tf_op jit(solution)/shard_map/ppermute | solution.py:237
  55.0 1.4 collective-permute-done.refs_1_.refs_5_.refs_9_
  56.4 2.6 choose.2
  59.0 2.2 collective-permute-start.6
  61.2 2.6 choose.3
  65.2 4.8 %attend_far.2 = (bf16[256,256]{1,0:T(8,128)(2,1)}, bf16[256,256]{1,0:T(8,128)(2,1)}, bf16[256,256]{1,0:T(8,128)(2,1)}, bf16[256,256]{1,0:T(8,128)(2,1)}) custom-call(s32[3]{0:T(128)} %pad_add_fusion.1.refs_0_.refs_4_, bf16[1024,256]{1,0:T(8,128)(2,1)} %refs_5_.1, f32[1024,256]{1,0:T(8,128)} %get-tuple-element.36.refs_2_.refs_6_, ...), custom_call_target="tpu_custom_call" | custom-call | flops 6442450944 | bytes 3145728 | tf_op jit(solution)/shard_map/attend_far/pallas_call | solution.py:109
  71.5 5.1 %attend_far.3 = (bf16[256,256]{1,0:T(8,128)(2,1)}, bf16[256,256]{1,0:T(8,128)(2,1)}, bf16[256,256]{1,0:T(8,128)(2,1)}, bf16[256,256]{1,0:T(8,128)(2,1)}) custom-call(bf16[256,256]{1,0:T(8,128)(2,1)} %get-tuple-element.42.refs_0_, ...), custom_call_target="tpu_custom_call", output_to_operand_aliasing={{0}: (0, {}), {1}: (1, {}), {2}: (2, {}), {3}: (3, {})} | custom-call | flops 6442450944 | bytes 3145728 | tf_op jit(solution)/shard_map/attend_far/pallas_call | solution.py:109
  76.5 2.1 collective-permute-start.8
  78.7 1.8 collective-permute-start.10
  81.8 2.5 collective-permute-done.9.refs_2_
  85.7 6.9 %project.1 = (bf16[64,3584]{1,0:T(8,128)(2,1)}, bf16[64,3584]{1,0:T(8,128)(2,1)}, bf16[64,3584]{1,0:T(8,128)(2,1)}, bf16[64,3584]{1,0:T(8,128)(2,1)}) custom-call(s32[2]{0:T(128)} %pad_add_fusion.spot_ref, bf16[256,256]{1,0:T(8,128)(2,1)} %get-tuple-element.46.refs_0_, bf16[256,256]{1,0:T(8,128)(2,1)} %copy-done.12, bf16[256,256]{1,0:T(8,128)(2,1)} %copy-done.13, ...), custom_call_target="tpu_custom_call" | custom-call | flops 4227858432 | bytes 7733248 | tf_op jit(solution)/shard_map/project/pallas_call | solution.py:181
  92.6 1.4 collective-permute-start.13
  94.0 1.5 collective-permute-start.14
  95.5 1.6 collective-permute-start.15
  97.0 9.1 %collective-permute-done.13 = bf16[64,3584]{1,0:T(8,128)(2,1)S(1)} collective-permute-done((bf16[64,3584]{1,0:T(8,128)(2,1)}, bf16[64,3584]{1,0:T(8,128)(2,1)S(1)}, u32[]{:S(2)}, u32[]{:S(2)}) %collective-permute-start.13) | collective-permute-done | bytes 458784 | tf_op jit(solution)/shard_map/ppermute | solution.py:215
  106.2 10.9 %collective-permute-done.15 = bf16[64,3584]{1,0:T(8,128)(2,1)S(1)} collective-permute-done((bf16[64,3584]{1,0:T(8,128)(2,1)}, bf16[64,3584]{1,0:T(8,128)(2,1)S(1)}, u32[]{:S(2)}, u32[]{:S(2)}) %collective-permute-start.15) | collective-permute-done | bytes 458784 | tf_op jit(solution)/shard_map/ppermute | solution.py:215
  117.1 1.5 multiply_reduce_fusion
  118.6 2.1 fusion
  120.8 98.1 %all_to_all.10 = bf16[128,8,3584]{2,1,0:T(8,128)(2,1)S(1)} all-to-all(bf16[128,8,3584]{2,1,0:T(8,128)(2,1)S(1)} %fusion), channel_id=1, replica_groups=mesh['seq'=8,'exp'=16] {'seq','exp'}, dimensions={0} | all-to-all | bytes 14680064 | tf_op jit(solution)/shard_map/all_to_all | solution.py:401
  219.0 29.7 %experts.1 = bf16[1024,3584]{1,0:T(8,128)(2,1)} custom-call(bf16[1024,3584]{1,0:T(8,128)(2,1)S(1)} %bitcast.46, bf16[1,3584,1024]{2,1,0:T(8,128)(2,1)S(1)} %bitcast.48, bf16[1,3584,1024]{2,1,0:T(8,128)(2,1)S(1)} %bitcast.50, bf16[1,1024,3584]{2,1,0:T(8,128)(2,1)} %refs_3_.1), custom_call_target="tpu_custom_call" | custom-call | flops 22548578304 | bytes 36700160 | tf_op jit(solution)/shard_map/experts/pallas_call | solution.py:300
  248.6 90.6 %all_to_all.11 = bf16[128,8,3584]{2,1,0:T(8,128)(2,1)S(1)} all-to-all(bf16[128,8,3584]{2,1,0:T(8,128)(2,1)} %bitcast.51), channel_id=1, replica_groups=mesh['seq'=8,'exp'=16] {'seq','exp'}, dimensions={0} | all-to-all | bytes 14680064 | tf_op jit(solution)/shard_map/all_to_all | solution.py:409
  339.2 2.7 combine.1
  (72 shorter events, 9.4 us)
Async XLA Ops:
  0.6 15.6 %copy-start.8 = (s32[64,8]{0,1:T(8,128)S(1)}, s32[64,8]{0,1:T(8,128)}, u32[]{:S(2)}) copy-start(s32[64,8]{0,1:T(8,128)} %param.19) | copy-start | bytes 6148
  0.6 15.6 %copy-start.9 = (f32[64,8]{0,1:T(8,128)S(1)}, f32[64,8]{0,1:T(8,128)}, u32[]{:S(2)}) copy-start(f32[64,8]{0,1:T(8,128)} %param.20) | copy-start | bytes 6148
  0.7 15.6 %copy-start.10 = (s32[8,3]{0,1:T(4,128)S(1)}, s32[8,3]{0,1:T(4,128)}, u32[]{:S(2)}) copy-start(s32[8,3]{0,1:T(4,128)} %param.15) | copy-start | bytes 292
  2.9 21.5 %collective-permute-start.4 = (bf16[128,3584]{1,0:T(8,128)(2,1)}, bf16[128,3584]{1,0:T(8,128)(2,1)}, u32[]{:S(2)}, u32[]{:S(2)}) collective-permute-start(bf16[128,3584]{1,0:T(8,128)(2,1)} %constant_dynamic-slice_fusion), channel_id=1, source_target_pairs={{0,12},{1,13},{2,14},{3,15},{4,0},{5,1},{6,2},{7,3},{8,4},{9,5},{1... | collective-permute-start | bytes 2752520 | tf_op jit(solution)/shard_map/ppermute | solution.py:210
  3.1 21.3 %collective-permute-start.3 = (bf16[128,3584]{1,0:T(8,128)(2,1)}, bf16[128,3584]{1,0:T(8,128)(2,1)}, u32[]{:S(2)}, u32[]{:S(2)}) collective-permute-start(bf16[128,3584]{1,0:T(8,128)(2,1)} %constant_dynamic-slice_fusion), channel_id=1, source_target_pairs={{0,4},{1,5},{2,6},{3,7},{4,8},{5,9},{6,10},{7,11},{8,12},{9,13},{1... | collective-permute-start | bytes 2752520 | tf_op jit(solution)/shard_map/ppermute | solution.py:210
  5.6 22.4 %copy-start = (bf16[2,1024,256]{2,1,0:T(8,128)(2,1)}, bf16[2,1024,256]{2,1,0:T(8,128)(2,1)S(1)}, u32[]{:S(2)}) copy-start(bf16[2,1024,256]{2,1,0:T(8,128)(2,1)S(1)} %pad_maximum_fusion.1.kv_ref.refs_0_) | copy-start | bytes 3145732
  5.6 49.3 %collective-permute-start.2 = (bf16[2,1024,256]{2,1,0:T(8,128)(2,1)S(1)}, bf16[2,1024,256]{2,1,0:T(8,128)(2,1)S(1)}, u32[]{:S(2)}, u32[]{:S(2)}) collective-permute-start(bf16[2,1024,256]{2,1,0:T(8,128)(2,1)S(1)} %pad_maximum_fusion.1.kv_ref.refs_0_), channel_id=1, source_target_pairs={{0,96},{16,112},{1,97},{17,113},{2,98},{18,114},{3,99},{19,115},{4... | collective-permute-start | bytes 3145736 | tf_op jit(solution)/shard_map/ppermute | solution.py:237
  11.4 43.6 %collective-permute-start.1 = (bf16[2,1024,256]{2,1,0:T(8,128)(2,1)S(1)}, bf16[2,1024,256]{2,1,0:T(8,128)(2,1)S(1)}, u32[]{:S(2)}, u32[]{:S(2)}) collective-permute-start(bf16[2,1024,256]{2,1,0:T(8,128)(2,1)S(1)} %pad_maximum_fusion.1.kv_ref.refs_0_), channel_id=1, source_target_pairs={{0,64},{16,80},{32,96},{48,112},{1,65},{17,81},{33,97},{49,113},{2... | collective-permute-start | bytes 3145736 | tf_op jit(solution)/shard_map/ppermute | solution.py:237
  12.7 43.6 %collective-permute-start = (bf16[2,1024,256]{2,1,0:T(8,128)(2,1)S(1)}, bf16[2,1024,256]{2,1,0:T(8,128)(2,1)}, u32[]{:S(2)}, u32[]{:S(2)}) collective-permute-start(bf16[2,1024,256]{2,1,0:T(8,128)(2,1)S(1)} %pad_maximum_fusion.1.kv_ref.refs_0_), channel_id=1, source_target_pairs={{0,32},{16,48},{32,64},{48,80},{64,96},{80,112},{1,33},{17,49},{33... | collective-permute-start | bytes 3145736 | tf_op jit(solution)/shard_map/ppermute | solution.py:237
  24.4 32.0 %collective-permute-start.5 = (bf16[128,3584]{1,0:T(8,128)(2,1)}, bf16[128,3584]{1,0:T(8,128)(2,1)}, u32[]{:S(2)}, u32[]{:S(2)}) collective-permute-start(bf16[128,3584]{1,0:T(8,128)(2,1)} %constant_dynamic-slice_fusion), channel_id=1, source_target_pairs={{0,8},{1,9},{2,10},{3,11},{4,12},{5,13},{6,14},{7,15},{8,0},{9,1},... | collective-permute-start | bytes 2752520 | tf_op jit(solution)/shard_map/ppermute | solution.py:210
  55.0 1.4 copy-start.1
  55.0 1.4 copy-start.2
  59.0 4.8 %copy-start.4 = (bf16[256,3584]{1,0:T(8,128)(2,1)S(1)}, bf16[256,3584]{1,0:T(8,128)(2,1)}, u32[]{:S(2)}) copy-start(bf16[256,3584]{1,0:T(8,128)(2,1)} %pad_maximum_fusion) | copy-start | bytes 5505028
  59.0 6.1 %collective-permute-start.6 = (bf16[2,2,1024,128]{3,2,1,0:T(8,128)(2,1)}, bf16[2,2,1024,128]{3,2,1,0:T(8,128)(2,1)}, u32[]{:S(2)}, u32[]{:S(2)}) collective-permute-start(bf16[2,2,1024,128]{3,2,1,0:T(8,128)(2,1)} %choose.2), channel_id=1, source_target_pairs={{0,16},{16,0},{32,48},{48,32},{64,80},{80,64},{96,112},{112,96},{1... | collective-permute-start | bytes 3145736 | tf_op jit(solution)/shard_map/ppermute | solution.py:220
  63.8 21.2 %collective-permute-start.11 = (bf16[256,3584]{1,0:T(8,128)(2,1)S(1)}, bf16[256,3584]{1,0:T(8,128)(2,1)}, u32[]{:S(2)}, u32[]{:S(2)}) collective-permute-start(bf16[256,3584]{1,0:T(8,128)(2,1)S(1)} %copy-done.4), channel_id=1, source_target_pairs={{0,16},{16,0},{32,48},{48,32},{64,80},{80,64},{96,112},{112,96},{1... | collective-permute-start | bytes 5505032 | tf_op jit(solution)/shard_map/ppermute | solution.py:220
  64.0 6.4 %collective-permute-start.7 = (bf16[2,2,1024,128]{3,2,1,0:T(8,128)(2,1)}, bf16[2,2,1024,128]{3,2,1,0:T(8,128)(2,1)S(1)}, u32[]{:S(2)}, u32[]{:S(2)}) collective-permute-start(bf16[2,2,1024,128]{3,2,1,0:T(8,128)(2,1)} %choose.3), channel_id=1, source_target_pairs={{0,16},{16,0},{32,48},{48,32},{64,80},{80,64},{96,112},{112,96},{1... | collective-permute-start | bytes 3145736 | tf_op jit(solution)/shard_map/ppermute | solution.py:220
  65.0 16.1 %collective-permute-start.12 = (bf16[128,3584]{1,0:T(8,128)(2,1)}, bf16[128,3584]{1,0:T(8,128)(2,1)}, u32[]{:S(2)}, u32[]{:S(2)}) collective-permute-start(bf16[128,3584]{1,0:T(8,128)(2,1)} %collective-permute-done.5.refs_7_), channel_id=1, source_target_pairs={{0,16},{16,0},{32,48},{48,32},{64,80},{80,64},{96,112},{112,96},{1... | collective-permute-start | bytes 2752520 | tf_op jit(solution)/shard_map/ppermute | solution.py:220
  70.4 1.1 copy-start.11
  76.5 5.3 %collective-permute-start.8 = (bf16[256,256]{1,0:T(8,128)(2,1)}, bf16[256,256]{1,0:T(8,128)(2,1)S(1)}, u32[]{:S(2)}, u32[]{:S(2)}) collective-permute-start(bf16[256,256]{1,0:T(8,128)(2,1)} %get-tuple-element.47), channel_id=1, source_target_pairs={{0,4},{1,5},{2,6},{3,7},{4,8},{5,9},{6,10},{7,11},{8,12},{9,13},{1... | collective-permute-start | bytes 393224 | tf_op jit(solution)/shard_map/ppermute | solution.py:210
  78.7 5.7 %collective-permute-start.9 = (bf16[256,256]{1,0:T(8,128)(2,1)}, bf16[256,256]{1,0:T(8,128)(2,1)S(1)}, u32[]{:S(2)}, u32[]{:S(2)}) collective-permute-start(bf16[256,256]{1,0:T(8,128)(2,1)} %get-tuple-element.48), channel_id=1, source_target_pairs={{0,12},{1,13},{2,14},{3,15},{4,0},{5,1},{6,2},{7,3},{8,4},{9,5},{1... | collective-permute-start | bytes 393224 | tf_op jit(solution)/shard_map/ppermute | solution.py:210
  78.7 6.4 %collective-permute-start.10 = (bf16[256,256]{1,0:T(8,128)(2,1)}, bf16[256,256]{1,0:T(8,128)(2,1)S(1)}, u32[]{:S(2)}, u32[]{:S(2)}) collective-permute-start(bf16[256,256]{1,0:T(8,128)(2,1)} %get-tuple-element.49), channel_id=1, source_target_pairs={{0,8},{1,9},{2,10},{3,11},{4,12},{5,13},{6,14},{7,15},{8,0},{9,1},... | collective-permute-start | bytes 393224 | tf_op jit(solution)/shard_map/ppermute | solution.py:210
  81.8 3.2 copy-start.12
  85.7 31.4 %copy-start.5 = (bf16[64,3584]{1,0:T(8,128)(2,1)S(1)}, bf16[64,3584]{1,0:T(8,128)(2,1)}, u32[]{:S(2)}) copy-start(bf16[64,3584]{1,0:T(8,128)(2,1)} %param.17) | copy-start | bytes 1376260
  85.7 32.9 %copy-start.7 = (f32[3584]{0:T(1024)S(1)}, f32[3584]{0:T(1024)}, u32[]{:S(2)}) copy-start(f32[3584]{0:T(1024)} %param.18) | copy-start | bytes 43012
  92.6 13.6 %collective-permute-start.13 = (bf16[64,3584]{1,0:T(8,128)(2,1)}, bf16[64,3584]{1,0:T(8,128)(2,1)S(1)}, u32[]{:S(2)}, u32[]{:S(2)}) collective-permute-start(bf16[64,3584]{1,0:T(8,128)(2,1)} %get-tuple-element.57), channel_id=1, source_target_pairs={{0,1},{1,2},{2,3},{3,0},{4,5},{5,6},{6,7},{7,4},{8,9},{9,10},{10,1... | collective-permute-start | bytes 1376264 | tf_op jit(solution)/shard_map/ppermute | solution.py:215
  94.0 12.2 %collective-permute-start.14 = (bf16[64,3584]{1,0:T(8,128)(2,1)}, bf16[64,3584]{1,0:T(8,128)(2,1)S(1)}, u32[]{:S(2)}, u32[]{:S(2)}) collective-permute-start(bf16[64,3584]{1,0:T(8,128)(2,1)} %get-tuple-element.58), channel_id=1, source_target_pairs={{0,3},{1,0},{2,1},{3,2},{4,7},{5,4},{6,5},{7,6},{8,11},{9,8},{10,9... | collective-permute-start | bytes 1376264 | tf_op jit(solution)/shard_map/ppermute | solution.py:215
  95.5 21.6 %collective-permute-start.15 = (bf16[64,3584]{1,0:T(8,128)(2,1)}, bf16[64,3584]{1,0:T(8,128)(2,1)S(1)}, u32[]{:S(2)}, u32[]{:S(2)}) collective-permute-start(bf16[64,3584]{1,0:T(8,128)(2,1)} %get-tuple-element.59), channel_id=1, source_target_pairs={{0,2},{1,3},{2,0},{3,1},{4,6},{5,7},{6,4},{7,5},{8,10},{9,11},{10,... | collective-permute-start | bytes 1376264 | tf_op jit(solution)/shard_map/ppermute | solution.py:215
  118.6 2.2 copy-start.6
  118.6 100.3 %slice-start = ((s8[7340032]{0:T(1024)(128)(4,1)}), s8[4194304]{0:T(1024)(128)(4,1)S(1)}, s32[]{:S(2)}) async-start(s8[7340032]{0:T(1024)(128)(4,1)} %bitcast.47), calls=%async_computation.2 | async-start | bytes 8388608
  118.6 100.3 %slice-start.2 = ((s8[7340032]{0:T(1024)(128)(4,1)}), s8[4194304]{0:T(1024)(128)(4,1)S(1)}, s32[]{:S(2)}) async-start(s8[7340032]{0:T(1024)(128)(4,1)} %bitcast.49), calls=%async_computation.4 | async-start | bytes 8388608
  120.8 98.2 %slice-start.1 = ((s8[7340032]{0:T(1024)(128)(4,1)}), s8[3145728]{0:T(1024)(128)(4,1)S(1)}, s32[]{:S(2)}) async-start(s8[7340032]{0:T(1024)(128)(4,1)} %bitcast.47), calls=%async_computation.3 | async-start | bytes 6291456
  120.8 98.2 %slice-start.3 = ((s8[7340032]{0:T(1024)(128)(4,1)}), s8[3145728]{0:T(1024)(128)(4,1)S(1)}, s32[]{:S(2)}) async-start(s8[7340032]{0:T(1024)(128)(4,1)} %bitcast.49), calls=%async_computation.5 | async-start | bytes 6291456
  (3 other events, 2.3 us)

commit v6 on v5

--- a/solution.py
+++ b/solution.py
@@ -119,7 +119,7 @@
         input_output_aliases={i: i for i in range(len(extra))},
         scratch_shapes=[pltpu.VMEM((2, n, HD), jnp.bfloat16)]
         + [pltpu.VMEM((n, HD), jnp.float32)] * 3,
-        compiler_params=pltpu.CompilerParams(vmem_limit_bytes=60 * 1024 * 1024),
+        compiler_params=pltpu.CompilerParams(vmem_limit_bytes=32 * 1024 * 1024),
         cost_estimate=pl.CostEstimate(
             flops=48 * n * n * HD, bytes_accessed=24 * n * HD, transcendentals=2 * n * n
         ),
@@ -142,12 +142,12 @@
     count = fars.shape[0]
     return pl.pallas_call(
         choose_kernel,
-        grid=(1,),
+        grid=(2, 2),
         in_specs=[pl.BlockSpec(memory_space=pltpu.SMEM)]
-        + [pl.BlockSpec((2, n, HD), lambda i: (0, 0, head))] * len(blocks),
-        out_specs=pl.BlockSpec((count, 2, n, HD), lambda i: (0, 0, 0, 0)),
+        + [pl.BlockSpec((1, n // 2, HD), lambda i, k: (i, k, head))] * len(blocks),
+        out_specs=pl.BlockSpec((count, 1, n // 2, HD), lambda i, k: (0, i, k, 0)),
         out_shape=jax.ShapeDtypeStruct((count, 2, n, HD), jnp.bfloat16),
-        compiler_params=pltpu.CompilerParams(vmem_limit_bytes=60 * 1024 * 1024),
+        compiler_params=pltpu.CompilerParams(vmem_limit_bytes=16 * 1024 * 1024),
         cost_estimate=pl.CostEstimate(flops=0, bytes_accessed=24 * n * HD, transcendentals=0),
         name="choose",
     )(fars, *blocks)
@@ -189,7 +189,7 @@
         out_specs=[pl.BlockSpec((n_rows // SIDE, tile), lambda i: (0, i))] * SIDE,
         out_shape=[jax.ShapeDtypeStruct((n_rows // SIDE, width), jnp.bfloat16)] * SIDE,
         scratch_shapes=[pltpu.VMEM((n_rows, tile), jnp.float32)],
-        compiler_params=pltpu.CompilerParams(vmem_limit_bytes=60 * 1024 * 1024),
+        compiler_params=pltpu.CompilerParams(vmem_limit_bytes=44 * 1024 * 1024),
         cost_estimate=pl.CostEstimate(
             flops=6 * n * n_rows * depth * width,
             bytes_accessed=2 * n * (n_rows * depth + depth * width) + 2 * n_rows * width,
@@ -239,8 +239,8 @@
     mine.append(send_share(after(share, *mine), 2))
     state = attend_own(queries, kv)
     joined = jnp.concatenate(mine[:2])
-    near, mine, joined, state, early = lax.optimization_barrier(
-        (near, mine, joined, state, early)
+    near, mine, joined, state, early, codes, partner_far = lax.optimization_barrier(
+        (near, mine, joined, state, early, codes, partner_far)
     )
     heads = range(queries.shape[1] // HD)
     asked = [choose(partner_far, [kv, *near], head) for head in heads]

time: 345 us -> 338 us (0.980)
  Pallas kernels: 60.5 us -> 55.1 us
  transfers between devices with their start and end apart: 16 -> 16, of which waited for: 9 -> 9; matrix products, arithmetic and copies ran while one was open for 2% -> 2% of each run, Pallas kernels for 5% -> 4%
where the time goes in v6:
time: 338 us; the launch traced here: 336 us
  blocking collectives  188 us (56%)
  Pallas kernels  55.1 us (16%)
  waiting for transfers between devices  51.1 us (15%)
  starting transfers between devices  27.1 us (8%)
  other arithmetic  6.2 us (2%)
  local copies, waits for them, and re-layouts  4.78 us (1%)
    all_to_all x1, blocking collectives, per_device(): lax.all_to_all(senders.reshape(n_experts, cap, width), ('seq', 'exp'), sp...  97 us
    all_to_all x1, blocking collectives, per_device(): lax.all_to_all(produced.reshape(n_experts, cap, width), ('seq', 'exp'), s...  90.6 us
    pallas_call x1, Pallas kernels, expert_rows(): pl.pallas_call(lambda *refs: expert_kernel(n_ff, *refs), grid=(n_ff + n_o...  29.7 us
    ppermute x3, waiting for transfers between devices, ring_y(): return lax.ppermute(array, 'exp', perm)  19.9 us
    ppermute x3, waiting for transfers between devices, attend(): near = [lax.ppermute(kv, 'seq', chip_perm(far)) for far in range(1, SIDE)]  18.3 us
    ppermute x3, starting transfers between devices, attend(): near = [lax.ppermute(kv, 'seq', chip_perm(far)) for far in range(1, SIDE)]  10.5 us
    ppermute x6, waiting for transfers between devices, ring_x(): return lax.ppermute(array, 'exp', perm)  10.4 us
    ppermute x6, starting transfers between devices, ring_x(): return lax.ppermute(array, 'exp', perm)  9.13 us
  transfers between devices with their start and end apart: 16, of which 9 were waited for; matrix products, arithmetic and copies ran while one was open for 2% of the time, Pallas kernels for 4%

profile of v6, /device:TPU:5, one launch (start us, length us, event | category | flops | bytes accessed | tf_op | source)
XLA Modules:
  0.0 335.5 jit_solution(302538137246935251)
XLA Ops:
  0.7 2.2 constant_dynamic-slice_fusion
  4.3 1.3 pad_maximum_fusion.1.kv_ref.refs_0_
  5.6 5.7 %collective-permute-start.2 = (bf16[2,1024,256]{2,1,0:T(8,128)(2,1)S(1)}, bf16[2,1024,256]{2,1,0:T(8,128)(2,1)S(1)}, u32[]{:S(2)}, u32[]{:S(2)}) collective-permute-start(bf16[2,1024,256]{2,1,0:T(8,128)(2,1)S(1)} %pad_maximum_fusion.1.kv_ref.refs_0_), channel_id=1, source_target_pairs={{0,96},{16,112},{1,97},{17,113},{2,98},{18,114},{3,99},{19,115},{4... | collective-permute-start | bytes 3145736 | tf_op jit(solution)/shard_map/ppermute | solution.py:237
  11.4 1.4 collective-permute-start.1
  12.7 3.4 %collective-permute-start = (bf16[2,1024,256]{2,1,0:T(8,128)(2,1)S(1)}, bf16[2,1024,256]{2,1,0:T(8,128)(2,1)}, u32[]{:S(2)}, u32[]{:S(2)}) collective-permute-start(bf16[2,1024,256]{2,1,0:T(8,128)(2,1)S(1)} %pad_maximum_fusion.1.kv_ref.refs_0_), channel_id=1, source_target_pairs={{0,32},{16,48},{32,64},{48,80},{64,96},{80,112},{1,33},{17,49},{33... | collective-permute-start | bytes 3145736 | tf_op jit(solution)/shard_map/ppermute | solution.py:237
  18.2 6.2 %collective-permute-done.4.refs_6_ = bf16[128,3584]{1,0:T(8,128)(2,1)} collective-permute-done((bf16[128,3584]{1,0:T(8,128)(2,1)}, bf16[128,3584]{1,0:T(8,128)(2,1)}, u32[]{:S(2)}, u32[]{:S(2)}) %collective-permute-start.4) | collective-permute-done | bytes 917536 | tf_op jit(solution)/shard_map/ppermute | solution.py:210
  24.4 3.6 %collective-permute-start.5 = (bf16[128,3584]{1,0:T(8,128)(2,1)}, bf16[128,3584]{1,0:T(8,128)(2,1)}, u32[]{:S(2)}, u32[]{:S(2)}) collective-permute-start(bf16[128,3584]{1,0:T(8,128)(2,1)} %constant_dynamic-slice_fusion), channel_id=1, source_target_pairs={{0,8},{1,9},{2,10},{3,11},{4,12},{5,13},{6,14},{7,15},{8,0},{9,1},... | collective-permute-start | bytes 2752520 | tf_op jit(solution)/shard_map/ppermute | solution.py:210
  28.0 6.1 %attend_own.1 = (f32[1024,256]{1,0:T(8,128)}, f32[1024,256]{1,0:T(8,128)}, f32[1024,256]{1,0:T(8,128)}) custom-call(bf16[1024,256]{1,0:T(8,128)(2,1)} %refs_5_.1, bf16[2,1024,256]{2,1,0:T(8,128)(2,1)} %copy-done), custom_call_target="tpu_custom_call" | custom-call | flops 2147483648 | bytes 4718592 | tf_op jit(solution)/shard_map/attend_own/pallas_call | solution.py:52
  35.3 2.8 pad_maximum_fusion
  38.1 16.9 %collective-permute-done.2.refs_3_.refs_7_.refs_11_ = bf16[2,1024,256]{2,1,0:T(8,128)(2,1)S(1)} collective-permute-done((bf16[2,1024,256]{2,1,0:T(8,128)(2,1)S(1)}, bf16[2,1024,256]{2,1,0:T(8,128)(2,1)S(1)}, u32[]{:S(2)}, u32[]{:S(2)}) %collective-permute-start.2) | collective-permute-done | bytes 1048608 | tf_op jit(solution)/shard_map/ppermute | solution.py:237
  55.0 1.4 collective-permute-done.refs_1_.refs_5_.refs_9_
  56.4 2.3 choose.2
  58.8 2.2 collective-permute-start.6
  61.0 2.3 choose.3
  64.1 3.1 attend_far.2
  67.3 2.5 collective-permute-done.7.refs_12_
  69.8 3.3 attend_far.3
  73.1 2.2 collective-permute-start.8
  75.3 1.9 collective-permute-start.10
  78.2 2.6 collective-permute-done.9.refs_2_
  81.5 1.5 copy-done.2
  83.0 5.5 %project.1 = (bf16[64,3584]{1,0:T(8,128)(2,1)S(1)}, bf16[64,3584]{1,0:T(8,128)(2,1)S(1)}, bf16[64,3584]{1,0:T(8,128)(2,1)S(1)}, bf16[64,3584]{1,0:T(8,128)(2,1)S(1)}) custom-call(s32[2]{0:T(128)S(1)} %pad_add_fusion.spot_ref, bf16[256,256]{1,0:T(8,128)(2,1)S(1)} %get-tuple-element.50.refs_0_, bf16[256,256]{1,0:T(8,128)(2,1)S(1)} %collective-permute-done.8.refs_1_, ...), custom_call_target="tpu_custom_call" | custom-call | flops 4227858432 | bytes 7733248 | tf_op jit(solution)/shard_map/project/pallas_call | solution.py:181
  88.5 1.4 collective-permute-start.13
  89.9 1.5 collective-permute-start.14
  91.4 1.6 collective-permute-start.15
  93.0 8.9 %collective-permute-done.13 = bf16[64,3584]{1,0:T(8,128)(2,1)S(1)} collective-permute-done((bf16[64,3584]{1,0:T(8,128)(2,1)S(1)}, bf16[64,3584]{1,0:T(8,128)(2,1)S(1)}, u32[]{:S(2)}, u32[]{:S(2)}) %collective-permute-start.13) | collective-permute-done | bytes 458784 | tf_op jit(solution)/shard_map/ppermute | solution.py:215
  101.9 10.9 %collective-permute-done.15 = bf16[64,3584]{1,0:T(8,128)(2,1)S(1)} collective-permute-done((bf16[64,3584]{1,0:T(8,128)(2,1)S(1)}, bf16[64,3584]{1,0:T(8,128)(2,1)S(1)}, u32[]{:S(2)}, u32[]{:S(2)}) %collective-permute-start.15) | collective-permute-done | bytes 458784 | tf_op jit(solution)/shard_map/ppermute | solution.py:215
  113.3 2.1 fusion
  115.5 97.0 %all_to_all.10 = bf16[128,8,3584]{2,1,0:T(8,128)(2,1)S(1)} all-to-all(bf16[128,8,3584]{2,1,0:T(8,128)(2,1)S(1)} %fusion), channel_id=1, replica_groups=mesh['seq'=8,'exp'=16] {'seq','exp'}, dimensions={0} | all-to-all | bytes 14680064 | tf_op jit(solution)/shard_map/all_to_all | solution.py:401
  212.6 29.7 %experts.1 = bf16[1024,3584]{1,0:T(8,128)(2,1)} custom-call(bf16[1024,3584]{1,0:T(8,128)(2,1)S(1)} %bitcast.46, bf16[1,3584,1024]{2,1,0:T(8,128)(2,1)S(1)} %bitcast.48, bf16[1,3584,1024]{2,1,0:T(8,128)(2,1)S(1)} %bitcast.50, bf16[1,1024,3584]{2,1,0:T(8,128)(2,1)} %refs_3_.1), custom_call_target="tpu_custom_call" | custom-call | flops 22548578304 | bytes 36700160 | tf_op jit(solution)/shard_map/experts/pallas_call | solution.py:300
  242.2 90.6 %all_to_all.11 = bf16[128,8,3584]{2,1,0:T(8,128)(2,1)S(1)} all-to-all(bf16[128,8,3584]{2,1,0:T(8,128)(2,1)} %bitcast.51), channel_id=1, replica_groups=mesh['seq'=8,'exp'=16] {'seq','exp'}, dimensions={0} | all-to-all | bytes 14680064 | tf_op jit(solution)/shard_map/all_to_all | solution.py:409
  332.8 2.7 combine.1
  (69 shorter events, 7.6 us)
Async XLA Ops:
  0.6 15.5 %copy-start.11 = (s32[64,8]{0,1:T(8,128)S(1)}, s32[64,8]{0,1:T(8,128)}, u32[]{:S(2)}) copy-start(s32[64,8]{0,1:T(8,128)} %param.19) | copy-start | bytes 6148
  0.6 15.6 %copy-start.12 = (f32[64,8]{0,1:T(8,128)S(1)}, f32[64,8]{0,1:T(8,128)}, u32[]{:S(2)}) copy-start(f32[64,8]{0,1:T(8,128)} %param.20) | copy-start | bytes 6148
  0.7 15.6 %copy-start.13 = (s32[8,3]{0,1:T(4,128)S(1)}, s32[8,3]{0,1:T(4,128)}, u32[]{:S(2)}) copy-start(s32[8,3]{0,1:T(4,128)} %param.15) | copy-start | bytes 292
  2.9 21.5 %collective-permute-start.4 = (bf16[128,3584]{1,0:T(8,128)(2,1)}, bf16[128,3584]{1,0:T(8,128)(2,1)}, u32[]{:S(2)}, u32[]{:S(2)}) collective-permute-start(bf16[128,3584]{1,0:T(8,128)(2,1)} %constant_dynamic-slice_fusion), channel_id=1, source_target_pairs={{0,12},{1,13},{2,14},{3,15},{4,0},{5,1},{6,2},{7,3},{8,4},{9,5},{1... | collective-permute-start | bytes 2752520 | tf_op jit(solution)/shard_map/ppermute | solution.py:210
  3.1 21.3 %collective-permute-start.3 = (bf16[128,3584]{1,0:T(8,128)(2,1)}, bf16[128,3584]{1,0:T(8,128)(2,1)}, u32[]{:S(2)}, u32[]{:S(2)}) collective-permute-start(bf16[128,3584]{1,0:T(8,128)(2,1)} %constant_dynamic-slice_fusion), channel_id=1, source_target_pairs={{0,4},{1,5},{2,6},{3,7},{4,8},{5,9},{6,10},{7,11},{8,12},{9,13},{1... | collective-permute-start | bytes 2752520 | tf_op jit(solution)/shard_map/ppermute | solution.py:210
  5.6 22.4 %copy-start = (bf16[2,1024,256]{2,1,0:T(8,128)(2,1)}, bf16[2,1024,256]{2,1,0:T(8,128)(2,1)S(1)}, u32[]{:S(2)}) copy-start(bf16[2,1024,256]{2,1,0:T(8,128)(2,1)S(1)} %pad_maximum_fusion.1.kv_ref.refs_0_) | copy-start | bytes 3145732
  5.6 49.3 %collective-permute-start.2 = (bf16[2,1024,256]{2,1,0:T(8,128)(2,1)S(1)}, bf16[2,1024,256]{2,1,0:T(8,128)(2,1)S(1)}, u32[]{:S(2)}, u32[]{:S(2)}) collective-permute-start(bf16[2,1024,256]{2,1,0:T(8,128)(2,1)S(1)} %pad_maximum_fusion.1.kv_ref.refs_0_), channel_id=1, source_target_pairs={{0,96},{16,112},{1,97},{17,113},{2,98},{18,114},{3,99},{19,115},{4... | collective-permute-start | bytes 3145736 | tf_op jit(solution)/shard_map/ppermute | solution.py:237
  11.4 43.6 %collective-permute-start.1 = (bf16[2,1024,256]{2,1,0:T(8,128)(2,1)S(1)}, bf16[2,1024,256]{2,1,0:T(8,128)(2,1)S(1)}, u32[]{:S(2)}, u32[]{:S(2)}) collective-permute-start(bf16[2,1024,256]{2,1,0:T(8,128)(2,1)S(1)} %pad_maximum_fusion.1.kv_ref.refs_0_), channel_id=1, source_target_pairs={{0,64},{16,80},{32,96},{48,112},{1,65},{17,81},{33,97},{49,113},{2... | collective-permute-start | bytes 3145736 | tf_op jit(solution)/shard_map/ppermute | solution.py:237
  12.7 43.6 %collective-permute-start = (bf16[2,1024,256]{2,1,0:T(8,128)(2,1)S(1)}, bf16[2,1024,256]{2,1,0:T(8,128)(2,1)}, u32[]{:S(2)}, u32[]{:S(2)}) collective-permute-start(bf16[2,1024,256]{2,1,0:T(8,128)(2,1)S(1)} %pad_maximum_fusion.1.kv_ref.refs_0_), channel_id=1, source_target_pairs={{0,32},{16,48},{32,64},{48,80},{64,96},{80,112},{1,33},{17,49},{33... | collective-permute-start | bytes 3145736 | tf_op jit(solution)/shard_map/ppermute | solution.py:237
  24.4 32.0 %collective-permute-start.5 = (bf16[128,3584]{1,0:T(8,128)(2,1)}, bf16[128,3584]{1,0:T(8,128)(2,1)}, u32[]{:S(2)}, u32[]{:S(2)}) collective-permute-start(bf16[128,3584]{1,0:T(8,128)(2,1)} %constant_dynamic-slice_fusion), channel_id=1, source_target_pairs={{0,8},{1,9},{2,10},{3,11},{4,12},{5,13},{6,14},{7,15},{8,0},{9,1},... | collective-permute-start | bytes 2752520 | tf_op jit(solution)/shard_map/ppermute | solution.py:210
  34.1 22.3 %copy-start.1 = (bf16[2,1024,256]{2,1,0:T(8,128)(2,1)S(1)}, bf16[2,1024,256]{2,1,0:T(8,128)(2,1)}, u32[]{:S(2)}) copy-start(bf16[2,1024,256]{2,1,0:T(8,128)(2,1)} %copy-done) | copy-start | bytes 3145732
  58.7 5.4 %copy-start.3 = (bf16[1024,256]{1,0:T(8,128)(2,1)S(1)}, bf16[1024,256]{1,0:T(8,128)(2,1)}, u32[]{:S(2)}) copy-start(bf16[1024,256]{1,0:T(8,128)(2,1)} %refs_5_.1) | copy-start | bytes 1572868
  58.7 5.4 %copy-start.4 = (f32[1024,256]{1,0:T(8,128)S(1)}, f32[1024,256]{1,0:T(8,128)}, u32[]{:S(2)}) copy-start(f32[1024,256]{1,0:T(8,128)} %get-tuple-element.39.refs_2_.refs_6_) | copy-start | bytes 3145732
  58.7 5.4 %copy-start.5 = (f32[1024,256]{1,0:T(8,128)S(1)}, f32[1024,256]{1,0:T(8,128)}, u32[]{:S(2)}) copy-start(f32[1024,256]{1,0:T(8,128)} %get-tuple-element.40.refs_3_.refs_7_) | copy-start | bytes 3145732
  58.7 5.4 %copy-start.6 = (f32[1024,256]{1,0:T(8,128)S(1)}, f32[1024,256]{1,0:T(8,128)}, u32[]{:S(2)}) copy-start(f32[1024,256]{1,0:T(8,128)} %get-tuple-element.41.refs_4_.refs_8_) | copy-start | bytes 3145732
  58.8 5.4 %collective-permute-start.6 = (bf16[2,2,1024,128]{3,2,1,0:T(8,128)(2,1)S(1)}, bf16[2,2,1024,128]{3,2,1,0:T(8,128)(2,1)S(1)}, u32[]{:S(2)}, u32[]{:S(2)}) collective-permute-start(bf16[2,2,1024,128]{3,2,1,0:T(8,128)(2,1)S(1)} %choose.2), channel_id=1, source_target_pairs={{0,16},{16,0},{32,48},{48,32},{64,80},{80,64},{96,112},{112,96},{1... | collective-permute-start | bytes 3145736 | tf_op jit(solution)/shard_map/ppermute | solution.py:220
  63.3 18.2 %collective-permute-start.11 = (bf16[256,3584]{1,0:T(8,128)(2,1)}, bf16[256,3584]{1,0:T(8,128)(2,1)}, u32[]{:S(2)}, u32[]{:S(2)}) collective-permute-start(bf16[256,3584]{1,0:T(8,128)(2,1)} %pad_maximum_fusion), channel_id=1, source_target_pairs={{0,16},{16,0},{32,48},{48,32},{64,80},{80,64},{96,112},{112,96},{1... | collective-permute-start | bytes 5505032 | tf_op jit(solution)/shard_map/ppermute | solution.py:220
  63.6 6.2 %collective-permute-start.7 = (bf16[2,2,1024,128]{3,2,1,0:T(8,128)(2,1)S(1)}, bf16[2,2,1024,128]{3,2,1,0:T(8,128)(2,1)S(1)}, u32[]{:S(2)}, u32[]{:S(2)}) collective-permute-start(bf16[2,2,1024,128]{3,2,1,0:T(8,128)(2,1)S(1)} %choose.3), channel_id=1, source_target_pairs={{0,16},{16,0},{32,48},{48,32},{64,80},{80,64},{96,112},{112,96},{1... | collective-permute-start | bytes 3145736 | tf_op jit(solution)/shard_map/ppermute | solution.py:220
  63.9 13.4 %collective-permute-start.12 = (bf16[128,3584]{1,0:T(8,128)(2,1)}, bf16[128,3584]{1,0:T(8,128)(2,1)}, u32[]{:S(2)}, u32[]{:S(2)}) collective-permute-start(bf16[128,3584]{1,0:T(8,128)(2,1)} %collective-permute-done.5.refs_7_), channel_id=1, source_target_pairs={{0,16},{16,0},{32,48},{48,32},{64,80},{80,64},{96,112},{112,96},{1... | collective-permute-start | bytes 2752520 | tf_op jit(solution)/shard_map/ppermute | solution.py:220
  73.1 5.1 %collective-permute-start.8 = (bf16[256,256]{1,0:T(8,128)(2,1)S(1)}, bf16[256,256]{1,0:T(8,128)(2,1)S(1)}, u32[]{:S(2)}, u32[]{:S(2)}) collective-permute-start(bf16[256,256]{1,0:T(8,128)(2,1)S(1)} %get-tuple-element.51), channel_id=1, source_target_pairs={{0,4},{1,5},{2,6},{3,7},{4,8},{5,9},{6,10},{7,11},{8,12},{9,13},{1... | collective-permute-start | bytes 393224 | tf_op jit(solution)/shard_map/ppermute | solution.py:210
  75.3 5.5 %collective-permute-start.9 = (bf16[256,256]{1,0:T(8,128)(2,1)S(1)}, bf16[256,256]{1,0:T(8,128)(2,1)S(1)}, u32[]{:S(2)}, u32[]{:S(2)}) collective-permute-start(bf16[256,256]{1,0:T(8,128)(2,1)S(1)} %get-tuple-element.52), channel_id=1, source_target_pairs={{0,12},{1,13},{2,14},{3,15},{4,0},{5,1},{6,2},{7,3},{8,4},{9,5},{1... | collective-permute-start | bytes 393224 | tf_op jit(solution)/shard_map/ppermute | solution.py:210
  75.3 6.2 %collective-permute-start.10 = (bf16[256,256]{1,0:T(8,128)(2,1)S(1)}, bf16[256,256]{1,0:T(8,128)(2,1)S(1)}, u32[]{:S(2)}, u32[]{:S(2)}) collective-permute-start(bf16[256,256]{1,0:T(8,128)(2,1)S(1)} %get-tuple-element.53), channel_id=1, source_target_pairs={{0,8},{1,9},{2,10},{3,11},{4,12},{5,13},{6,14},{7,15},{8,0},{9,1},... | collective-permute-start | bytes 393224 | tf_op jit(solution)/shard_map/ppermute | solution.py:210
  83.0 29.8 %copy-start.8 = (bf16[64,3584]{1,0:T(8,128)(2,1)S(1)}, bf16[64,3584]{1,0:T(8,128)(2,1)}, u32[]{:S(2)}) copy-start(bf16[64,3584]{1,0:T(8,128)(2,1)} %param.17) | copy-start | bytes 1376260
  83.0 30.3 %copy-start.10 = (f32[3584]{0:T(1024)S(1)}, f32[3584]{0:T(1024)}, u32[]{:S(2)}) copy-start(f32[3584]{0:T(1024)} %param.18) | copy-start | bytes 43012
  88.5 13.4 %collective-permute-start.13 = (bf16[64,3584]{1,0:T(8,128)(2,1)S(1)}, bf16[64,3584]{1,0:T(8,128)(2,1)S(1)}, u32[]{:S(2)}, u32[]{:S(2)}) collective-permute-start(bf16[64,3584]{1,0:T(8,128)(2,1)S(1)} %get-tuple-element.61), channel_id=1, source_target_pairs={{0,1},{1,2},{2,3},{3,0},{4,5},{5,6},{6,7},{7,4},{8,9},{9,10},{10,1... | collective-permute-start | bytes 1376264 | tf_op jit(solution)/shard_map/ppermute | solution.py:215
  89.9 12.0 %collective-permute-start.14 = (bf16[64,3584]{1,0:T(8,128)(2,1)S(1)}, bf16[64,3584]{1,0:T(8,128)(2,1)S(1)}, u32[]{:S(2)}, u32[]{:S(2)}) collective-permute-start(bf16[64,3584]{1,0:T(8,128)(2,1)S(1)} %get-tuple-element.62), channel_id=1, source_target_pairs={{0,3},{1,0},{2,1},{3,2},{4,7},{5,4},{6,5},{7,6},{8,11},{9,8},{10,9... | collective-permute-start | bytes 1376264 | tf_op jit(solution)/shard_map/ppermute | solution.py:215
  91.4 21.4 %collective-permute-start.15 = (bf16[64,3584]{1,0:T(8,128)(2,1)S(1)}, bf16[64,3584]{1,0:T(8,128)(2,1)S(1)}, u32[]{:S(2)}, u32[]{:S(2)}) collective-permute-start(bf16[64,3584]{1,0:T(8,128)(2,1)S(1)} %get-tuple-element.63), channel_id=1, source_target_pairs={{0,2},{1,3},{2,0},{3,1},{4,6},{5,7},{6,4},{7,5},{8,10},{9,11},{10,... | collective-permute-start | bytes 1376264 | tf_op jit(solution)/shard_map/ppermute | solution.py:215
  113.3 2.2 copy-start.9
  113.3 99.2 %slice-start = ((s8[7340032]{0:T(1024)(128)(4,1)}), s8[4194304]{0:T(1024)(128)(4,1)S(1)}, s32[]{:S(2)}) async-start(s8[7340032]{0:T(1024)(128)(4,1)} %bitcast.47), calls=%async_computation.2 | async-start | bytes 8388608
  113.3 99.2 %slice-start.2 = ((s8[7340032]{0:T(1024)(128)(4,1)}), s8[4194304]{0:T(1024)(128)(4,1)S(1)}, s32[]{:S(2)}) async-start(s8[7340032]{0:T(1024)(128)(4,1)} %bitcast.49), calls=%async_computation.4 | async-start | bytes 8388608
  115.5 97.1 %slice-start.1 = ((s8[7340032]{0:T(1024)(128)(4,1)}), s8[3145728]{0:T(1024)(128)(4,1)S(1)}, s32[]{:S(2)}) async-start(s8[7340032]{0:T(1024)(128)(4,1)} %bitcast.47), calls=%async_computation.3 | async-start | bytes 6291456
  115.5 97.1 %slice-start.3 = ((s8[7340032]{0:T(1024)(128)(4,1)}), s8[3145728]{0:T(1024)(128)(4,1)S(1)}, s32[]{:S(2)}) async-start(s8[7340032]{0:T(1024)(128)(4,1)} %bitcast.49), calls=%async_computation.5 | async-start | bytes 6291456
  (2 other events, 2.4 us)

commit v7 on v6

--- a/solution.py
+++ b/solution.py
@@ -224,7 +224,7 @@
     return lax.optimization_barrier((array, *earlier))[0]
 
 
-def attend(queries, keys, values, gates, share, send_share, early):
+def attend(queries, keys, values, gates, share_after, send_share, early):
     me = lax.axis_index("seq")
     chip, core = me // CORES, me % CORES
     wanted = gates[me, 1:]
@@ -234,6 +234,7 @@
     codes = jnp.append(codes, lax.axis_index("exp") // SIDE).astype(jnp.int32)
     partner_far = jnp.clip(chip - gates[me ^ 1, 1:] // CORES, 0, SIDE - 1).astype(jnp.int32)
     kv = jnp.stack([keys, values])
+    share = share_after(kv)
     near = [lax.ppermute(kv, "seq", chip_perm(far)) for far in range(1, SIDE)]
     mine = [send_share(share, 1), send_share(share, 3)]
     mine.append(send_share(after(share, *mine), 2))
@@ -254,8 +255,13 @@
 
 def projected(queries, keys, values, gates, o_proj, early):
     core = lax.axis_index("seq") % CORES
-    share = lax.dynamic_slice(o_proj, (core * HD, 0), (HD, o_proj.shape[1]))
-    pieces, mine, theirs, early = attend(queries, keys, values, gates, share, ring_x, early)
+
+    def share_after(seen):
+        return lax.dynamic_slice(after(o_proj, seen), (core * HD, 0), (HD, o_proj.shape[1]))
+
+    pieces, mine, theirs, early = attend(
+        queries, keys, values, gates, share_after, ring_x, early
+    )
     rows = [pieces[0]] + [ring_x(piece, far) for piece, far in zip(pieces[1:], ORDER)]
     spot = jnp.stack([core, lax.axis_index("exp") % SIDE]).astype(jnp.int32)
     sums = project(spot, rows, o_proj, mine, theirs)

time: 338 us -> 339 us (level)
  no operation moved by 1% of the time
where the time goes in v7:
time: 339 us; the launch traced here: 336 us
  blocking collectives  188 us (55%)
  Pallas kernels  55.1 us (16%)
  waiting for transfers between devices  51.1 us (15%)
  starting transfers between devices  27.1 us (8%)
  other arithmetic  6.2 us (2%)
  local copies, waits for them, and re-layouts  5.16 us (2%)
    all_to_all x1, blocking collectives, per_device(): lax.all_to_all(senders.reshape(n_experts, cap, width), ('seq', 'exp'), sp...  97 us
    all_to_all x1, blocking collectives, per_device(): lax.all_to_all(produced.reshape(n_experts, cap, width), ('seq', 'exp'), s...  90.6 us
    pallas_call x1, Pallas kernels, expert_rows(): pl.pallas_call(lambda *refs: expert_kernel(n_ff, *refs), grid=(n_ff + n_o...  29.7 us
    ppermute x3, waiting for transfers between devices, ring_y(): return lax.ppermute(array, 'exp', perm)  19.9 us
    ppermute x3, waiting for transfers between devices, attend(): near = [lax.ppermute(kv, 'seq', chip_perm(far)) for far in range(1, SIDE)]  16.9 us
    ppermute x6, waiting for transfers between devices, ring_x(): return lax.ppermute(array, 'exp', perm)  11.7 us
    ppermute x3, starting transfers between devices, attend(): near = [lax.ppermute(kv, 'seq', chip_perm(far)) for far in range(1, SIDE)]  10.5 us
    ppermute x6, starting transfers between devices, ring_x(): return lax.ppermute(array, 'exp', perm)  9.13 us
  transfers between devices with their start and end apart: 16, of which 9 were waited for; matrix products, arithmetic and copies ran while one was open for 2% of the time, Pallas kernels for 4%

profile of v7, /device:TPU:5, one launch (start us, length us, event | category | flops | bytes accessed | tf_op | source)
XLA Modules:
  0.0 335.9 jit_solution(15793812503033460939)
XLA Ops:
  0.7 1.3 pad_maximum_fusion.1.kv_ref.refs_0_
  2.0 2.6 constant_dynamic-slice_fusion
  6.0 5.7 %collective-permute-start.2 = (bf16[2,1024,256]{2,1,0:T(8,128)(2,1)S(1)}, bf16[2,1024,256]{2,1,0:T(8,128)(2,1)S(1)}, u32[]{:S(2)}, u32[]{:S(2)}) collective-permute-start(bf16[2,1024,256]{2,1,0:T(8,128)(2,1)S(1)} %pad_maximum_fusion.1.kv_ref.refs_0_), channel_id=1, source_target_pairs={{0,96},{16,112},{1,97},{17,113},{2,98},{18,114},{3,99},{19,115},{4... | collective-permute-start | bytes 3145736 | tf_op jit(solution)/shard_map/ppermute | solution.py:238
  11.7 1.4 collective-permute-start.1
  13.1 3.4 %collective-permute-start = (bf16[2,1024,256]{2,1,0:T(8,128)(2,1)S(1)}, bf16[2,1024,256]{2,1,0:T(8,128)(2,1)}, u32[]{:S(2)}, u32[]{:S(2)}) collective-permute-start(bf16[2,1024,256]{2,1,0:T(8,128)(2,1)S(1)} %pad_maximum_fusion.1.kv_ref.refs_0_), channel_id=1, source_target_pairs={{0,32},{16,48},{32,64},{48,80},{64,96},{80,112},{1,33},{17,49},{33... | collective-permute-start | bytes 3145736 | tf_op jit(solution)/shard_map/ppermute | solution.py:238
  18.6 7.5 %collective-permute-done.4.refs_6_ = bf16[128,3584]{1,0:T(8,128)(2,1)} collective-permute-done((bf16[128,3584]{1,0:T(8,128)(2,1)}, bf16[128,3584]{1,0:T(8,128)(2,1)}, u32[]{:S(2)}, u32[]{:S(2)}) %collective-permute-start.4) | collective-permute-done | bytes 917536 | tf_op jit(solution)/shard_map/ppermute | solution.py:210
  26.1 3.6 %collective-permute-start.5 = (bf16[128,3584]{1,0:T(8,128)(2,1)}, bf16[128,3584]{1,0:T(8,128)(2,1)}, u32[]{:S(2)}, u32[]{:S(2)}) collective-permute-start(bf16[128,3584]{1,0:T(8,128)(2,1)} %constant_dynamic-slice_fusion), channel_id=1, source_target_pairs={{0,8},{1,9},{2,10},{3,11},{4,12},{5,13},{6,14},{7,15},{8,0},{9,1},... | collective-permute-start | bytes 2752520 | tf_op jit(solution)/shard_map/ppermute | solution.py:210
  29.7 6.1 %attend_own.1 = (f32[1024,256]{1,0:T(8,128)}, f32[1024,256]{1,0:T(8,128)}, f32[1024,256]{1,0:T(8,128)}) custom-call(bf16[1024,256]{1,0:T(8,128)(2,1)} %refs_5_.1, bf16[2,1024,256]{2,1,0:T(8,128)(2,1)} %copy-done), custom_call_target="tpu_custom_call" | custom-call | flops 2147483648 | bytes 4718592 | tf_op jit(solution)/shard_map/attend_own/pallas_call | solution.py:52
  37.0 2.8 pad_maximum_fusion
  39.8 15.5 %collective-permute-done.2.refs_3_.refs_7_.refs_11_ = bf16[2,1024,256]{2,1,0:T(8,128)(2,1)S(1)} collective-permute-done((bf16[2,1024,256]{2,1,0:T(8,128)(2,1)S(1)}, bf16[2,1024,256]{2,1,0:T(8,128)(2,1)S(1)}, u32[]{:S(2)}, u32[]{:S(2)}) %collective-permute-start.2) | collective-permute-done | bytes 1048608 | tf_op jit(solution)/shard_map/ppermute | solution.py:238
  55.4 1.4 collective-permute-done.refs_1_.refs_5_.refs_9_
  56.8 2.3 choose.2
  59.1 2.2 collective-permute-start.6
  61.4 2.3 choose.3
  64.5 3.1 attend_far.2
  67.6 2.5 collective-permute-done.7.refs_12_
  70.2 3.3 attend_far.3
  73.5 2.2 collective-permute-start.8
  75.7 1.9 collective-permute-start.10
  78.6 2.6 collective-permute-done.9.refs_2_
  81.9 1.5 copy-done.2
  83.4 5.5 %project.1 = (bf16[64,3584]{1,0:T(8,128)(2,1)S(1)}, bf16[64,3584]{1,0:T(8,128)(2,1)S(1)}, bf16[64,3584]{1,0:T(8,128)(2,1)S(1)}, bf16[64,3584]{1,0:T(8,128)(2,1)S(1)}) custom-call(s32[2]{0:T(128)S(1)} %pad_add_fusion.spot_ref, bf16[256,256]{1,0:T(8,128)(2,1)S(1)} %get-tuple-element.52.refs_0_, bf16[256,256]{1,0:T(8,128)(2,1)S(1)} %collective-permute-done.8.refs_1_, ...), custom_call_target="tpu_custom_call" | custom-call | flops 4227858432 | bytes 7733248 | tf_op jit(solution)/shard_map/project/pallas_call | solution.py:181
  88.9 1.4 collective-permute-start.13
  90.3 1.5 collective-permute-start.14
  91.8 1.6 collective-permute-start.15
  93.3 8.9 %collective-permute-done.13 = bf16[64,3584]{1,0:T(8,128)(2,1)S(1)} collective-permute-done((bf16[64,3584]{1,0:T(8,128)(2,1)S(1)}, bf16[64,3584]{1,0:T(8,128)(2,1)S(1)}, u32[]{:S(2)}, u32[]{:S(2)}) %collective-permute-start.13) | collective-permute-done | bytes 458784 | tf_op jit(solution)/shard_map/ppermute | solution.py:215
  102.3 10.9 %collective-permute-done.15 = bf16[64,3584]{1,0:T(8,128)(2,1)S(1)} collective-permute-done((bf16[64,3584]{1,0:T(8,128)(2,1)S(1)}, bf16[64,3584]{1,0:T(8,128)(2,1)S(1)}, u32[]{:S(2)}, u32[]{:S(2)}) %collective-permute-start.15) | collective-permute-done | bytes 458784 | tf_op jit(solution)/shard_map/ppermute | solution.py:215
  113.7 2.1 fusion
  115.9 97.0 %all_to_all.10 = bf16[128,8,3584]{2,1,0:T(8,128)(2,1)S(1)} all-to-all(bf16[128,8,3584]{2,1,0:T(8,128)(2,1)S(1)} %fusion), channel_id=1, replica_groups=mesh['seq'=8,'exp'=16] {'seq','exp'}, dimensions={0} | all-to-all | bytes 14680064 | tf_op jit(solution)/shard_map/all_to_all | solution.py:407
  213.0 29.7 %experts.1 = bf16[1024,3584]{1,0:T(8,128)(2,1)} custom-call(bf16[1024,3584]{1,0:T(8,128)(2,1)S(1)} %bitcast.46, bf16[1,3584,1024]{2,1,0:T(8,128)(2,1)S(1)} %bitcast.48, bf16[1,3584,1024]{2,1,0:T(8,128)(2,1)S(1)} %bitcast.50, bf16[1,1024,3584]{2,1,0:T(8,128)(2,1)} %refs_3_.1), custom_call_target="tpu_custom_call" | custom-call | flops 22548578304 | bytes 36700160 | tf_op jit(solution)/shard_map/experts/pallas_call | solution.py:306
  242.6 90.6 %all_to_all.11 = bf16[128,8,3584]{2,1,0:T(8,128)(2,1)S(1)} all-to-all(bf16[128,8,3584]{2,1,0:T(8,128)(2,1)} %bitcast.51), channel_id=1, replica_groups=mesh['seq'=8,'exp'=16] {'seq','exp'}, dimensions={0} | all-to-all | bytes 14680064 | tf_op jit(solution)/shard_map/all_to_all | solution.py:415
  333.2 2.7 combine.1
  (69 shorter events, 7.6 us)
Async XLA Ops:
  0.6 15.9 %copy-start.11 = (s32[64,8]{0,1:T(8,128)S(1)}, s32[64,8]{0,1:T(8,128)}, u32[]{:S(2)}) copy-start(s32[64,8]{0,1:T(8,128)} %param.19) | copy-start | bytes 6148
  0.6 15.9 %copy-start.12 = (f32[64,8]{0,1:T(8,128)S(1)}, f32[64,8]{0,1:T(8,128)}, u32[]{:S(2)}) copy-start(f32[64,8]{0,1:T(8,128)} %param.20) | copy-start | bytes 6148
  0.7 16.0 %copy-start.13 = (s32[8,3]{0,1:T(4,128)S(1)}, s32[8,3]{0,1:T(4,128)}, u32[]{:S(2)}) copy-start(s32[8,3]{0,1:T(4,128)} %param.15) | copy-start | bytes 292
  2.0 27.7 %copy-start = (bf16[2,1024,256]{2,1,0:T(8,128)(2,1)}, bf16[2,1024,256]{2,1,0:T(8,128)(2,1)S(1)}, u32[]{:S(2)}) copy-start(bf16[2,1024,256]{2,1,0:T(8,128)(2,1)S(1)} %pad_maximum_fusion.1.kv_ref.refs_0_) | copy-start | bytes 3145732
  4.5 21.5 %collective-permute-start.4 = (bf16[128,3584]{1,0:T(8,128)(2,1)}, bf16[128,3584]{1,0:T(8,128)(2,1)}, u32[]{:S(2)}, u32[]{:S(2)}) collective-permute-start(bf16[128,3584]{1,0:T(8,128)(2,1)} %constant_dynamic-slice_fusion), channel_id=1, source_target_pairs={{0,12},{1,13},{2,14},{3,15},{4,0},{5,1},{6,2},{7,3},{8,4},{9,5},{1... | collective-permute-start | bytes 2752520 | tf_op jit(solution)/shard_map/ppermute | solution.py:210
  4.8 21.3 %collective-permute-start.3 = (bf16[128,3584]{1,0:T(8,128)(2,1)}, bf16[128,3584]{1,0:T(8,128)(2,1)}, u32[]{:S(2)}, u32[]{:S(2)}) collective-permute-start(bf16[128,3584]{1,0:T(8,128)(2,1)} %constant_dynamic-slice_fusion), channel_id=1, source_target_pairs={{0,4},{1,5},{2,6},{3,7},{4,8},{5,9},{6,10},{7,11},{8,12},{9,13},{1... | collective-permute-start | bytes 2752520 | tf_op jit(solution)/shard_map/ppermute | solution.py:210
  6.0 49.3 %collective-permute-start.2 = (bf16[2,1024,256]{2,1,0:T(8,128)(2,1)S(1)}, bf16[2,1024,256]{2,1,0:T(8,128)(2,1)S(1)}, u32[]{:S(2)}, u32[]{:S(2)}) collective-permute-start(bf16[2,1024,256]{2,1,0:T(8,128)(2,1)S(1)} %pad_maximum_fusion.1.kv_ref.refs_0_), channel_id=1, source_target_pairs={{0,96},{16,112},{1,97},{17,113},{2,98},{18,114},{3,99},{19,115},{4... | collective-permute-start | bytes 3145736 | tf_op jit(solution)/shard_map/ppermute | solution.py:238
  11.7 43.6 %collective-permute-start.1 = (bf16[2,1024,256]{2,1,0:T(8,128)(2,1)S(1)}, bf16[2,1024,256]{2,1,0:T(8,128)(2,1)S(1)}, u32[]{:S(2)}, u32[]{:S(2)}) collective-permute-start(bf16[2,1024,256]{2,1,0:T(8,128)(2,1)S(1)} %pad_maximum_fusion.1.kv_ref.refs_0_), channel_id=1, source_target_pairs={{0,64},{16,80},{32,96},{48,112},{1,65},{17,81},{33,97},{49,113},{2... | collective-permute-start | bytes 3145736 | tf_op jit(solution)/shard_map/ppermute | solution.py:238
  13.1 43.6 %collective-permute-start = (bf16[2,1024,256]{2,1,0:T(8,128)(2,1)S(1)}, bf16[2,1024,256]{2,1,0:T(8,128)(2,1)}, u32[]{:S(2)}, u32[]{:S(2)}) collective-permute-start(bf16[2,1024,256]{2,1,0:T(8,128)(2,1)S(1)} %pad_maximum_fusion.1.kv_ref.refs_0_), channel_id=1, source_target_pairs={{0,32},{16,48},{32,64},{48,80},{64,96},{80,112},{1,33},{17,49},{33... | collective-permute-start | bytes 3145736 | tf_op jit(solution)/shard_map/ppermute | solution.py:238
  26.1 30.7 %collective-permute-start.5 = (bf16[128,3584]{1,0:T(8,128)(2,1)}, bf16[128,3584]{1,0:T(8,128)(2,1)}, u32[]{:S(2)}, u32[]{:S(2)}) collective-permute-start(bf16[128,3584]{1,0:T(8,128)(2,1)} %constant_dynamic-slice_fusion), channel_id=1, source_target_pairs={{0,8},{1,9},{2,10},{3,11},{4,12},{5,13},{6,14},{7,15},{8,0},{9,1},... | collective-permute-start | bytes 2752520 | tf_op jit(solution)/shard_map/ppermute | solution.py:210
  35.8 21.0 %copy-start.1 = (bf16[2,1024,256]{2,1,0:T(8,128)(2,1)S(1)}, bf16[2,1024,256]{2,1,0:T(8,128)(2,1)}, u32[]{:S(2)}) copy-start(bf16[2,1024,256]{2,1,0:T(8,128)(2,1)} %copy-done) | copy-start | bytes 3145732
  59.1 5.4 %copy-start.3 = (bf16[1024,256]{1,0:T(8,128)(2,1)S(1)}, bf16[1024,256]{1,0:T(8,128)(2,1)}, u32[]{:S(2)}) copy-start(bf16[1024,256]{1,0:T(8,128)(2,1)} %refs_5_.1) | copy-start | bytes 1572868
  59.1 5.4 %copy-start.4 = (f32[1024,256]{1,0:T(8,128)S(1)}, f32[1024,256]{1,0:T(8,128)}, u32[]{:S(2)}) copy-start(f32[1024,256]{1,0:T(8,128)} %get-tuple-element.41.refs_2_.refs_6_) | copy-start | bytes 3145732
  59.1 5.4 %copy-start.5 = (f32[1024,256]{1,0:T(8,128)S(1)}, f32[1024,256]{1,0:T(8,128)}, u32[]{:S(2)}) copy-start(f32[1024,256]{1,0:T(8,128)} %get-tuple-element.42.refs_3_.refs_7_) | copy-start | bytes 3145732
  59.1 5.4 %copy-start.6 = (f32[1024,256]{1,0:T(8,128)S(1)}, f32[1024,256]{1,0:T(8,128)}, u32[]{:S(2)}) copy-start(f32[1024,256]{1,0:T(8,128)} %get-tuple-element.43.refs_4_.refs_8_) | copy-start | bytes 3145732
  59.1 5.4 %collective-permute-start.6 = (bf16[2,2,1024,128]{3,2,1,0:T(8,128)(2,1)S(1)}, bf16[2,2,1024,128]{3,2,1,0:T(8,128)(2,1)S(1)}, u32[]{:S(2)}, u32[]{:S(2)}) collective-permute-start(bf16[2,2,1024,128]{3,2,1,0:T(8,128)(2,1)S(1)} %choose.2), channel_id=1, source_target_pairs={{0,16},{16,0},{32,48},{48,32},{64,80},{80,64},{96,112},{112,96},{1... | collective-permute-start | bytes 3145736 | tf_op jit(solution)/shard_map/ppermute | solution.py:220
  63.7 18.2 %collective-permute-start.11 = (bf16[256,3584]{1,0:T(8,128)(2,1)}, bf16[256,3584]{1,0:T(8,128)(2,1)}, u32[]{:S(2)}, u32[]{:S(2)}) collective-permute-start(bf16[256,3584]{1,0:T(8,128)(2,1)} %pad_maximum_fusion), channel_id=1, source_target_pairs={{0,16},{16,0},{32,48},{48,32},{64,80},{80,64},{96,112},{112,96},{1... | collective-permute-start | bytes 5505032 | tf_op jit(solution)/shard_map/ppermute | solution.py:220
  64.0 6.2 %collective-permute-start.7 = (bf16[2,2,1024,128]{3,2,1,0:T(8,128)(2,1)S(1)}, bf16[2,2,1024,128]{3,2,1,0:T(8,128)(2,1)S(1)}, u32[]{:S(2)}, u32[]{:S(2)}) collective-permute-start(bf16[2,2,1024,128]{3,2,1,0:T(8,128)(2,1)S(1)} %choose.3), channel_id=1, source_target_pairs={{0,16},{16,0},{32,48},{48,32},{64,80},{80,64},{96,112},{112,96},{1... | collective-permute-start | bytes 3145736 | tf_op jit(solution)/shard_map/ppermute | solution.py:220
  64.3 13.4 %collective-permute-start.12 = (bf16[128,3584]{1,0:T(8,128)(2,1)}, bf16[128,3584]{1,0:T(8,128)(2,1)}, u32[]{:S(2)}, u32[]{:S(2)}) collective-permute-start(bf16[128,3584]{1,0:T(8,128)(2,1)} %collective-permute-done.5.refs_7_), channel_id=1, source_target_pairs={{0,16},{16,0},{32,48},{48,32},{64,80},{80,64},{96,112},{112,96},{1... | collective-permute-start | bytes 2752520 | tf_op jit(solution)/shard_map/ppermute | solution.py:220
  73.5 5.1 %collective-permute-start.8 = (bf16[256,256]{1,0:T(8,128)(2,1)S(1)}, bf16[256,256]{1,0:T(8,128)(2,1)S(1)}, u32[]{:S(2)}, u32[]{:S(2)}) collective-permute-start(bf16[256,256]{1,0:T(8,128)(2,1)S(1)} %get-tuple-element.53), channel_id=1, source_target_pairs={{0,4},{1,5},{2,6},{3,7},{4,8},{5,9},{6,10},{7,11},{8,12},{9,13},{1... | collective-permute-start | bytes 393224 | tf_op jit(solution)/shard_map/ppermute | solution.py:210
  75.7 5.5 %collective-permute-start.9 = (bf16[256,256]{1,0:T(8,128)(2,1)S(1)}, bf16[256,256]{1,0:T(8,128)(2,1)S(1)}, u32[]{:S(2)}, u32[]{:S(2)}) collective-permute-start(bf16[256,256]{1,0:T(8,128)(2,1)S(1)} %get-tuple-element.54), channel_id=1, source_target_pairs={{0,12},{1,13},{2,14},{3,15},{4,0},{5,1},{6,2},{7,3},{8,4},{9,5},{1... | collective-permute-start | bytes 393224 | tf_op jit(solution)/shard_map/ppermute | solution.py:210
  75.7 6.2 %collective-permute-start.10 = (bf16[256,256]{1,0:T(8,128)(2,1)S(1)}, bf16[256,256]{1,0:T(8,128)(2,1)S(1)}, u32[]{:S(2)}, u32[]{:S(2)}) collective-permute-start(bf16[256,256]{1,0:T(8,128)(2,1)S(1)} %get-tuple-element.55), channel_id=1, source_target_pairs={{0,8},{1,9},{2,10},{3,11},{4,12},{5,13},{6,14},{7,15},{8,0},{9,1},... | collective-permute-start | bytes 393224 | tf_op jit(solution)/shard_map/ppermute | solution.py:210
  83.4 29.8 %copy-start.8 = (bf16[64,3584]{1,0:T(8,128)(2,1)S(1)}, bf16[64,3584]{1,0:T(8,128)(2,1)}, u32[]{:S(2)}) copy-start(bf16[64,3584]{1,0:T(8,128)(2,1)} %param.17) | copy-start | bytes 1376260
  83.4 30.3 %copy-start.10 = (f32[3584]{0:T(1024)S(1)}, f32[3584]{0:T(1024)}, u32[]{:S(2)}) copy-start(f32[3584]{0:T(1024)} %param.18) | copy-start | bytes 43012
  88.9 13.4 %collective-permute-start.13 = (bf16[64,3584]{1,0:T(8,128)(2,1)S(1)}, bf16[64,3584]{1,0:T(8,128)(2,1)S(1)}, u32[]{:S(2)}, u32[]{:S(2)}) collective-permute-start(bf16[64,3584]{1,0:T(8,128)(2,1)S(1)} %get-tuple-element.63), channel_id=1, source_target_pairs={{0,1},{1,2},{2,3},{3,0},{4,5},{5,6},{6,7},{7,4},{8,9},{9,10},{10,1... | collective-permute-start | bytes 1376264 | tf_op jit(solution)/shard_map/ppermute | solution.py:215
  90.3 12.0 %collective-permute-start.14 = (bf16[64,3584]{1,0:T(8,128)(2,1)S(1)}, bf16[64,3584]{1,0:T(8,128)(2,1)S(1)}, u32[]{:S(2)}, u32[]{:S(2)}) collective-permute-start(bf16[64,3584]{1,0:T(8,128)(2,1)S(1)} %get-tuple-element.64), channel_id=1, source_target_pairs={{0,3},{1,0},{2,1},{3,2},{4,7},{5,4},{6,5},{7,6},{8,11},{9,8},{10,9... | collective-permute-start | bytes 1376264 | tf_op jit(solution)/shard_map/ppermute | solution.py:215
  91.8 21.4 %collective-permute-start.15 = (bf16[64,3584]{1,0:T(8,128)(2,1)S(1)}, bf16[64,3584]{1,0:T(8,128)(2,1)S(1)}, u32[]{:S(2)}, u32[]{:S(2)}) collective-permute-start(bf16[64,3584]{1,0:T(8,128)(2,1)S(1)} %get-tuple-element.65), channel_id=1, source_target_pairs={{0,2},{1,3},{2,0},{3,1},{4,6},{5,7},{6,4},{7,5},{8,10},{9,11},{10,... | collective-permute-start | bytes 1376264 | tf_op jit(solution)/shard_map/ppermute | solution.py:215
  113.6 2.2 copy-start.9
  113.7 99.2 %slice-start = ((s8[7340032]{0:T(1024)(128)(4,1)}), s8[4194304]{0:T(1024)(128)(4,1)S(1)}, s32[]{:S(2)}) async-start(s8[7340032]{0:T(1024)(128)(4,1)} %bitcast.47), calls=%async_computation.2 | async-start | bytes 8388608
  113.7 99.2 %slice-start.2 = ((s8[7340032]{0:T(1024)(128)(4,1)}), s8[4194304]{0:T(1024)(128)(4,1)S(1)}, s32[]{:S(2)}) async-start(s8[7340032]{0:T(1024)(128)(4,1)} %bitcast.49), calls=%async_computation.4 | async-start | bytes 8388608
  115.8 97.1 %slice-start.1 = ((s8[7340032]{0:T(1024)(128)(4,1)}), s8[3145728]{0:T(1024)(128)(4,1)S(1)}, s32[]{:S(2)}) async-start(s8[7340032]{0:T(1024)(128)(4,1)} %bitcast.47), calls=%async_computation.3 | async-start | bytes 6291456
  115.9 97.1 %slice-start.3 = ((s8[7340032]{0:T(1024)(128)(4,1)}), s8[3145728]{0:T(1024)(128)(4,1)S(1)}, s32[]{:S(2)}) async-start(s8[7340032]{0:T(1024)(128)(4,1)} %bitcast.49), calls=%async_computation.5 | async-start | bytes 6291456
  (2 other events, 2.4 us)
